TPU v7x, 128 devices: a whole 4x4x4 slice. The times are simulated.
128 devices in a mesh: batch: 32 (over y, x, core), chan: 4 (over z).
Axes of the slice: x: 4, y: 4, z: 4, core: 2. Of those that a mesh axis runs over, the one named last changes fastest.
Arguments:
- image_global: bfloat16 [192, 14, 14, 1024], P('batch', None, None, 'chan'), may hold values from -32 to 32
- image_local: bfloat16 [384, 6, 6, 1024], P('batch', None, None, 'chan'), may hold values from -32 to 32
- cotangent_global: bfloat16 [192, 7, 7, 2048], P('batch', None, None, 'chan'), may hold values from -6 to 6
- cotangent_local: bfloat16 [384, 3, 3, 2048], P('batch', None, None, 'chan'), may hold values from -6 to 6
- reduce_one: bfloat16 [1024, 512], P(None, 'chan'), may hold values from -0.1875 to 0.1875
- spatial_one: bfloat16 [3, 3, 512, 512], P(None, None, None, 'chan'), may hold values from -0.09375 to 0.09375
- expand_one: bfloat16 [512, 2048], P(None, 'chan'), may hold values from -0.25 to 0.25
- shortcut: bfloat16 [1024, 2048], P(None, 'chan'), may hold values from -0.1875 to 0.1875
- reduce_two: bfloat16 [2048, 512], P(None, 'chan'), may hold values from -0.125 to 0.125
- spatial_two: bfloat16 [3, 3, 512, 512], P(None, None, None, 'chan'), may hold values from -0.09375 to 0.09375
- expand_two: bfloat16 [512, 2048], P(None, 'chan'), may hold values from -0.25 to 0.25
- factors_mid: float32 [4, 512], P(None, 'chan'), may hold values from 0.5 to 1.5
- factors_out: float32 [3, 2048], P(None, 'chan'), may hold values from 0.5 to 1.5
- shifts_mid: float32 [4, 512], P(None, 'chan'), may hold values from -2 to 2
- shifts_out: float32 [3, 2048], P(None, 'chan'), may hold values from -2 to 2
Outputs:
- output_global: float32 [192, 7, 7, 2048], P('batch', None, None, 'chan')
- output_local: float32 [384, 3, 3, 2048], P('batch', None, None, 'chan')
- image_global_grad: float32 [192, 14, 14, 1024], P('batch', None, None, 'chan')
- image_local_grad: float32 [384, 6, 6, 1024], P('batch', None, None, 'chan')
- reduce_one_grad: float32 [1024, 512], P(None, 'chan')
- spatial_one_grad: float32 [3, 3, 512, 512], P(None, None, None, 'chan')
- expand_one_grad: float32 [512, 2048], P(None, 'chan')
- shortcut_grad: float32 [1024, 2048], P(None, 'chan')
- reduce_two_grad: float32 [2048, 512], P(None, 'chan')
- spatial_two_grad: float32 [3, 3, 512, 512], P(None, None, None, 'chan')
- expand_two_grad: float32 [512, 2048], P(None, 'chan')
- factors_mid_grad: float32 [4, 512], P(None, 'chan')
- factors_out_grad: float32 [3, 2048], P(None, 'chan')
- shifts_mid_grad: float32 [4, 512], P(None, 'chan')
- shifts_out_grad: float32 [3, 2048], P(None, 'chan')
- ratios: float32 [7], replicated
All inputs are finite; a program needn't handle non-finite values.
Results may differ from a plain program's by a relative error of at most 0.03.
Values may be sent and summed in bfloat16 or wider, within the bound.
No kernel may reach another device: no remote copies, remote signals or barrier semaphores. Data moves between devices by JAX's collectives and lax.ppermute only.
A program may use at most 192 MiB of HBM per device.

v0:
```python
import functools
import math

import jax
import jax.numpy as jnp
import numpy as np
from jax import lax
from jax.experimental import pallas as pl
from jax.experimental.pallas import tpu as pltpu
from jax.sharding import Mesh, PartitionSpec as P

EPS = 1e-05
DECAY = 5e-05
BATCH = ("y", "x", "c")
PLANE = ("y", "x")
EVERY = ("y", "x", "c", "z")
BF = jnp.bfloat16
F32 = jnp.float32
SLOPE = math.sqrt(2.0 / math.pi)
CUBE = 0.044715

LIN, GIN, RIN = 576, 1568, 2144
LOUT, GOUT, ROUT = 144, 392, 544
M_IN = (36 * 12 * 32.0, 196 * 6 * 32.0)
M_OUT = (9 * 12 * 32.0, 49 * 6 * 32.0)
ANY = pl.BlockSpec(memory_space=pl.ANY)
VM = pl.BlockSpec(memory_space=pltpu.VMEM)
SM = pl.BlockSpec(memory_space=pltpu.SMEM)


def shape(dims, dtype=F32):
    return jax.ShapeDtypeStruct(dims, dtype)


def launch(name, body, ins, outs, scratch=(), cost=(0, 0)):
    return pl.pallas_call(
        body,
        name=name,
        out_shape=tuple(outs),
        in_specs=[s for _, s in ins],
        out_specs=tuple(VM for _ in outs),
        scratch_shapes=list(scratch),
        compiler_params=pltpu.CompilerParams(vmem_limit_bytes=56 * 1024 * 1024),
        cost_estimate=pl.CostEstimate(flops=cost[0], bytes_accessed=cost[1], transcendentals=0),
    )(*[a for a, _ in ins])


def act(v):
    return 0.5 * v * (1.0 + jnp.tanh(SLOPE * (v + CUBE * (v * v * v))))


def slope(v):
    s = v * v
    t = jnp.tanh(SLOPE * (v + CUBE * (v * s)))
    return 0.5 * (1.0 + t) + (0.5 * SLOPE) * v * (1.0 - t * t) * (1.0 + (3.0 * CUBE) * s)


def rows8(v):
    return jnp.sum(v.reshape(-1, 8, v.shape[-1]), axis=0)


def row1(v):
    return jnp.sum(v, axis=0, keepdims=True)


def coefs(sums, k, members, g, b):
    m = sums[2 * k : 2 * k + 1] / members
    inv = lax.rsqrt(sums[2 * k + 1 : 2 * k + 2] / members - m * m + EPS)
    a = inv * g
    return m, inv, a, b - m * a


def back_coefs(sums, grads, k, members, g, b):
    m, inv, a, _ = coefs(sums, k, members, g, b)
    c1 = a * inv * (grads[2 * k + 1 : 2 * k + 2] / members)
    return a, c1, a * (grads[2 * k : 2 * k + 1] / members) - m * c1


def keep(rows, width, group, start):
    i = lax.broadcasted_iota(jnp.int32, (rows, width), 0)
    if group == 0:
        return (i & 15) < 12
    return ((i & 7) < 6) & (i + start < LOUT + GOUT)


def sweep(body, init):
    done = []
    for group, (first, steps, rows) in enumerate(((0, 3, 48), (144, 5, 80))):

        def step(s, carry, group=group, first=first, rows=rows):
            return body(group, pl.multiple_of(first + s * rows, 16), rows, carry)

        done.append(lax.fori_loop(0, steps, step, init))
    return done


def wide_sweep(body, init):
    done = []
    for group, (first, steps, rows) in enumerate(((0, 6, 96), (576, 14, 112))):

        def step(s, carry, group=group, first=first, rows=rows):
            return body(group, s, pl.multiple_of(first + s * rows, 16), rows, carry)

        done.append(lax.fori_loop(0, steps, step, init))
    return done


def two(width):
    z = jnp.zeros((8, width), F32)
    return (z, z)


def put_stats(out, done, cols=None):
    rows = jnp.concatenate([row1(s) for group in done for s in group], axis=0)
    if cols is None:
        for p in range(out.shape[0]):
            out[p] = rows
    else:
        out[:, cols] = rows


def moments(z_ref, cols):
    width = cols.size if hasattr(cols, "size") else z_ref.shape[1]

    def body(group, start, rows, carry):
        v = z_ref[pl.ds(start, rows), cols]
        return carry[0] + rows8(v), carry[1] + rows8(v * v)

    return sweep(body, two(width))


def dot(a, b):
    return jnp.dot(a, b, preferred_element_type=F32)


def dot_t(a, b):
    return lax.dot_general(a, b, (((1,), (1,)), ((), ())), preferred_element_type=F32)


def fetch(copies, sem):
    started = []
    for i, (src, dst) in enumerate(copies):
        c = pltpu.make_async_copy(src, dst, sem.at[i])
        c.start()
        started.append(c)
    return started


def wait(started):
    for c in started:
        c.wait()


def pack_kernel(side, local, glob, out, tmp):
    tmp[...] = jnp.zeros_like(tmp)
    base = side[0] * side[0] * 16
    for lane in range(tmp.shape[0]):
        cols = slice(lane * 128, lane * 128 + 128)
        for n in range(12):
            for h in range(side[0]):
                v = local[n, h, :, cols].astype(F32)
                tmp[lane, pl.ds(h * side[0] * 16 + n, side[0], stride=16), :] = v
        for n in range(6):
            for h in range(side[1]):
                v = glob[n, h, :, cols].astype(F32)
                tmp[lane, pl.ds(base + h * side[1] * 8 + n, side[1], stride=8), :] = v
        out[:, cols] = tmp[lane].astype(out.dtype)


def pack(name, local, glob, side, rows):
    c = local.shape[-1]
    return launch(
        name,
        functools.partial(pack_kernel, side),
        [(local, VM), (glob, VM)],
        [shape((rows, c), BF)],
        [pltpu.VMEM((c // 128, rows, 128), F32)],
        (0, 4 * rows * c),
    )[0]


def unpack_kernel(side, lanes, local, glob):
    base = side[0] * side[0] * 16
    for lane in range(lanes.shape[0]):
        cols = slice(lane * 128, lane * 128 + 128)
        for n in range(12):
            for h in range(side[0]):
                v = lanes[lane, pl.ds(h * side[0] * 16 + n, side[0], stride=16), :]
                local[n, h, :, cols] = v
        for n in range(6):
            for h in range(side[1]):
                v = lanes[lane, pl.ds(base + h * side[1] * 8 + n, side[1], stride=8), :]
                glob[n, h, :, cols] = v


def unpack_whole(side, rows, local, glob, lanes):
    for lane in range(lanes.shape[0]):
        lanes[lane] = rows[:, lane * 128 : lane * 128 + 128]
    unpack_kernel(side, lanes, local, glob)


def unpack(name, rows, side):
    c = rows.shape[-1]
    return launch(
        name,
        functools.partial(unpack_whole, side),
        [(rows, VM)],
        [shape((12, side[0], side[0], c)), shape((6, side[1], side[1], c))],
        [pltpu.VMEM((c // 128,) + rows.shape[:1] + (128,), F32)],
        (0, 8 * rows.size),
    )


def first_kernel(zi, x0, x1, x2, x3, g1, z1, stats, w, sem):
    started = fetch([(g1.at[:, z], w.at[:, :, pl.ds(z * 128, 128)]) for z in range(4)], sem)
    wait(started)
    wf = w.reshape(1024, 512)
    done = []

    def body(group, s, start, rows, carry):
        acc = jnp.zeros((rows, 512), F32)
        for k, x in enumerate((x0, x1, x2, x3)):
            q = pl.multiple_of(zi[k] * 256, 256)
            acc = acc + dot(x[pl.ds(start, rows), :], wf[pl.ds(q, 256), :])
        z1[pl.ds(start, rows), :] = acc
        return carry[0] + rows8(acc), carry[1] + rows8(acc * acc)

    for group, (first, steps, rows) in enumerate(((0, 2, 288), (576, 4, 392))):

        def step(s, carry, group=group, first=first, rows=rows):
            return body(group, s, pl.multiple_of(first + s * rows, 8), rows, carry)

        if group == 0:
            done.append(lax.fori_loop(0, steps, step, two(512)))
        else:
            rows = 224

            def step(s, carry):
                return body(1, s, pl.multiple_of(576 + s * 224, 16), 224, carry)

            done.append(lax.fori_loop(0, 7, step, two(512)))
    put_stats(stats, done)


def gather_weight(g, w, sem, at=0):
    rows = w.shape[1]
    return fetch(
        [(g.at[:, z, pl.ds(at, rows), :], w.at[:, :, pl.ds(z * 128, 128)]) for z in range(4)], sem
    )


def load_taps(local, glob, i, j, stride):
    c = local.shape[-1]
    if stride == 2:
        lv = local.reshape(4, 2, 4, 2, 16, c)
        gv = glob.reshape(8, 2, 8, 2, 8, c)
        a, p, b, q = i // 2, i % 2, j // 2, j % 2
        lt = lv[a : a + 3, p, b : b + 3, q]
        gt = gv[a : a + 7, p, b : b + 7, q]
    else:
        lt = local[i : i + 3, j : j + 3]
        gt = glob[i : i + 7, j : j + 7]
    return jnp.concatenate(
        [lt.reshape(LOUT, c), gt.reshape(GOUT, c), jnp.zeros((8, c), F32)], axis=0
    )


def clear_border(ref):
    side = ref.shape[0]
    zero = jnp.zeros((side,) + ref.shape[2:], F32)
    ref[0] = zero
    ref[side - 1] = zero
    for r in range(1, side - 1):
        ref[r, 0] = zero[0]
        ref[r, side - 1] = zero[0]


def conv_tail(taps, w, z):
    wf = w.reshape(4608, 512)
    z[...] = dot(taps[:, 0:512], wf[0:512, :])

    def step(k, carry):
        at = pl.multiple_of(k * 512, 512)
        z[...] += dot(taps[:, pl.ds(at, 512)], wf[pl.ds(at, 512), :])
        return carry

    lax.fori_loop(1, 9, step, 0)


def second_kernel(st, z1, gb, g2, taps, z2, stats, hl, hg, w, sem):
    started = gather_weight(g2, w, sem)
    sums = jnp.sum(st[...], axis=0)
    g, b = gb[0:1], gb[1:2]
    cs = [coefs(sums, k, M_IN[k], g, b) for k in (0, 1)]
    clear_border(hl)
    clear_border(hg)

    def body(group, s, start, rows, carry):
        _, _, a, sh = cs[group]
        i = lax.broadcasted_iota(jnp.int32, (rows, 512), 0)
        ok = (i & 15) < 12 if group == 0 else (i & 7) < 6
        h = jnp.where(ok, act(z1[pl.ds(start, rows), :] * a + sh), 0.0)
        if group == 0:
            hl[s + 1, 1:7] = h.reshape(6, 16, 512)
        else:
            hg[s + 1, 1:15] = h.reshape(14, 8, 512)
        return carry

    wide_sweep(body, 0)
    for i in range(3):
        for j in range(3):
            k = 3 * i + j
            taps[:, k * 512 : (k + 1) * 512] = load_taps(hl, hg, i, j, 2).astype(BF)
    wait(started)
    conv_tail(taps, w, z2)
    put_stats(stats, moments(z2, slice(None)))


def fifth_kernel(st, z4, gb, late, taps, z5, stats, hl, hg, w, sem):
    started = gather_weight(late, w, sem, 64)
    sums = jnp.sum(st[...], axis=0)
    g, b = gb[0:1], gb[1:2]
    cs = [coefs(sums, k, M_OUT[k], g, b) for k in (0, 1)]
    hl[...] = jnp.zeros_like(hl)
    hg[...] = jnp.zeros_like(hg)
    for group, (first, side, rows) in enumerate(((0, 3, 48), (144, 7, 56))):
        _, _, a, sh = cs[group]
        i = lax.broadcasted_iota(jnp.int32, (rows, 512), 0)
        ok = (i & 15) < 12 if group == 0 else (i & 7) < 6

        def step(s, carry, group=group, first=first, side=side, rows=rows, a=a, sh=sh, ok=ok):
            v = z4[pl.ds(pl.multiple_of(first + s * rows, 8), rows), :]
            h = jnp.where(ok, act(v * a + sh), 0.0)
            if group == 0:
                hl[s + 1, 1:4] = h.reshape(3, 16, 512)
            else:
                hg[s + 1, 1:8] = h.reshape(7, 8, 512)
            return carry

        lax.fori_loop(0, side, step, 0)
    for i in range(3):
        for j in range(3):
            k = 3 * i + j
            taps[:, k * 512 : (k + 1) * 512] = load_taps(hl, hg, i, j, 1).astype(BF)
    wait(started)
    conv_tail(taps, w, z5)
    put_stats(stats, moments(z5, slice(None)))


def conv_forward(name, kernel, st, z, gb, gw, sides):
    sl, sg = sides
    return launch(
        name,
        kernel,
        [(st, VM), (z, VM), (gb, VM), (gw, ANY)],
        [shape((ROUT, 4608), BF), shape((ROUT, 512)), shape((32, 4, 512))],
        [
            pltpu.VMEM((sl, sl, 16, 512), F32),
            pltpu.VMEM((sg, sg, 8, 512), F32),
            pltpu.VMEM((32, 144, 512), BF),
            pltpu.SemaphoreType.DMA((4,)),
        ],
        (2 * 544 * 4608 * 512, 20_000_000),
    )


def hidden_rows(st, z, gb, h):
    sums = jnp.sum(st[...], axis=0)
    g, b = gb[0:1], gb[1:2]
    cs = [coefs(sums, k, M_OUT[k], g, b) for k in (0, 1)]

    def body(group, start, rows, carry):
        _, _, a, sh = cs[group]
        v = act(z[pl.ds(start, rows), :] * a + sh)
        h[pl.ds(start, rows), :] = jnp.where(keep(rows, 512, group, start), v, 0.0).astype(BF)
        return carry

    sweep(body, 0)


def expand_kernel(plan, st, z, gb, zi, *refs):
    srcs, (h, zo, stats, w, sem) = refs[: len(refs) - 5], refs[len(refs) - 5 :]
    started = fetch(plan(zi, srcs, w), sem)
    hidden_rows(st, z, gb, h)
    wait(started)
    for n in range(4):
        cols = pl.ds(n * 512, 512)
        zo[:, cols] = dot(h[...], w[:, cols])
        put_stats(stats, moments(zo, cols), cols)


def plan_split(zi, srcs, w):
    own, mine, other = srcs
    copies = [(own, w.at[:, pl.ds(pl.multiple_of(zi[0] * 512, 512), 512)])]
    for k in (1, 2, 3):
        cols = pl.ds(pl.multiple_of(zi[k] * 512, 512), 512)
        r = pl.multiple_of(zi[4] * 256, 256)
        copies.append((mine.at[k - 1, pl.ds(512, 256), :], w.at[pl.ds(r, 256), cols]))
        copies.append((other.at[k - 1, pl.ds(512, 256), :], w.at[pl.ds(256 - r, 256), cols]))
    return copies


def plan_skip(zi, srcs, w):
    own, mine, other = srcs
    copies = [(own, w.at[:, pl.ds(pl.multiple_of(zi[0] * 512, 512), 512)])]
    for k in (1, 2, 3):
        cols = pl.ds(pl.multiple_of(zi[k] * 512, 512), 512)
        r = pl.multiple_of(zi[4] * 512, 512)
        copies.append((mine.at[k - 1, pl.ds(0, 512), :], w.at[pl.ds(r, 512), cols]))
        copies.append((other.at[k - 1, pl.ds(0, 512), :], w.at[pl.ds(512 - r, 512), cols]))
    return copies


def plan_late(zi, srcs, w):
    (late,) = srcs
    wv = w.reshape(32, 16, 2048)
    return [
        (late.at[:, z, pl.ds(208 + 16 * j, 16), :], wv.at[:, :, pl.ds(z * 512 + j * 128, 128)])
        for z in range(4)
        for j in range(4)
    ]


def expand_forward(name, plan, n, st, z, gb, zi, srcs):
    return launch(
        name,
        functools.partial(expand_kernel, plan),
        [(st, VM), (z, VM), (gb, VM), (zi, SM)] + [(s, ANY) for s in srcs],
        [shape((ROUT, 512), BF), shape((ROUT, 2048)), shape((4, 2048))],
        [pltpu.VMEM((512, 2048), BF), pltpu.SemaphoreType.DMA((n,))],
        (2 * 544 * 512 * 2048, 9_000_000),
    )


def skip_kernel(zi, x0, x1, x2, x3, own, mine, other, xe, zs, stats, tmp, w, sem):
    started = fetch(plan_skip(zi, (own, mine, other), w), sem)
    tmp[pl.ds(536, 8), :] = jnp.zeros((8, 256), F32)
    for k, x in enumerate((x0, x1, x2, x3)):
        for r in range(3):
            v = x[pl.ds(r * 192, 96), :].astype(F32).reshape(3, 2, 16, 256)[:, 0]
            tmp[pl.ds(r * 48, 48), :] = v.reshape(48, 256)
        for r in range(7):
            v = x[pl.ds(576 + r * 224, 112), :].astype(F32).reshape(7, 2, 8, 256)[:, 0]
            tmp[pl.ds(144 + r * 56, 56), :] = v.reshape(56, 256)
        at = pl.multiple_of(zi[k] * 256, 256)
        xe[:, pl.ds(at, 256)] = tmp[...].astype(BF)
    wait(started)
    for n in range(4):
        cols = pl.ds(n * 512, 512)
        zs[:, cols] = dot(xe[...], w[:, cols])
        put_stats(stats, moments(zs, cols), cols)


def middle_kernel(st3, sts, z3, zs, gb, late, mid, h3, z4, stats, w, sem):
    started = fetch(
        [
            (late.at[:, z, pl.ds(0, 64), :], w.at[:, :, pl.ds(z * 128, 128)])
            for z in range(4)
        ],
        sem,
    )
    for n in range(4):
        cols = pl.ds(n * 512, 512)
        s3 = jnp.sum(st3[:, :, cols], axis=0)
        ss = jnp.sum(sts[:, :, cols], axis=0)
        cs = []
        for k in (0, 1):
            _, _, a3, b3 = coefs(s3, k, M_OUT[k], gb[0:1, cols], gb[1:2, cols])
            _, _, a5, b5 = coefs(ss, k, M_OUT[k], gb[2:3, cols], gb[3:4, cols])
            cs.append((a3, a5, b3 + b5))

        def body(group, start, rows, carry, cols=cols, cs=cs):
            a3, a5, b = cs[group]
            here = (pl.ds(start, rows), cols)
            v = act(z3[here] * a3 + zs[here] * a5 + b)
            v = jnp.where(keep(rows, 512, group, start), v, 0.0)
            mid[here] = v
            h3[here] = v.astype(BF)
            return carry

        sweep(body, 0)
    wait(started)
    z4[...] = dot(h3[...], w.reshape(2048, 512)[...])
    put_stats(stats, moments(z4, slice(None)))


def last_kernel(zi, st, z6, mid, gb, c0, c1, c2, c3, out, dv6, stats):
    for k, cot in enumerate((c0, c1, c2, c3)):
        cols = pl.ds(pl.multiple_of(zi[k] * 512, 512), 512)
        sums = jnp.sum(st[:, :, cols], axis=0)
        cs = [coefs(sums, j, M_OUT[j], gb[0:1, cols], gb[1:2, cols]) for j in (0, 1)]

        def body(group, start, rows, carry, cols=cols, cs=cs, k=k, cot=cot):
            m, _, a, sh = cs[group]
            here = (pl.ds(start, rows), cols)
            z = z6[here]
            v = z * a + sh + mid[here]
            if k == 0:
                out[pl.ds(start, rows), :] = act(v)
            d = slope(v) * cot[pl.ds(start, rows), :].astype(F32)
            dv6[here] = d
            return carry[0] + rows8(d), carry[1] + rows8(d * (z - m))

        done = sweep(body, two(512))
        done = [(s, q * cs[j][1]) for j, (s, q) in enumerate(done)]
        put_stats(stats, done, cols)


def grads_out(ref, sums, rows=((0, 2), (1, 3))):
    for i, (a, b) in enumerate(rows):
        ref[i : i + 1, :] = sums[a : a + 1] + sums[b : b + 1]


def mid_sums(dy, z, cs):
    def body(group, start, rows, carry):
        here = (pl.ds(start, rows), slice(None))
        d = dy[here]
        return carry[0] + rows8(d), carry[1] + rows8(d * (z[here] - cs[group][0]))

    return [(s, q * cs[j][1]) for j, (s, q) in enumerate(sweep(body, two(512)))]


def slope_rows(dy, z, cs, mask=True):
    def body(group, start, rows, carry):
        m, _, a, sh = cs[group]
        here = (pl.ds(start, rows), slice(None))
        v = z[here]
        d = jnp.where(keep(rows, 512, group, start), slope(v * a + sh) * dy[here], 0.0)
        dy[here] = d
        return carry[0] + rows8(d), carry[1] + rows8(d * (v - m))

    return [(s, q * cs[j][1]) for j, (s, q) in enumerate(sweep(body, two(512)))]


def out_coefs(st, gb, at=0):
    sums = jnp.sum(st[...], axis=0)
    return [coefs(sums, k, M_OUT[k], gb[at : at + 1], gb[at + 1 : at + 2]) for k in (0, 1)]


def norm_rows(dy, z, sums, grads, g, b, cols, dz):
    cs = [back_coefs(sums, grads, k, M_OUT[k], g, b) for k in (0, 1)]

    def body(group, start, rows, carry):
        a, c1, c0 = cs[group]
        here = (pl.ds(start, rows), cols)
        d = a * dy[here] - c1 * z[here] - c0
        dz[here] = jnp.where(keep(rows, 512, group, start), d, 0.0).astype(BF)
        return carry

    sweep(body, 0)


def wide_norm(stb, st, z, dy, gb, dz, grad, at=0, rows=(0, 1, 2, 3)):
    for n in range(4):
        cols = pl.ds(n * 512, 512)
        grads = jnp.sum(stb[:, :, cols], axis=0)
        grads = jnp.concatenate([grads[r : r + 1] for r in rows], axis=0)
        sums = jnp.sum(st[:, :, cols], axis=0)
        norm_rows(dy, z, sums, grads, gb[at : at + 1, cols], gb[at + 1 : at + 2, cols], cols, dz)
        for i, (p, q) in enumerate(((0, 2), (1, 3))):
            grad[i : i + 1, cols] = grads[p : p + 1] + grads[q : q + 1]


def own_cols(dst, src, zi, width):
    at = pl.multiple_of(zi[0] * width, width)
    dst[...] = src[:, pl.ds(at, width)]


def back_six_kernel(zi, stb, st6, z6, dv6, gb6, st5, z5, gb5, late, own, dv5, stats, grad, dz, w, sem):
    started = fetch(plan_late(zi, (late,), w), sem)
    wide_norm(stb, st6, z6, dv6, gb6, dz, grad)
    own_cols(own, dz, zi, 512)
    wait(started)
    dv5[...] = dot_t(dz[...], w[...])
    put_stats(stats, slope_rows(dv5, z5, out_coefs(st5, gb5)))


def pad_back(dzl, dzg, dz, at):
    dzl[...] = jnp.zeros_like(dzl)
    dzg[...] = jnp.zeros_like(dzg)
    for r in range(3):
        dzl[at + r, at : at + 3] = dz[pl.ds(48 * r, 48), :].reshape(3, 16, 512)
    for r in range(7):
        dzg[at + r, at : at + 7] = dz[pl.ds(144 + 56 * r, 56), :].reshape(7, 8, 512)


def back_five_kernel(zi, stb, st5, z5, dv5, gb5, st4, z4, gb4, late, own, dv4, stats, grad, dzf, dz, dzl, dzg, w, sem):
    started = gather_weight(late, w, sem, 64)
    sums = jnp.sum(st5[...], axis=0)
    grads = jnp.sum(stb[...], axis=0)
    cs = [back_coefs(sums, grads, k, M_OUT[k], gb5[0:1], gb5[1:2]) for k in (0, 1)]

    def body(group, start, rows, carry):
        a, c1, c0 = cs[group]
        here = (pl.ds(start, rows), slice(None))
        d = a * dv5[here] - c1 * z5[here] - c0
        dzf[here] = jnp.where(keep(rows, 512, group, start), d, 0.0)
        return carry

    sweep(body, 0)
    at = pl.multiple_of(zi[0] * 128, 128)
    own[...] = dzf[:, pl.ds(at, 128)].astype(BF)
    grads_out(grad, grads)
    pad_back(dzl, dzg, dzf, 1)
    wait(started)
    wf = w.reshape(4608, 512)
    for i in range(3):
        for j in range(3):
            k = 3 * i + j
            dz[...] = load_taps(dzl, dzg, 2 - i, 2 - j, 1).astype(BF)
            part = dot_t(dz[...], wf[k * 512 : (k + 1) * 512, :])
            if k == 0:
                dv4[...] = part
            else:
                dv4[...] += part
    put_stats(stats, slope_rows(dv4, z4, out_coefs(st4, gb4)))


def back_four_kernel(zi, stb, st4, z4, dv4, gb4, dv6, st3, sts, z3, zs, gb3, late, own, dpre, stats, grad, dz, w, sem):
    started = fetch(
        [
            (late.at[:, z, pl.ds(0, 64), :], w.at[:, :, pl.ds(z * 128, 128)])
            for z in range(4)
        ],
        sem,
    )
    sums = jnp.sum(st4[...], axis=0)
    grads = jnp.sum(stb[...], axis=0)
    norm_rows(dv4, z4, sums, grads, gb4[0:1], gb4[1:2], slice(None), dz)
    own_cols(own, dz, zi, 128)
    grads_out(grad, grads)
    wait(started)
    wf = w.reshape(2048, 512)
    for n in range(4):
        cols = pl.ds(n * 512, 512)
        dpre[:, cols] = dot_t(dz[...], wf[n * 512 : (n + 1) * 512, :])
        s3 = jnp.sum(st3[:, :, cols], axis=0)
        ss = jnp.sum(sts[:, :, cols], axis=0)
        cs = []
        for k in (0, 1):
            m3, i3, a3, b3 = coefs(s3, k, M_OUT[k], gb3[0:1, cols], gb3[1:2, cols])
            ms, is_, a5, b5 = coefs(ss, k, M_OUT[k], gb3[2:3, cols], gb3[3:4, cols])
            cs.append((a3, a5, b3 + b5, m3, ms, i3, is_))

        def body(group, start, rows, carry, cols=cols, cs=cs):
            a3, a5, b, m3, ms, _, _ = cs[group]
            here = (pl.ds(start, rows), cols)
            u, v = z3[here], zs[here]
            d = slope(u * a3 + v * a5 + b) * (dpre[here] + dv6[here])
            d = jnp.where(keep(rows, 512, group, start), d, 0.0)
            dpre[here] = d
            return (
                carry[0] + rows8(d),
                carry[1] + rows8(d * (u - m3)),
                carry[2] + rows8(d * (v - ms)),
            )

        z8 = jnp.zeros((8, 512), F32)
        done = sweep(body, (z8, z8, z8))
        done = [(s, p * cs[j][5], q * cs[j][6]) for j, (s, p, q) in enumerate(done)]
        put_stats(stats, done, cols)


def back_three_kernel(zi, stb, st3, sts, z3, zs, dpre, gb3, st2, z2, gb2, e_own, e_mine, e_other, own3, dzs, dv2, stats, grad3, grads, dz, w, sem):
    started = fetch(plan_split(zi, (e_own, e_mine, e_other), w), sem)
    wide_norm(stb, st3, z3, dpre, gb3, dz, grad3, 0, (0, 1, 3, 4))
    own_cols(own3, dz, zi, 512)
    wait(started)
    dv2[...] = dot_t(dz[...], w[...])
    put_stats(stats, slope_rows(dv2, z2, out_coefs(st2, gb2)))
    wide_norm(stb, sts, zs, dpre, gb3, dzs, grads, 2, (0, 2, 3, 5))


def back_two_kernel(zi, stb, st2, z2, dv2, gb2, st1, z1, gb1, g2, own, dv1, stats, grad, dzf, dz, acc, dzl, dzg, w, sem):
    started = gather_weight(g2, w, sem)
    sums = jnp.sum(st2[...], axis=0)
    grads = jnp.sum(stb[...], axis=0)
    cs = [back_coefs(sums, grads, k, M_OUT[k], gb2[0:1], gb2[1:2]) for k in (0, 1)]

    def body(group, start, rows, carry):
        a, c1, c0 = cs[group]
        here = (pl.ds(start, rows), slice(None))
        d = a * dv2[here] - c1 * z2[here] - c0
        dzf[here] = jnp.where(keep(rows, 512, group, start), d, 0.0)
        return carry

    sweep(body, 0)
    at = pl.multiple_of(zi[0] * 128, 128)
    own[...] = dzf[:, pl.ds(at, 128)].astype(BF)
    grads_out(grad, grads)
    pad_back(dzl, dzg, dzf, 0)
    wait(started)
    wf = w.reshape(4608, 512)
    s1 = jnp.sum(st1[...], axis=0)
    c1s = [coefs(s1, k, M_IN[k], gb1[0:1], gb1[1:2]) for k in (0, 1)]
    reach = (((1, 0),), ((2, 0), (0, 1)))
    z8 = jnp.zeros((8, 512), F32)
    totals = [(z8, z8), (z8, z8)]
    for p in (0, 1):
        for q in (0, 1):
            first = True
            for i, di in reach[p]:
                for j, dj in reach[q]:
                    k = 3 * i + j
                    dz[...] = load_taps(dzl, dzg, di, dj, 1).astype(BF)
                    part = dot_t(dz[...], wf[k * 512 : (k + 1) * 512, :])
                    if first:
                        acc[...] = part
                    else:
                        acc[...] += part
                    first = False
            for group, (base, side, n, from_row) in enumerate(((0, 3, 16, 0), (576, 7, 8, 144))):
                m, _, a, sh = c1s[group]
                okay = lax.broadcasted_iota(jnp.int32, (n, 512), 0) < (12 if group == 0 else 6)

                def step(r, carry, side=side, n=n, base=base, from_row=from_row, m=m, a=a, sh=sh, okay=okay, p=p, q=q):
                    s, t = carry
                    for c in range(side):
                        at = base + ((2 * r + p) * 2 * side + 2 * c + q) * n
                        rows = pl.ds(pl.multiple_of(at, 8), n)
                        v = z1[rows, :]
                        g = acc[pl.ds(pl.multiple_of(from_row + (r * side + c) * n, 8), n), :]
                        d = jnp.where(okay, slope(v * a + sh) * g, 0.0)
                        dv1[rows, :] = d
                        s = s + rows8(d)
                        t = t + rows8(d * (v - m))
                    return s, t

                totals[group] = lax.fori_loop(0, side, step, totals[group])
    put_stats(stats, [(s, t * c1s[j][1]) for j, (s, t) in enumerate(totals)])


def back_one_kernel(zi, stb, st1, z1, dv1, gb1, g1, skip, own, local, glob, grad, dz, img, w, sem):
    started = gather_weight(g1, w, sem)
    sums = jnp.sum(st1[...], axis=0)
    grads = jnp.sum(stb[...], axis=0)
    cs = [back_coefs(sums, grads, k, M_IN[k], gb1[0:1], gb1[1:2]) for k in (0, 1)]

    def body(group, s, start, rows, carry):
        a, c1, c0 = cs[group]
        here = (pl.ds(start, rows), slice(None))
        i = lax.broadcasted_iota(jnp.int32, (rows, 512), 0)
        ok = (i & 15) < 12 if group == 0 else (i & 7) < 6
        d = a * dv1[here] - c1 * z1[here] - c0
        dz[here] = jnp.where(ok, d, 0.0).astype(BF)
        return carry

    wide_sweep(body, 0)
    own_cols(own, dz, zi, 128)
    grads_out(grad, grads)
    wait(started)
    mine = w.reshape(1024, 512)[pl.ds(pl.multiple_of(zi[0] * 256, 256), 256), :]
    for lane in range(2):
        cols = slice(lane * 128, lane * 128 + 128)
        img[lane] = dot_t(dz[...], mine[lane * 128 : lane * 128 + 128])
        lv = img.at[lane, pl.ds(0, LIN)].reshape(3, 2, 3, 2, 16, 128)
        gv = img.at[lane, pl.ds(LIN, GIN)].reshape(7, 2, 7, 2, 8, 128)
        lv[:, 0, :, 0] += skip[pl.ds(0, LOUT), cols].reshape(3, 3, 16, 128)
        gv[:, 0, :, 0] += skip[pl.ds(LOUT, GOUT), cols].reshape(7, 7, 8, 128)
    unpack_kernel((6, 14), img, local, glob)


def ring(n, k):
    return [(i, (i + k) % n) for i in range(n)]


def spread(v, axes, n):
    return lax.all_to_all(jnp.broadcast_to(v[None], (n,) + v.shape), axes, 0, 0)


def share(v):
    v = v + lax.ppermute(v, "c", ring(2, 1))
    return spread(v, PLANE, 16)


def tell(v):
    return lax.all_to_all(v, BATCH, 0, 0)


def batch_index():
    return (lax.axis_index("y") * 4 + lax.axis_index("x")) * 2 + lax.axis_index("c")


def piece(shard):
    n = shard.shape[0] // 32
    return lax.dynamic_slice_in_dim(shard, batch_index() * n, n, 0)


def around(v, half):
    left = lax.ppermute(v, "z", ring(4, 1))
    right = lax.ppermute(v, "z", ring(4, 3))
    far = jnp.concatenate(
        [lax.ppermute(left[:half], "z", ring(4, 1)), lax.ppermute(right[half:], "z", ring(4, 3))]
    )
    return right, far, left


def batch_total(parts):
    flat = [p.astype(BF).reshape(32, -1, 128) for p in parts]
    sizes = [f.shape[1] for f in flat]
    v = jnp.concatenate(flat, axis=1)
    half = v.reshape(2, 16, v.shape[1], 128)
    ci = lax.axis_index("c")
    keep_ = lax.dynamic_index_in_dim(half, ci, 0, keepdims=False)
    give = lax.dynamic_index_in_dim(half, 1 - ci, 0, keepdims=False)
    got = lax.ppermute(give, "c", ring(2, 1))
    s = (keep_.astype(F32) + got.astype(F32)).astype(BF)
    s = lax.all_to_all(s, PLANE, 0, 0)
    s = jnp.sum(s.astype(F32), axis=0).astype(BF)
    mine = spread(s, PLANE, 16)
    other = lax.ppermute(mine, "c", ring(2, 1))
    low = jnp.where(ci == 0, mine, other)
    high = jnp.where(ci == 0, other, mine)
    v = jnp.concatenate([low, high], axis=0)
    out, at = [], 0
    for p, size in zip(parts, sizes):
        out.append(v[:, at : at + size].reshape(p.shape).astype(F32))
        at += size
    return out


def dot_w(a, b):
    return lax.dot_general(a, b, (((0,), (0,)), ((), ())), preferred_element_type=F32)


def body(
    image_global,
    image_local,
    cotangent_global,
    cotangent_local,
    reduce_one,
    spatial_one,
    expand_one,
    shortcut,
    reduce_two,
    spatial_two,
    expand_two,
    factors_mid,
    factors_out,
    shifts_mid,
    shifts_out,
):
    zi = lax.axis_index("z")
    ci = lax.axis_index("c")
    where = jnp.stack([zi, (zi + 1) % 4, (zi + 2) % 4, (zi + 3) % 4, ci]).astype(jnp.int32)
    flat2, flat5 = spatial_one.reshape(-1, 128), spatial_two.reshape(-1, 128)
    own = [reduce_one, flat2, expand_one, shortcut, reduce_two, flat5, expand_two]

    early = spread(jnp.concatenate([piece(reduce_one), piece(flat2)]), "z", 4)
    g1 = spread(early[:, :32], BATCH, 32)
    g2 = spread(early[:, 32:], BATCH, 32)
    e2 = piece(expand_two)
    late = lax.all_gather(
        jnp.concatenate(
            [piece(reduce_two), piece(flat5)] + [e2[:, 128 * j : 128 * j + 128] for j in range(4)]
        ),
        EVERY,
        axis=0,
    ).reshape(32, 4, 272, 128)

    x = pack("pack_image", image_local, image_global, (6, 14), RIN)
    xs = (x,) + around(x, 1072)
    top = jnp.concatenate([shortcut[:512], expand_one[:256]])
    low = jnp.concatenate([shortcut[512:], expand_one[256:]])
    mine = jnp.stack(around(jnp.where(ci == 0, top, low), 384))
    other = lax.ppermute(mine, "c", ring(2, 1))
    cot = pack("pack_cotangent", cotangent_local, cotangent_global, (3, 7), ROUT)
    cots = (cot,) + around(cot, 272)

    norms = jnp.concatenate(
        [factors_mid, shifts_mid, factors_out.reshape(12, 128), shifts_out.reshape(12, 128)]
    )
    norms = spread(norms, "z", 4)
    fm = norms[:, 0:4].transpose(1, 0, 2).reshape(4, 512)
    sm = norms[:, 4:8].transpose(1, 0, 2).reshape(4, 512)
    fo = norms[:, 8:20].reshape(4, 3, 512).transpose(1, 0, 2).reshape(3, 2048)
    so = norms[:, 20:32].reshape(4, 3, 512).transpose(1, 0, 2).reshape(3, 2048)
    gb1, gb2, gb4, gb5 = [jnp.stack([fm[i], sm[i]]) for i in range(4)]
    gb3 = jnp.stack([fo[0], so[0], fo[1], so[1]])
    gb6 = jnp.stack([fo[2], so[2]])

    z1, s1 = launch(
        "reduce_one",
        first_kernel,
        [(where, SM)] + [(v, VM) for v in xs] + [(g1, ANY)],
        [shape((RIN, 512)), shape((32, 4, 512))],
        [pltpu.VMEM((32, 32, 512), BF), pltpu.SemaphoreType.DMA((4,))],
        (2 * RIN * 1024 * 512, 10_000_000),
    )
    st1 = tell(s1)
    xe, zs, ss = launch(
        "shortcut",
        skip_kernel,
        [(where, SM)] + [(v, VM) for v in xs] + [(shortcut, ANY), (mine, ANY), (other, ANY)],
        [shape((ROUT, 1024), BF), shape((ROUT, 2048)), shape((4, 2048))],
        [pltpu.VMEM((ROUT, 256), F32), pltpu.VMEM((1024, 2048), BF), pltpu.SemaphoreType.DMA((7,))],
        (2 * ROUT * 1024 * 2048, 14_000_000),
    )
    sts = share(ss)
    t1, z2, s2 = conv_forward("spatial_one", second_kernel, st1, z1, gb1, g2, (8, 16))
    st2 = tell(s2)
    h2, z3, s3 = expand_forward(
        "expand_one", plan_split, 7, st2, z2, gb2, where, (expand_one, mine, other)
    )
    st3 = share(s3)
    mid, h3, z4, s4 = launch(
        "reduce_two",
        middle_kernel,
        [(v, VM) for v in (st3, sts, z3, zs, gb3)] + [(late, ANY)],
        [shape((ROUT, 2048)), shape((ROUT, 2048), BF), shape((ROUT, 512)), shape((32, 4, 512))],
        [pltpu.VMEM((32, 64, 512), BF), pltpu.SemaphoreType.DMA((4,))],
        (2 * ROUT * 2048 * 512, 20_000_000),
    )
    st4 = tell(s4)
    t4, z5, s5 = conv_forward("spatial_two", fifth_kernel, st4, z4, gb4, late, (5, 9))
    st5 = tell(s5)
    h5, z6, s6 = expand_forward("expand_two", plan_late, 16, st5, z5, gb5, where, (late,))
    st6 = share(s6)
    out, dv6, b6 = launch(
        "output",
        last_kernel,
        [(where, SM)] + [(v, VM) for v in (st6, z6, mid, gb6) + cots],
        [shape((ROUT, 512)), shape((ROUT, 2048)), shape((4, 2048))],
        (),
        (0, 20_000_000),
    )
    output_local, output_global = unpack("unpack_output", out, (3, 7))
    bt6 = share(b6)

    mid_out = [shape((ROUT, 512)), shape((32, 4, 512))]
    mid_grad, out_grad = shape((2, 512)), shape((2, 2048))
    o6, dv5, b5, gr6 = launch(
        "back_expand_two",
        back_six_kernel,
        [(where, SM)] + [(v, VM) for v in (bt6, st6, z6, dv6, gb6, st5, z5, gb5)] + [(late, ANY)],
        [shape((ROUT, 512), BF)] + mid_out + [out_grad],
        [
            pltpu.VMEM((ROUT, 2048), BF),
            pltpu.VMEM((512, 2048), BF),
            pltpu.SemaphoreType.DMA((16,)),
        ],
        (2 * ROUT * 2048 * 512, 14_000_000),
    )
    bt5 = tell(b5)
    gw6 = dot_w(h5, o6)
    conv_scratch = [
        pltpu.VMEM((ROUT, 512), F32),
        pltpu.VMEM((ROUT, 512), BF),
    ]
    conv_weight = [pltpu.VMEM((32, 144, 512), BF), pltpu.SemaphoreType.DMA((4,))]
    o5, dv4, b4, gr5 = launch(
        "back_spatial_two",
        back_five_kernel,
        [(where, SM)] + [(v, VM) for v in (bt5, st5, z5, dv5, gb5, st4, z4, gb4)] + [(late, ANY)],
        [shape((ROUT, 128), BF)] + mid_out + [mid_grad],
        conv_scratch
        + [pltpu.VMEM((5, 5, 16, 512), F32), pltpu.VMEM((9, 9, 8, 512), F32)]
        + conv_weight,
        (2 * ROUT * 4608 * 512, 10_000_000),
    )
    bt4 = tell(b4)
    gw5 = dot_w(t4, o5)
    o4, dpre, b3, gr4 = launch(
        "back_reduce_two",
        back_four_kernel,
        [(where, SM)]
        + [(v, VM) for v in (bt4, st4, z4, dv4, gb4, dv6, st3, sts, z3, zs, gb3)]
        + [(late, ANY)],
        [shape((ROUT, 128), BF), shape((ROUT, 2048)), shape((6, 2048)), mid_grad],
        [
            pltpu.VMEM((ROUT, 512), BF),
            pltpu.VMEM((32, 64, 512), BF),
            pltpu.SemaphoreType.DMA((4,)),
        ],
        (2 * ROUT * 2048 * 512, 22_000_000),
    )
    bt3 = share(b3)
    gw4 = dot_w(h3, o4)
    o3, dzs, dv2, b2, gr3, grs = launch(
        "back_expand_one",
        back_three_kernel,
        [(where, SM)]
        + [(v, VM) for v in (bt3, st3, sts, z3, zs, dpre, gb3, st2, z2, gb2)]
        + [(v, ANY) for v in (expand_one, mine, other)],
        [shape((ROUT, 512), BF), shape((ROUT, 2048), BF)] + mid_out + [out_grad, out_grad],
        [
            pltpu.VMEM((ROUT, 2048), BF),
            pltpu.VMEM((512, 2048), BF),
            pltpu.SemaphoreType.DMA((7,)),
        ],
        (2 * ROUT * 2048 * 512, 22_000_000),
    )
    bt2 = tell(b2)
    gw3 = dot_w(h2, o3)
    own_s = lax.dynamic_slice_in_dim(dzs, zi * 512, 512, 1)
    gws = dot_w(xe, own_s)
    o2, dv1, b1, gr2 = launch(
        "back_spatial_one",
        back_two_kernel,
        [(where, SM)] + [(v, VM) for v in (bt2, st2, z2, dv2, gb2, st1, z1, gb1)] + [(g2, ANY)],
        [shape((ROUT, 128), BF), shape((RIN, 512)), shape((32, 4, 512)), mid_grad],
        conv_scratch
        + [
            pltpu.VMEM((ROUT, 512), F32),
            pltpu.VMEM((4, 4, 16, 512), F32),
            pltpu.VMEM((8, 8, 8, 512), F32),
        ]
        + conv_weight,
        (2 * ROUT * 4608 * 512, 20_000_000),
    )
    bt1 = tell(b1)
    gw2 = dot_w(t1, o2)
    skip_w = [lax.dynamic_slice_in_dim(shortcut, zi * 256, 256, 0)]
    at = zi * 256
    cut = jnp.concatenate(
        [jnp.where(ci == 0, mine[:, :512], other[:, :512]), jnp.where(ci == 0, other[:, :512], mine[:, :512])],
        axis=1,
    )
    cut = lax.dynamic_slice_in_dim(cut, at, 256, 1)
    skip = jnp.zeros((ROUT, 256), F32)
    for k, w in enumerate([skip_w[0], cut[0], cut[1], cut[2]]):
        part = lax.dynamic_slice_in_dim(dzs, where[k] * 512, 512, 1)
        skip = skip + dot_t(part, w)
    o1, dimage_local, dimage_global, gr1 = launch(
        "back_reduce_one",
        back_one_kernel,
        [(where, SM)] + [(v, VM) for v in (bt1, st1, z1, dv1, gb1)] + [(g1, ANY), (skip, VM)],
        [
            shape((RIN, 128), BF),
            shape((12, 6, 6, 256)),
            shape((6, 14, 14, 256)),
            mid_grad,
        ],
        [
            pltpu.VMEM((RIN, 512), BF),
            pltpu.VMEM((2, RIN, 128), F32),
            pltpu.VMEM((32, 32, 512), BF),
            pltpu.SemaphoreType.DMA((4,)),
        ],
        (2 * RIN * 512 * 256, 16_000_000),
    )
    gw1 = jnp.zeros((4, 256, 128), F32)
    for k in range(4):
        gw1 = lax.dynamic_update_index_in_dim(gw1, dot_w(xs[k], o1), where[k], 0)
    gw1 = gw1.reshape(1024, 128)

    t6, t5, t4w, t3, ts = batch_total([gw6, gw5, gw4, gw3, gws])
    t2, t1w = batch_total([gw2, gw1])
    totals = [t1w, t2, t3, ts, t4w, t5, t6]
    weight_sq = jnp.stack([jnp.sum(jnp.square(w.astype(F32))) for w in own])
    grad_sq = jnp.stack([jnp.sum(jnp.square(t)) for t in totals])
    sq = lax.psum(jnp.stack([weight_sq, grad_sq]), "z")
    weight_norm = jnp.sqrt(sq[0])
    ratios = weight_norm / (jnp.sqrt(sq[1]) / 12864.0 + DECAY * weight_norm)

    def cut_own(v, n):
        return lax.dynamic_slice_in_dim(v, zi * n, n, 2)

    mids = cut_own(jnp.stack([gr1, gr2, gr4, gr5]), 128)
    wides = cut_own(jnp.stack([gr3, grs, gr6]), 512)
    return (
        output_global,
        output_local,
        dimage_global,
        dimage_local,
        totals[0],
        totals[1].reshape(spatial_one.shape),
        totals[2],
        totals[3],
        totals[4],
        totals[5].reshape(spatial_two.shape),
        totals[6],
        mids[:, 1],
        wides[:, 1],
        mids[:, 0],
        wides[:, 0],
        ratios,
    )


def solution(mesh):
    fine = Mesh(np.asarray(mesh.devices).reshape(4, 4, 2, 4), EVERY)
    crops = P(BATCH, None, None, "z")
    mat = P(None, "z")
    conv = P(None, None, None, "z")
    weights = (mat, conv, mat, mat, mat, conv, mat)
    return jax.shard_map(
        body,
        mesh=fine,
        in_specs=(crops,) * 4 + weights + (mat,) * 4,
        out_specs=(crops,) * 4 + weights + (mat,) * 4 + (P(),),
        check_vma=False,
    )
```

profile of v0, /device:TPU:1, one launch (start us, length us, event | category | flops | bytes accessed | tf_op | source)
XLA Modules:
  0.0 678.2 jit_solution(12459830206794930167)
XLA Ops:
  24.6 20.1 %collective-permute-done.1.x3 = bf16[2144,256]{1,0:T(8,128)(2,1)S(1)} collective-permute-done((bf16[2144,256]{1,0:T(8,128)(2,1)}, bf16[2144,256]{1,0:T(8,128)(2,1)S(1)}, u32[]{:S(2)}, u32[]{:S(2)}) %collective-permute-start.1) | collective-permute-done | bytes 1097760 | tf_op jit(solution)/shard_map/ppermute | solution.py:790
  48.4 9.1 %all-to-all-start.1 = ((bf16[32,4,32,128]{3,2,1,0:T(8,128)(2,1)}), bf16[32,4,32,128]{3,2,1,0:T(8,128)(2,1)S(1)}, u32[]{:S(2)}, u32[]{:S(2)}) async-start(bf16[32,4,32,128]{3,2,1,0:T(8,128)(2,1)} %broadcast_in_dim.37), calls=%async_computation.1 | async-start | bytes 2097152 | tf_op jit(solution)/shard_map/all_to_all | solution.py:768
  64.5 11.8 %collective-permute-done.3 = bf16[1072,256]{1,0:T(8,128)(2,1)} collective-permute-done((bf16[1072,256]{1,0:T(8,128)(2,1)}, bf16[1072,256]{1,0:T(8,128)(2,1)}, u32[]{:S(2)}, u32[]{:S(2)}) %collective-permute-start.3) | collective-permute-done | bytes 548896 | tf_op jit(solution)/shard_map/ppermute | solution.py:793
  82.8 9.6 %reduce_one.1 = (f32[2144,512]{1,0:T(8,128)}, f32[32,4,512]{2,1,0:T(4,128)}) custom-call(s32[5]{0:T(128)} %stack.137.zi, bf16[2144,256]{1,0:T(8,128)(2,1)} %pack_image.1.x0, bf16[2144,256]{1,0:T(8,128)(2,1)} %copy-done.12, bf16[2144,256]{1,0:T(8,128)(2,1)} %copy-done.13, bf16[2144,256]{1,0:T(8,128)(2,1)} %copy-done.10, bf16[32,4,32,128]{3,2,1,0:T(8,128)(2,1)} %copy-done.19), custom_call_target="tpu_custom_call" | custom-call | flops 2248146944 | bytes 10000000 | tf_op jit(solution)/shard_map/reduce_one/pallas_call | solution.py:36
  92.5 9.7 %all-to-all-start.2 = ((f32[32,4,512]{2,1,0:T(4,128)}), f32[32,4,512]{2,1,0:T(4,128)S(1)}, u32[]{:S(2)}, u32[]{:S(2)}) async-start(f32[32,4,512]{2,1,0:T(4,128)} %get-tuple-element.68), calls=%async_computation.2 | async-start | bytes 524288 | tf_op jit(solution)/shard_map/all_to_all | solution.py:777
  102.2 8.9 %all-to-all-done.2.st.st1 = f32[32,4,512]{2,1,0:T(4,128)S(1)} async-done(((f32[32,4,512]{2,1,0:T(4,128)}), f32[32,4,512]{2,1,0:T(4,128)S(1)}, u32[]{:S(2)}, u32[]{:S(2)}) %all-to-all-start.2) | async-done | bytes 262176 | tf_op jit(solution)/shard_map/all_to_all | solution.py:777
  122.6 17.5 %collective-permute-done.5 = bf16[768,512]{1,0:T(8,128)(2,1)S(1)} collective-permute-done((bf16[768,512]{1,0:T(8,128)(2,1)S(1)}, bf16[768,512]{1,0:T(8,128)(2,1)S(1)}, u32[]{:S(2)}, u32[]{:S(2)}) %collective-permute-start.5) | collective-permute-done | bytes 786464 | tf_op jit(solution)/shard_map/ppermute | solution.py:790
  143.0 8.2 %collective-permute-done.6 = bf16[384,512]{1,0:T(8,128)(2,1)S(1)} collective-permute-done((bf16[384,512]{1,0:T(8,128)(2,1)S(1)}, bf16[384,512]{1,0:T(8,128)(2,1)S(1)}, u32[]{:S(2)}, u32[]{:S(2)}) %collective-permute-start.6) | collective-permute-done | bytes 393248 | tf_op jit(solution)/shard_map/ppermute | solution.py:793
  154.0 21.1 %all-to-all-done.4.g2 = bf16[32,4,144,128]{3,2,1,0:T(8,128)(2,1)} async-done(((bf16[32,4,144,128]{3,2,1,0:T(8,128)(2,1)}), bf16[32,4,144,128]{3,2,1,0:T(8,128)(2,1)}, u32[]{:S(2)}, u32[]{:S(2)}) %all-to-all-start.4) | async-done | bytes 4718624 | tf_op jit(solution)/shard_map/all_to_all | solution.py:768
  175.1 11.9 %spatial_one.1 = (bf16[544,4608]{1,0:T(8,128)(2,1)}, f32[544,512]{1,0:T(8,128)}, f32[32,4,512]{2,1,0:T(4,128)}) custom-call(f32[32,4,512]{2,1,0:T(4,128)} %copy-done.22, f32[2144,512]{1,0:T(8,128)} %get-tuple-element.69.z1, f32[2,512]{1,0:T(2,128)} %pad_maximum_fusion.8.gb.gb1, bf16[32,4,144,128]{3,2,1,0:T(8,128)(2,1)} %all-to-all-done.4.g2), custom_call_target="tpu_custom_call" | custom-call | flops 2566914048 | bytes 20000000 | tf_op jit(solution)/shard_map/spatial_one/pallas_call | solution.py:36
  187.0 8.2 %all-to-all-start.5 = ((f32[32,4,512]{2,1,0:T(4,128)}), f32[32,4,512]{2,1,0:T(4,128)S(1)}, u32[]{:S(2)}, u32[]{:S(2)}) async-start(f32[32,4,512]{2,1,0:T(4,128)} %get-tuple-element.70), calls=%async_computation.5 | async-start | bytes 524288 | tf_op jit(solution)/shard_map/all_to_all | solution.py:777
  195.1 10.6 %shortcut.1 = (bf16[544,1024]{1,0:T(8,128)(2,1)}, f32[544,2048]{1,0:T(8,128)}, f32[4,2048]{1,0:T(4,128)}) custom-call(s32[5]{0:T(128)} %stack.137.zi, bf16[2144,256]{1,0:T(8,128)(2,1)} %pack_image.1.x0, bf16[2144,256]{1,0:T(8,128)(2,1)} %copy-done.12, bf16[2144,256]{1,0:T(8,128)(2,1)} %copy-done.13, bf16[2144,256]{1,0:T(8,128)(2,1)} %copy-done.10, ...), custom_call_target="tpu_custom_call" | custom-call | flops 2281701376 | bytes 14000000 | tf_op jit(solution)/shard_map/shortcut/pallas_call | solution.py:36
  216.4 7.7 %expand_one.1 = (bf16[544,512]{1,0:T(8,128)(2,1)}, f32[544,2048]{1,0:T(8,128)}, f32[4,2048]{1,0:T(4,128)}) custom-call(f32[32,4,512]{2,1,0:T(4,128)} %copy-done.16, f32[544,512]{1,0:T(8,128)} %get-tuple-element.71.z.z2, f32[2,512]{1,0:T(2,128)} %pad_maximum_fusion.9.gb.gb2, s32[5]{0:T(128)} %stack.137.zi, bf16[512,512]{1,0:T(8,128)(2,1)} %e_own.1, ...), custom_call_target="tpu_custom_call" | custom-call | flops 1140850688 | bytes 9000000 | tf_op jit(solution)/shard_map/expand_one/pallas_call | solution.py:36
  235.3 10.0 %all-to-all-done.6.st3 = f32[16,4,2048]{2,1,0:T(4,128)S(1)} async-done(((f32[16,4,2048]{2,1,0:T(4,128)}), f32[16,4,2048]{2,1,0:T(4,128)S(1)}, u32[]{:S(2)}, u32[]{:S(2)}) %all-to-all-start.6) | async-done | bytes 524320 | tf_op jit(solution)/shard_map/all_to_all | solution.py:768
  246.1 11.5 %reduce_two.1 = (f32[544,2048]{1,0:T(8,128)}, bf16[544,2048]{1,0:T(8,128)(2,1)}, f32[544,512]{1,0:T(8,128)}, f32[32,4,512]{2,1,0:T(4,128)}) custom-call(f32[16,4,2048]{2,1,0:T(4,128)} %copy-done.9, f32[16,4,2048]{2,1,0:T(4,128)} %copy-done.8, f32[544,2048]{1,0:T(8,128)} %get-tuple-element.74.z3, f32[544,2048]{1,0:T(8,128)} %get-tuple-element.75.zs, ...), custom_call_target="tpu_custom_call" | custom-call | flops 1140850688 | bytes 20000000 | tf_op jit(solution)/shard_map/reduce_two/pallas_call | solution.py:36
  272.7 10.7 %spatial_two.1 = (bf16[544,4608]{1,0:T(8,128)(2,1)}, f32[544,512]{1,0:T(8,128)}, f32[32,4,512]{2,1,0:T(4,128)}) custom-call(f32[32,4,512]{2,1,0:T(4,128)} %copy-done.17, f32[544,512]{1,0:T(8,128)} %get-tuple-element.77.z4, f32[2,512]{1,0:T(2,128)} %pad_maximum_fusion.10.gb.gb4, bf16[32,4,272,128]{3,2,1,0:T(8,128)(2,1)} %bitcast.145), custom_call_target="tpu_custom_call" | custom-call | flops 2566914048 | bytes 20000000 | tf_op jit(solution)/shard_map/spatial_two/pallas_call | solution.py:36
  288.5 8.3 %all-to-all-done.9.st.st5 = f32[32,4,512]{2,1,0:T(4,128)S(1)} async-done(((f32[32,4,512]{2,1,0:T(4,128)}), f32[32,4,512]{2,1,0:T(4,128)S(1)}, u32[]{:S(2)}, u32[]{:S(2)}) %all-to-all-start.9) | async-done | bytes 262176 | tf_op jit(solution)/shard_map/all_to_all | solution.py:777
  297.6 7.9 %expand_two.1 = (bf16[544,512]{1,0:T(8,128)(2,1)}, f32[544,2048]{1,0:T(8,128)}, f32[4,2048]{1,0:T(4,128)}) custom-call(f32[32,4,512]{2,1,0:T(4,128)} %copy-done.18, f32[544,512]{1,0:T(8,128)} %get-tuple-element.79.z.z5, f32[2,512]{1,0:T(2,128)} %pad_maximum_fusion.11.gb.gb5, s32[5]{0:T(128)} %stack.137.zi, bf16[32,4,272,128]{3,2,1,0:T(8,128)(2,1)} %bitcast.146), custom_call_target="tpu_custom_call" | custom-call | flops 1140850688 | bytes 9000000 | tf_op jit(solution)/shard_map/expand_two/pallas_call | solution.py:36
  324.6 11.3 %output.1 = (f32[544,512]{1,0:T(8,128)}, f32[544,2048]{1,0:T(8,128)}, f32[4,2048]{1,0:T(4,128)}) custom-call(s32[5]{0:T(128)} %stack.137.zi, f32[16,4,2048]{2,1,0:T(4,128)} %copy-done.15, f32[544,2048]{1,0:T(8,128)} %get-tuple-element.81.z6, f32[544,2048]{1,0:T(8,128)} %get-tuple-element.82.mid, f32[2,2048]{1,0:T(2,128)} %pad_maximum_fusion.7.gb.gb6, ...), custom_call_target="tpu_custom_call" | custom-call | bytes 20000000 | tf_op jit(solution)/shard_map/output/pallas_call | solution.py:36
  345.4 10.7 %all-to-all-done.11.stb = f32[16,4,2048]{2,1,0:T(4,128)S(1)} async-done(((f32[16,4,2048]{2,1,0:T(4,128)}), f32[16,4,2048]{2,1,0:T(4,128)S(1)}, u32[]{:S(2)}, u32[]{:S(2)}) %all-to-all-start.11) | async-done | bytes 524320 | tf_op jit(solution)/shard_map/all_to_all | solution.py:768
  356.9 9.7 %back_expand_two.1 = (bf16[544,512]{1,0:T(8,128)(2,1)}, f32[544,512]{1,0:T(8,128)}, f32[32,4,512]{2,1,0:T(4,128)}, f32[2,2048]{1,0:T(2,128)}) custom-call(s32[5]{0:T(128)} %stack.137.zi, f32[16,4,2048]{2,1,0:T(4,128)} %copy-done.24, f32[16,4,2048]{2,1,0:T(4,128)} %copy-done.15, f32[544,2048]{1,0:T(8,128)} %get-tuple-element.81.z6, ...), custom_call_target="tpu_custom_call" | custom-call | flops 1140850688 | bytes 14000000 | tf_op jit(solution)/shard_map/back_expand_two/pallas_call | solution.py:36
  381.6 9.5 %back_spatial_two.1 = (bf16[544,128]{1,0:T(8,128)(2,1)}, f32[544,512]{1,0:T(8,128)}, f32[32,4,512]{2,1,0:T(4,128)}, f32[2,512]{1,0:T(2,128)}) custom-call(s32[5]{0:T(128)} %stack.137.zi, f32[32,4,512]{2,1,0:T(4,128)} %copy-done.31, f32[32,4,512]{2,1,0:T(4,128)} %copy-done.18, f32[544,512]{1,0:T(8,128)} %get-tuple-element.79.z.z5, ...), custom_call_target="tpu_custom_call" | custom-call | flops 2566914048 | bytes 10000000 | tf_op jit(solution)/shard_map/back_spatial_two/pallas_call | solution.py:36
  404.8 16.9 %back_reduce_two.1 = (bf16[544,128]{1,0:T(8,128)(2,1)}, f32[544,2048]{1,0:T(8,128)}, f32[6,2048]{1,0:T(8,128)}, f32[2,512]{1,0:T(2,128)}) custom-call(s32[5]{0:T(128)} %stack.137.zi, f32[32,4,512]{2,1,0:T(4,128)} %copy-done.29, f32[32,4,512]{2,1,0:T(4,128)} %copy-done.17, f32[544,512]{1,0:T(8,128)} %get-tuple-element.77.z4, ...), custom_call_target="tpu_custom_call" | custom-call | flops 1140850688 | bytes 22000000 | tf_op jit(solution)/shard_map/back_reduce_two/pallas_call | solution.py:36
  437.0 9.8 %all-to-all-done.14.stb = f32[16,6,2048]{2,1,0:T(8,128)S(1)} async-done(((f32[16,6,2048]{2,1,0:T(8,128)}), f32[16,6,2048]{2,1,0:T(8,128)S(1)}, u32[]{:S(2)}, u32[]{:S(2)}) %all-to-all-start.14) | async-done | bytes 786464 | tf_op jit(solution)/shard_map/all_to_all | solution.py:768
  447.8 13.2 %back_expand_one.1 = (bf16[544,512]{1,0:T(8,128)(2,1)}, bf16[544,2048]{1,0:T(8,128)(2,1)}, f32[544,512]{1,0:T(8,128)}, f32[32,4,512]{2,1,0:T(4,128)}, f32[2,2048]{1,0:T(2,128)}, /*index=5*/f32[2,2048]{1,0:T(2,128)}) custom-call(s32[5]{0:T(128)} %stack.137.zi, f32[16,6,2048]{2,1,0:T(8,128)} %copy-done.20, f32[16,4,2048]{2,1,0:T(4,128)} %copy-done.9, ...), custom_call_target="tpu_custom_call" | custom-call | flops 1140850688 | bytes 22000000 | tf_op jit(solution)/shard_map/back_expand_one/pallas_call | solution.py:36
  479.5 15.2 %back_spatial_one.1 = (bf16[544,128]{1,0:T(8,128)(2,1)}, f32[2144,512]{1,0:T(8,128)}, f32[32,4,512]{2,1,0:T(4,128)}, f32[2,512]{1,0:T(2,128)}) custom-call(s32[5]{0:T(128)} %stack.137.zi, f32[32,4,512]{2,1,0:T(4,128)} %copy-done.30, f32[32,4,512]{2,1,0:T(4,128)} %copy-done.16, f32[544,512]{1,0:T(8,128)} %get-tuple-element.71.z.z2, ...), custom_call_target="tpu_custom_call" | custom-call | flops 2566914048 | bytes 20000000 | tf_op jit(solution)/shard_map/back_spatial_one/pallas_call | solution.py:36
  494.7 7.4 %all-to-all-start.16 = ((f32[32,4,512]{2,1,0:T(4,128)}), f32[32,4,512]{2,1,0:T(4,128)S(1)}, u32[]{:S(2)}, u32[]{:S(2)}) async-start(f32[32,4,512]{2,1,0:T(4,128)} %get-tuple-element.96), calls=%async_computation.16 | async-start | bytes 524288 | tf_op jit(solution)/shard_map/all_to_all | solution.py:777
  511.7 7.6 %back_reduce_one.1 = (bf16[2144,128]{1,0:T(8,128)(2,1)}, f32[12,6,6,256]{3,2,1,0:T(8,128)}, f32[6,14,14,256]{3,2,1,0:T(8,128)}, f32[2,512]{1,0:T(2,128)}) custom-call(s32[5]{0:T(128)} %stack.137.zi, f32[32,4,512]{2,1,0:T(4,128)} %copy-done.32, f32[32,4,512]{2,1,0:T(4,128)} %copy-done.22, f32[2144,512]{1,0:T(8,128)} %get-tuple-element.69.z1, ...), custom_call_target="tpu_custom_call" | custom-call | flops 562036736 | bytes 16000000 | tf_op jit(solution)/shard_map/back_reduce_one/pallas_call | solution.py:36
  537.3 23.2 %all-to-all-done.19 = bf16[16,464,128]{2,1,0:T(8,128)(2,1)} async-done(((bf16[16,464,128]{2,1,0:T(8,128)(2,1)}), bf16[16,464,128]{2,1,0:T(8,128)(2,1)}, u32[]{:S(2)}, u32[]{:S(2)}) %all-to-all-start.19) | async-done | bytes 1900576 | tf_op jit(solution)/shard_map/all_to_all | solution.py:808
  565.9 10.5 %all-to-all-done.17 = bf16[16,176,128]{2,1,0:T(8,128)(2,1)S(1)} async-done(((bf16[16,176,128]{2,1,0:T(8,128)(2,1)}), bf16[16,176,128]{2,1,0:T(8,128)(2,1)S(1)}, u32[]{:S(2)}, u32[]{:S(2)}) %all-to-all-start.17) | async-done | bytes 720928 | tf_op jit(solution)/shard_map/all_to_all | solution.py:808
  586.2 20.7 %all-to-all-done.20 = bf16[16,464,128]{2,1,0:T(8,128)(2,1)S(1)} async-done(((bf16[16,464,128]{2,1,0:T(8,128)(2,1)}), bf16[16,464,128]{2,1,0:T(8,128)(2,1)S(1)}, u32[]{:S(2)}, u32[]{:S(2)}) %all-to-all-start.20) | async-done | bytes 1900576 | tf_op jit(solution)/shard_map/all_to_all | solution.py:768
  656.7 8.7 %psum.7 = f32[2,7]{1,0:T(2,128)S(1)} all-reduce(f32[2,7]{1,0:T(2,128)S(1)} %pad_maximum_fusion.12), channel_id=1, replica_groups=mesh['y'=4,'x'=4,'c'=2,'z'=4] {'z'}, use_global_device_ids=true, to_apply=%region_16.17 | all-reduce | flops 14 | bytes 112 | tf_op jit(solution)/shard_map/psum | solution.py:1052
  (291 shorter events, 285.3 us)
Async XLA Ops:
  7.2 238.1 %all-gather.3.cloned.1.call-start = ((), (), s32[]{:S(2)}) async-start(), calls=%async_computation.21 | async-start | bytes 8982528 | tf_op jit(solution)/shard_map/all_gather | solution.py:853
  15.3 29.5 %collective-permute-start.1 = (bf16[2144,256]{1,0:T(8,128)(2,1)}, bf16[2144,256]{1,0:T(8,128)(2,1)S(1)}, u32[]{:S(2)}, u32[]{:S(2)}) collective-permute-start(bf16[2144,256]{1,0:T(8,128)(2,1)} %pack_image.1.x0), channel_id=1, source_target_pairs={{0,1},{1,2},{2,3},{3,0},{4,5},{5,6},{6,7},{7,4},{8,9},{9,10},{10,1... | collective-permute-start | bytes 3293192 | tf_op jit(solution)/shard_map/ppermute | solution.py:790
  17.7 39.8 %collective-permute-start = (bf16[2144,256]{1,0:T(8,128)(2,1)}, bf16[2144,256]{1,0:T(8,128)(2,1)S(1)}, u32[]{:S(2)}, u32[]{:S(2)}) collective-permute-start(bf16[2144,256]{1,0:T(8,128)(2,1)} %pack_image.1.x0), channel_id=1, source_target_pairs={{0,3},{1,0},{2,1},{3,2},{4,7},{5,4},{6,5},{7,6},{8,11},{9,8},{10,9... | collective-permute-start | bytes 3293192 | tf_op jit(solution)/shard_map/ppermute | solution.py:791
  21.3 26.0 %all-to-all-start = ((bf16[4,176,128]{2,1,0:T(8,128)(2,1)}), bf16[4,176,128]{2,1,0:T(8,128)(2,1)S(1)}, u32[]{:S(2)}, u32[]{:S(2)}) async-start(bf16[4,176,128]{2,1,0:T(8,128)(2,1)} %broadcast_in_dim.36), calls=%async_computation | async-start | bytes 360448 | tf_op jit(solution)/shard_map/all_to_all | solution.py:768
  45.6 17.8 %collective-permute-start.2 = (bf16[1072,256]{1,0:T(8,128)(2,1)}, bf16[1072,256]{1,0:T(8,128)(2,1)}, u32[]{:S(2)}, u32[]{:S(2)}) collective-permute-start(bf16[1072,256]{1,0:T(8,128)(2,1)} %slice.266), channel_id=1, source_target_pairs={{0,1},{1,2},{2,3},{3,0},{4,5},{5,6},{6,7},{7,4},{8,9},{9,10},{10,1... | collective-permute-start | bytes 1646600 | tf_op jit(solution)/shard_map/ppermute | solution.py:793
  48.4 29.0 %all-to-all-start.1 = ((bf16[32,4,32,128]{3,2,1,0:T(8,128)(2,1)}), bf16[32,4,32,128]{3,2,1,0:T(8,128)(2,1)S(1)}, u32[]{:S(2)}, u32[]{:S(2)}) async-start(bf16[32,4,32,128]{3,2,1,0:T(8,128)(2,1)} %broadcast_in_dim.37), calls=%async_computation.1 | async-start | bytes 2097152 | tf_op jit(solution)/shard_map/all_to_all | solution.py:768
  58.4 17.9 %collective-permute-start.3 = (bf16[1072,256]{1,0:T(8,128)(2,1)}, bf16[1072,256]{1,0:T(8,128)(2,1)}, u32[]{:S(2)}, u32[]{:S(2)}) collective-permute-start(bf16[1072,256]{1,0:T(8,128)(2,1)} %slice.267), channel_id=1, source_target_pairs={{0,3},{1,0},{2,1},{3,2},{4,7},{5,4},{6,5},{7,6},{8,11},{9,8},{10,9... | collective-permute-start | bytes 1646600 | tf_op jit(solution)/shard_map/ppermute | solution.py:793
  78.2 14.3 %all-to-all-start.3 = ((f32[4,32,128]{2,1,0:T(8,128)}), f32[4,32,128]{2,1,0:T(8,128)S(1)}, u32[]{:S(2)}, u32[]{:S(2)}) async-start(f32[4,32,128]{2,1,0:T(8,128)} %broadcast_in_dim.39), calls=%async_computation.3 | async-start | bytes 131072 | tf_op jit(solution)/shard_map/all_to_all | solution.py:768
  92.5 18.6 %all-to-all-start.2 = ((f32[32,4,512]{2,1,0:T(4,128)}), f32[32,4,512]{2,1,0:T(4,128)S(1)}, u32[]{:S(2)}, u32[]{:S(2)}) async-start(f32[32,4,512]{2,1,0:T(4,128)} %get-tuple-element.68), calls=%async_computation.2 | async-start | bytes 524288 | tf_op jit(solution)/shard_map/all_to_all | solution.py:777
  114.4 60.7 %all-to-all-start.4 = ((bf16[32,4,144,128]{3,2,1,0:T(8,128)(2,1)}), bf16[32,4,144,128]{3,2,1,0:T(8,128)(2,1)}, u32[]{:S(2)}, u32[]{:S(2)}) async-start(bf16[32,4,144,128]{3,2,1,0:T(8,128)(2,1)} %broadcast_in_dim.40), calls=%async_computation.4 | async-start | bytes 9437184 | tf_op jit(solution)/shard_map/all_to_all | solution.py:768
  119.6 20.5 %collective-permute-start.5 = (bf16[768,512]{1,0:T(8,128)(2,1)S(1)}, bf16[768,512]{1,0:T(8,128)(2,1)S(1)}, u32[]{:S(2)}, u32[]{:S(2)}) collective-permute-start(bf16[768,512]{1,0:T(8,128)(2,1)S(1)} %maximum_select_fusion), channel_id=1, source_target_pairs={{0,1},{1,2},{2,3},{3,0},{4,5},{5,6},{6,7},{7,4},{8,9},{9,10},{10,1... | collective-permute-start | bytes 2359304 | tf_op jit(solution)/shard_map/ppermute | solution.py:790
  121.2 18.9 %collective-permute-start.4 = (bf16[768,512]{1,0:T(8,128)(2,1)S(1)}, bf16[768,512]{1,0:T(8,128)(2,1)S(1)}, u32[]{:S(2)}, u32[]{:S(2)}) collective-permute-start(bf16[768,512]{1,0:T(8,128)(2,1)S(1)} %maximum_select_fusion), channel_id=1, source_target_pairs={{0,3},{1,0},{2,1},{3,2},{4,7},{5,4},{6,5},{7,6},{8,11},{9,8},{10,9... | collective-permute-start | bytes 2359304 | tf_op jit(solution)/shard_map/ppermute | solution.py:791
  151.5 43.6 %collective-permute-start.8 = (bf16[3,768,512]{2,1,0:T(8,128)(2,1)S(1)}, bf16[3,768,512]{2,1,0:T(8,128)(2,1)}, u32[]{:S(2)}, u32[]{:S(2)}) collective-permute-start(bf16[3,768,512]{2,1,0:T(8,128)(2,1)S(1)} %pad_maximum_fusion.refs_1_.mine.e_mine), channel_id=1, source_target_pairs={{0,4},{4,0},{1,5},{5,1},{2,6},{6,2},{3,7},{7,3},{8,12},{12,8},{9,1... | collective-permute-start | bytes 7077896 | tf_op jit(solution)/shard_map/ppermute | solution.py:866
  187.0 21.1 %all-to-all-start.5 = ((f32[32,4,512]{2,1,0:T(4,128)}), f32[32,4,512]{2,1,0:T(4,128)S(1)}, u32[]{:S(2)}, u32[]{:S(2)}) async-start(f32[32,4,512]{2,1,0:T(4,128)} %get-tuple-element.70), calls=%async_computation.5 | async-start | bytes 524288 | tf_op jit(solution)/shard_map/all_to_all | solution.py:777
  209.0 17.7 %all-to-all-start.7 = ((f32[16,4,2048]{2,1,0:T(4,128)}), f32[16,4,2048]{2,1,0:T(4,128)S(1)}, u32[]{:S(2)}, u32[]{:S(2)}) async-start(f32[16,4,2048]{2,1,0:T(4,128)} %broadcast_in_dim.42), calls=%async_computation.7 | async-start | bytes 1048576 | tf_op jit(solution)/shard_map/all_to_all | solution.py:768
  227.6 17.7 %all-to-all-start.6 = ((f32[16,4,2048]{2,1,0:T(4,128)}), f32[16,4,2048]{2,1,0:T(4,128)S(1)}, u32[]{:S(2)}, u32[]{:S(2)}) async-start(f32[16,4,2048]{2,1,0:T(4,128)} %broadcast_in_dim.41), calls=%async_computation.6 | async-start | bytes 1048576 | tf_op jit(solution)/shard_map/all_to_all | solution.py:768
  257.7 14.3 %all-to-all-start.8 = ((f32[32,4,512]{2,1,0:T(4,128)}), f32[32,4,512]{2,1,0:T(4,128)S(1)}, u32[]{:S(2)}, u32[]{:S(2)}) async-start(f32[32,4,512]{2,1,0:T(4,128)} %get-tuple-element.76), calls=%async_computation.8 | async-start | bytes 524288 | tf_op jit(solution)/shard_map/all_to_all | solution.py:777
  265.2 47.5 %collective-permute-start.13 = (bf16[544,512]{1,0:T(8,128)(2,1)}, bf16[544,512]{1,0:T(8,128)(2,1)S(1)}, u32[]{:S(2)}, u32[]{:S(2)}) collective-permute-start(bf16[544,512]{1,0:T(8,128)(2,1)} %pack_cotangent.1.c0), channel_id=1, source_target_pairs={{0,1},{1,2},{2,3},{3,0},{4,5},{5,6},{6,7},{7,4},{8,9},{9,10},{10,1... | collective-permute-start | bytes 1671176 | tf_op jit(solution)/shard_map/ppermute | solution.py:790
  266.8 46.9 %collective-permute-start.12 = (bf16[544,512]{1,0:T(8,128)(2,1)}, bf16[544,512]{1,0:T(8,128)(2,1)S(1)}, u32[]{:S(2)}, u32[]{:S(2)}) collective-permute-start(bf16[544,512]{1,0:T(8,128)(2,1)} %pack_cotangent.1.c0), channel_id=1, source_target_pairs={{0,3},{1,0},{2,1},{3,2},{4,7},{5,4},{6,5},{7,6},{8,11},{9,8},{10,9... | collective-permute-start | bytes 1671176 | tf_op jit(solution)/shard_map/ppermute | solution.py:791
  283.4 13.5 %all-to-all-start.9 = ((f32[32,4,512]{2,1,0:T(4,128)}), f32[32,4,512]{2,1,0:T(4,128)S(1)}, u32[]{:S(2)}, u32[]{:S(2)}) async-start(f32[32,4,512]{2,1,0:T(4,128)} %get-tuple-element.78), calls=%async_computation.9 | async-start | bytes 524288 | tf_op jit(solution)/shard_map/all_to_all | solution.py:777
  309.1 14.7 %all-to-all-start.10 = ((f32[16,4,2048]{2,1,0:T(4,128)}), f32[16,4,2048]{2,1,0:T(4,128)S(1)}, u32[]{:S(2)}, u32[]{:S(2)}) async-start(f32[16,4,2048]{2,1,0:T(4,128)} %broadcast_in_dim.43), calls=%async_computation.10 | async-start | bytes 1048576 | tf_op jit(solution)/shard_map/all_to_all | solution.py:768
  339.9 16.1 %all-to-all-start.11 = ((f32[16,4,2048]{2,1,0:T(4,128)}), f32[16,4,2048]{2,1,0:T(4,128)S(1)}, u32[]{:S(2)}, u32[]{:S(2)}) async-start(f32[16,4,2048]{2,1,0:T(4,128)} %broadcast_in_dim.44), calls=%async_computation.11 | async-start | bytes 1048576 | tf_op jit(solution)/shard_map/all_to_all | solution.py:768
  366.6 14.3 %all-to-all-start.12 = ((f32[32,4,512]{2,1,0:T(4,128)}), f32[32,4,512]{2,1,0:T(4,128)S(1)}, u32[]{:S(2)}, u32[]{:S(2)}) async-start(f32[32,4,512]{2,1,0:T(4,128)} %get-tuple-element.88), calls=%async_computation.12 | async-start | bytes 524288 | tf_op jit(solution)/shard_map/all_to_all | solution.py:777
  425.1 21.7 %all-to-all-start.14 = ((f32[16,6,2048]{2,1,0:T(8,128)}), f32[16,6,2048]{2,1,0:T(8,128)S(1)}, u32[]{:S(2)}, u32[]{:S(2)}) async-start(f32[16,6,2048]{2,1,0:T(8,128)} %broadcast_in_dim.45), calls=%async_computation.14 | async-start | bytes 2097152 | tf_op jit(solution)/shard_map/all_to_all | solution.py:768
  461.0 17.8 %all-to-all-start.15 = ((f32[32,4,512]{2,1,0:T(4,128)}), f32[32,4,512]{2,1,0:T(4,128)S(1)}, u32[]{:S(2)}, u32[]{:S(2)}) async-start(f32[32,4,512]{2,1,0:T(4,128)} %get-tuple-element.94), calls=%async_computation.15 | async-start | bytes 524288 | tf_op jit(solution)/shard_map/all_to_all | solution.py:777
  476.3 44.7 %collective-permute-start.20 = (bf16[16,464,128]{2,1,0:T(8,128)(2,1)}, bf16[16,464,128]{2,1,0:T(8,128)(2,1)}, u32[]{:S(2)}, u32[]{:S(2)}) collective-permute-start(bf16[16,464,128]{2,1,0:T(8,128)(2,1)} %dynamic-slice_bitcast_fusion), channel_id=1, source_target_pairs={{0,4},{4,0},{1,5},{5,1},{2,6},{6,2},{3,7},{7,3},{8,12},{12,8},{9,1... | collective-permute-start | bytes 5701640 | tf_op jit(solution)/shard_map/ppermute | solution.py:806
  494.7 16.4 %all-to-all-start.16 = ((f32[32,4,512]{2,1,0:T(4,128)}), f32[32,4,512]{2,1,0:T(4,128)S(1)}, u32[]{:S(2)}, u32[]{:S(2)}) async-start(f32[32,4,512]{2,1,0:T(4,128)} %get-tuple-element.96), calls=%async_computation.16 | async-start | bytes 524288 | tf_op jit(solution)/shard_map/all_to_all | solution.py:777
  524.8 35.6 %all-to-all-start.19 = ((bf16[16,464,128]{2,1,0:T(8,128)(2,1)}), bf16[16,464,128]{2,1,0:T(8,128)(2,1)}, u32[]{:S(2)}, u32[]{:S(2)}) async-start(bf16[16,464,128]{2,1,0:T(8,128)(2,1)} %fusion), calls=%async_computation.19 | async-start | bytes 3801088 | tf_op jit(solution)/shard_map/all_to_all | solution.py:808
  560.5 16.0 %all-to-all-start.17 = ((bf16[16,176,128]{2,1,0:T(8,128)(2,1)}), bf16[16,176,128]{2,1,0:T(8,128)(2,1)S(1)}, u32[]{:S(2)}, u32[]{:S(2)}) async-start(bf16[16,176,128]{2,1,0:T(8,128)(2,1)} %fusion.1), calls=%async_computation.17 | async-start | bytes 1441792 | tf_op jit(solution)/shard_map/all_to_all | solution.py:808
  577.9 29.0 %all-to-all-start.20 = ((bf16[16,464,128]{2,1,0:T(8,128)(2,1)}), bf16[16,464,128]{2,1,0:T(8,128)(2,1)S(1)}, u32[]{:S(2)}, u32[]{:S(2)}) async-start(bf16[16,464,128]{2,1,0:T(8,128)(2,1)} %broadcast_in_dim.97), calls=%async_computation.20 | async-start | bytes 3801088 | tf_op jit(solution)/shard_map/all_to_all | solution.py:768
  607.8 18.5 %all-to-all-start.18 = ((bf16[16,176,128]{2,1,0:T(8,128)(2,1)}), bf16[16,176,128]{2,1,0:T(8,128)(2,1)}, u32[]{:S(2)}, u32[]{:S(2)}) async-start(bf16[16,176,128]{2,1,0:T(8,128)(2,1)} %broadcast_in_dim.96), calls=%async_computation.18 | async-start | bytes 1441792 | tf_op jit(solution)/shard_map/all_to_all | solution.py:768
  615.7 28.7 %collective-permute-start.21 = (bf16[16,464,128]{2,1,0:T(8,128)(2,1)S(1)}, bf16[16,464,128]{2,1,0:T(8,128)(2,1)}, u32[]{:S(2)}, u32[]{:S(2)}) collective-permute-start(bf16[16,464,128]{2,1,0:T(8,128)(2,1)S(1)} %all-to-all-done.20), channel_id=1, source_target_pairs={{0,4},{4,0},{1,5},{5,1},{2,6},{6,2},{3,7},{7,3},{8,12},{12,8},{9,1... | collective-permute-start | bytes 5701640 | tf_op jit(solution)/shard_map/ppermute | solution.py:811
  (62 other events, 528.2 us)
Sparse Core Ops, SparseCore 0:
  12.3 76.6 all-gather.2
where the time goes:
time: 690 us; the launch traced here: 678 us
  waiting for transfers between devices  226 us (33%)
  Pallas kernels  161 us (23%)
  starting transfers between devices  145 us (21%)
  local copies, waits for them, and re-layouts  57.7 us (8%)
  other arithmetic  40.9 us (6%)
  matrix products  23.2 us (3%)
  between operations  15.5 us (2%)
  blocking collectives  8.75 us (1%)
    pallas_call x17, Pallas kernels, launch(): pl.pallas_call(body, name=name, out_shape=tuple(outs), in_specs=[s for _,...  161 us
    all_to_all x11, waiting for transfers between devices, spread(): return lax.all_to_all(jnp.broadcast_to(v[None], (n,) + v.shape), axes, 0, 0)  80.2 us
    all_to_all x11, starting transfers between devices, spread(): return lax.all_to_all(jnp.broadcast_to(v[None], (n,) + v.shape), axes, 0, 0)  59.1 us
    all_to_all x8, starting transfers between devices, tell(): return lax.all_to_all(v, BATCH, 0, 0)  49.5 us
    all_to_all x8, waiting for transfers between devices, tell(): return lax.all_to_all(v, BATCH, 0, 0)  38.9 us
    ppermute x3, waiting for transfers between devices, around(): left = lax.ppermute(v, 'z', ring(4, 1))  37.6 us
    all_to_all x2, waiting for transfers between devices, batch_total(): s = lax.all_to_all(s, PLANE, 0, 0)  33.8 us
    dot_general x10, matrix products, dot_w(): lax.dot_general(a, b, (((0,), (0,)), ((), ())), preferred_element_type=F32)  21 us
  transfers between devices with their start and end apart: 44, of which 28 were waited for; matrix products, arithmetic and copies ran while one was open for 12% of the time, Pallas kernels for 13%

commit v1 on v0

v1 whole, which is shorter than its diff:
```python
import functools
import math

import jax
import jax.numpy as jnp
import numpy as np
from jax import lax
from jax.experimental import pallas as pl
from jax.experimental.pallas import tpu as pltpu
from jax.sharding import Mesh, PartitionSpec as P

EPS = 1e-05
DECAY = 5e-05
BATCH = ("y", "x", "c")
PLANE = ("y", "x")
EVERY = ("y", "x", "c", "z")
BF = jnp.bfloat16
F32 = jnp.float32
SLOPE = math.sqrt(2.0 / math.pi)
CUBE = 0.044715

LIN, GIN, RIN = 576, 1568, 2144
LOUT, GOUT, ROUT = 144, 392, 544
M_IN = (36 * 12 * 32.0, 196 * 6 * 32.0)
M_OUT = (9 * 12 * 32.0, 49 * 6 * 32.0)
ANY = pl.BlockSpec(memory_space=pltpu.HBM)
VM = pl.BlockSpec(memory_space=pltpu.VMEM)
NEAR = "near"
FAR = "far"
SM = pl.BlockSpec(memory_space=pltpu.SMEM)


def shape(dims, dtype=F32):
    return jax.ShapeDtypeStruct(dims, dtype)


def launch(name, body, ins, outs, scratch=(), cost=(0, 0)):
    def placed(a, s):
        if s is VM or s is SM:
            return a
        return pltpu.with_memory_space_constraint(a, pltpu.VMEM if s is NEAR else pltpu.HBM)

    return pl.pallas_call(
        body,
        name=name,
        out_shape=tuple(pltpu.HBM(o.shape, o.dtype) if s is not VM else o for o, s in outs),
        in_specs=[VM if s is NEAR else s for _, s in ins],
        out_specs=tuple(VM if s is FAR else s for _, s in outs),
        scratch_shapes=list(scratch),
        compiler_params=pltpu.CompilerParams(vmem_limit_bytes=50 * 1024 * 1024),
        cost_estimate=pl.CostEstimate(flops=cost[0], bytes_accessed=cost[1], transcendentals=0),
    )(*[placed(a, s) for a, s in ins])


def sems(*dims):
    return pltpu.SemaphoreType.DMA(dims)


def go(src, dst, sem):
    c = pltpu.make_async_copy(src, dst, sem)
    c.start()
    return c


def wait(copies):
    for c in copies:
        c.wait()


def quarter(n):
    return pl.ds(n * 512, 512)


def act(v):
    t = jnp.tanh(v * (SLOPE + (SLOPE * CUBE) * (v * v)))
    h = 0.5 * v
    return h + h * t


def slope(v):
    s = v * v
    t = jnp.tanh(v * (SLOPE + (SLOPE * CUBE) * s))
    p = 0.5 + 0.5 * t
    return p + p * (1.0 - t) * (v * (SLOPE + (3.0 * SLOPE * CUBE) * s))


def rows8(v):
    return jnp.sum(v.reshape(-1, 8, v.shape[-1]), axis=0)


def row1(v):
    return jnp.sum(v, axis=0, keepdims=True)


def coefs(sums, k, members, gb):
    g, b = gb
    m = sums[2 * k : 2 * k + 1] / members
    inv = lax.rsqrt(sums[2 * k + 1 : 2 * k + 2] / members - m * m + EPS)
    a = inv * g
    return m, inv, a, b - m * a


def back_coefs(sums, grads, k, members, gb):
    m, inv, a, _ = coefs(sums, k, members, gb)
    c1 = a * inv * (grads[2 * k + 1 : 2 * k + 2] / members)
    return a, c1, a * (grads[2 * k : 2 * k + 1] / members) - m * c1


def mid_gb(norms, i):
    return [
        jnp.concatenate([norms[z, r : r + 1, :] for z in range(4)], axis=1) for r in (i, 4 + i)
    ]


def out_gb(norms, i, z):
    return [
        jnp.concatenate([norms[z, r + l : r + l + 1, :] for l in range(4)], axis=1)
        for r in (8 + 4 * i, 20 + 4 * i)
    ]


def keep(rows, width, group, start):
    i = lax.broadcasted_iota(jnp.int32, (rows, width), 0)
    if group == 0:
        return (i & 15) < 12
    return ((i & 7) < 6) & (i + start < LOUT + GOUT)


def sweep(body, init):
    done = []
    for group, (first, steps, rows) in enumerate(((0, 1, 144), (144, 5, 80))):

        def step(s, carry, group=group, first=first, rows=rows):
            return body(group, pl.multiple_of(first + s * rows, 16), rows, carry)

        done.append(lax.fori_loop(0, steps, step, init))
    return done


LINES = ((0, 6, 96), (576, 14, 112))


def wide_sweep(body, init):
    done = []
    for group, (first, steps, rows) in enumerate(LINES):

        def step(s, carry, group=group, first=first, rows=rows):
            return body(group, s, pl.multiple_of(first + s * rows, 16), rows, carry)

        done.append(lax.fori_loop(0, steps, step, init))
    return done


def lines_in(src, dst, sem):
    for group, (first, steps, rows) in enumerate(LINES):
        for s in range(steps):
            here = pl.ds(first + s * rows, rows)
            go(src.at[here, :], dst.at[here, :], sem.at[6 * group + s])


def line_wait(src, dst, sem, group, s, start, rows):
    here = pl.ds(start, rows)
    pltpu.make_async_copy(src.at[here, :], dst.at[here, :], sem.at[6 * group + s]).wait()


def two(width):
    z = jnp.zeros((8, width), F32)
    return (z, z)


def put_stats(out, done, cols=None):
    rows = jnp.concatenate([row1(s) for group in done for s in group], axis=0)
    if cols is None:
        for p in range(out.shape[0]):
            out[p] = rows
    else:
        out[:, cols] = rows


def moments(z_ref, cols=slice(None)):
    def body(group, start, rows, carry):
        v = z_ref[pl.ds(start, rows), cols]
        return carry[0] + rows8(v), carry[1] + rows8(v * v)

    return sweep(body, two(512))


def added(st, cols=None):
    return jnp.sum(st[...] if cols is None else st[:, :, cols], axis=0)


def dot(a, b):
    return jnp.dot(a, b, preferred_element_type=F32)


def dot_t(a, b):
    return lax.dot_general(a, b, (((1,), (1,)), ((), ())), preferred_element_type=F32)


def riding_in(zi, tops, w, sem):
    return [
        go(
            tops[k].at[pl.ds(TOP, 512), pl.ds(128 * i, 128)],
            w.at[pl.ds(512 * i, 512), pl.ds(pl.multiple_of(zi[k] * 128, 128), 128)],
            sem.at[2 * k + i],
        )
        for k in range(4)
        for i in (0, 1)
    ]


def bundle_in(bundle, at, w, sem):
    n = w.shape[1]
    return [
        go(bundle.at[:, z, pl.ds(at, n), :], w.at[:, :, pl.ds(z * 128, 128)], sem.at[z])
        for z in range(4)
    ]


def bundle_out_in(bundle, at, w, sem):
    n = w.shape[1]
    return [
        go(
            bundle.at[:, z, pl.ds(at + n * j, n), :],
            w.at[:, :, pl.ds(z * 512 + j * 128, 128)],
            sem.at[4 * z + j],
        )
        for z in range(4)
        for j in range(4)
    ]


def halves_in(zi, srcs, w, sem):
    copies = [go(srcs[0], w.at[:, pl.ds(pl.multiple_of(zi[0] * 512, 512), 512)], sem.at[0])]
    for c in (0, 1):
        r = zi[4] * 512 if c == 0 else 512 - zi[4] * 512
        for i in range(6):
            cols = pl.ds(pl.multiple_of(zi[1 + i // 2] * 512, 512), 512)
            dst = w.at[pl.ds(pl.multiple_of(r + 256 * (i % 2), 256), 256), cols]
            copies.append(go(srcs[1 + 6 * c + i], dst, sem.at[1 + 6 * c + i]))
    return copies


def pack_kernel(side, cuts, local, glob, *refs):
    more, outs, tmp = refs[: -1 - len(cuts)], refs[-1 - len(cuts) : -1], refs[-1]
    tmp[...] = jnp.zeros_like(tmp)
    base = side[0] * side[0] * 16
    if more:
        outs[0][pl.ds(outs[0].shape[0] - 512, 512), 0:128] = more[0][0:512, :]
        outs[0][pl.ds(outs[0].shape[0] - 512, 512), 128:256] = more[0][512:1024, :]
    for lane in range(tmp.shape[0]):
        cols = slice(lane * 128, lane * 128 + 128)
        for n in range(12):
            for h in range(side[0]):
                v = local[n, h, :, cols].astype(F32)
                tmp[lane, pl.ds(h * side[0] * 16 + n, side[0], stride=16), :] = v
        for n in range(6):
            for h in range(side[1]):
                v = glob[n, h, :, cols].astype(F32)
                tmp[lane, pl.ds(base + h * side[1] * 8 + n, side[1], stride=8), :] = v
        at = 0
        for out, n in zip(outs, cuts):
            out[pl.ds(0, n), cols] = tmp[lane, pl.ds(at, n), :].astype(out.dtype)
            at += n


def pack(name, local, glob, side, cuts, more=()):
    c = local.shape[-1]
    rows = sum(cuts)
    extra = (512 * len(more), 0)
    return launch(
        name,
        functools.partial(pack_kernel, side, cuts),
        [(v, VM) for v in (local, glob) + more],
        [(shape((n + e, c), BF), VM) for n, e in zip(cuts, extra)],
        [pltpu.VMEM((c // 128, rows, 128), F32)],
        (0, 4 * rows * c),
    )


def unpack_kernel(side, lanes, local, glob):
    base = side[0] * side[0] * 16
    for lane in range(lanes.shape[0]):
        cols = slice(lane * 128, lane * 128 + 128)
        for n in range(12):
            for h in range(side[0]):
                v = lanes[lane, pl.ds(h * side[0] * 16 + n, side[0], stride=16), :]
                local[n, h, :, cols] = v
        for n in range(6):
            for h in range(side[1]):
                v = lanes[lane, pl.ds(base + h * side[1] * 8 + n, side[1], stride=8), :]
                glob[n, h, :, cols] = v


def unpack_whole(side, rows, local, glob, lanes):
    for lane in range(lanes.shape[0]):
        lanes[lane] = rows[:, lane * 128 : lane * 128 + 128]
    unpack_kernel(side, lanes, local, glob)


def unpack(name, rows, side):
    c = rows.shape[-1]
    return launch(
        name,
        functools.partial(unpack_whole, side),
        [(rows, VM)],
        [
            (shape((12, side[0], side[0], c)), VM),
            (shape((6, side[1], side[1], c)), VM),
        ],
        [pltpu.VMEM((c // 128,) + rows.shape[:1] + (128,), F32)],
        (0, 8 * rows.size),
    )


def pieces_kernel(at, spatial_one, expand_one, reduce_two, spatial_two, expand_two, near, late, sem):
    copies = []

    def take(src, dst, first):
        n = src.shape[0] // 32
        rows = pl.ds(pl.multiple_of(at[0] * n, 16), n)
        for j in range(src.shape[1] // 128):
            here = dst.at[pl.ds(first, n), :]
            copies.append(go(src.at[rows, pl.ds(128 * j, 128)], here, sem.at[len(copies)]))
            first += n

    take(spatial_one, near, 0)
    take(expand_one, near, 144)
    take(reduce_two, near, 208)
    take(spatial_two, late, 0)
    take(expand_two, late, 144)
    wait(copies)


def square_kernel(*refs):
    out = refs[-1]
    for i, w in enumerate(refs[:-1]):
        n = w.shape[0] // 8
        total = jnp.zeros((8, 128), F32)
        for lane in range(w.shape[1] // 128):
            cols = slice(lane * 128, lane * 128 + 128)

            def step(s, t, w=w, cols=cols, n=n):
                v = w[pl.ds(pl.multiple_of(s * n, 16), n), cols].astype(F32)
                return t + rows8(v * v)

            total = lax.fori_loop(0, 8, step, total)
        out[i] = total


PARTS = ((0, 576), (576, 224), (800, 672), (1472, 672))
TOP = 800


def wide_moments(z_ref, parts):
    z8 = jnp.zeros((8, 512), F32)
    carry = (z8, z8)
    for first, rows in parts:

        def step(s, c, first=first):
            v = z_ref[pl.ds(pl.multiple_of(first + s * 64, 16), 64), :]
            return c[0] + rows8(v), c[1] + rows8(v * v)

        carry = lax.fori_loop(0, rows // 64, step, carry)
        left = rows % 64
        if left:
            v = z_ref[pl.ds(first + rows - left, left), :]
            carry = (carry[0] + rows8(v), carry[1] + rows8(v * v))
    return carry


def first_kernel(zi, *refs):
    xs, rest = refs[:8], refs[8:]
    z1, stats, xv, zv, w, xsem, osem, ws = rest
    weight = riding_in(zi, xs[::2], w, ws)
    cin = []
    for i, (first, rows) in enumerate(PARTS):
        half, base = (0, 0) if first < TOP else (1, TOP)
        one = []
        for k in range(4):
            cols = pl.ds(pl.multiple_of(zi[k] * 256, 256), 256)
            src = xs[2 * k + half].at[pl.ds(first - base, rows), :]
            one.append(go(src, xv.at[pl.ds(first, rows), cols], xsem.at[i, k]))
        cin.append(one)
    wait(weight)
    wf = w
    out, sums = [], []
    for i, (first, rows) in enumerate(PARTS):
        here = pl.ds(first, rows)
        wait(cin[i])
        zv[here, :] = dot(xv[here, :], wf[...])
        out.append(go(zv.at[here, :], z1.at[here, :], osem.at[i]))
    put_stats(stats, [wide_moments(zv, PARTS[:1]), wide_moments(zv, PARTS[1:])])
    wait(out)


def load_taps(local, glob, i, j, stride):
    c = local.shape[-1]
    if stride == 2:
        lv = local.reshape(4, 2, 4, 2, 16, c)
        gv = glob.reshape(8, 2, 8, 2, 8, c)
        a, p, b, q = i // 2, i % 2, j // 2, j % 2
        lt = lv[a : a + 3, p, b : b + 3, q]
        gt = gv[a : a + 7, p, b : b + 7, q]
    else:
        lt = local[i : i + 3, j : j + 3]
        gt = glob[i : i + 7, j : j + 7]
    return jnp.concatenate(
        [lt.reshape(LOUT, c), gt.reshape(GOUT, c), jnp.zeros((8, c), F32)], axis=0
    )


def clear_border(ref):
    side = ref.shape[0]
    zero = jnp.zeros((side,) + ref.shape[2:], F32)
    ref[0] = zero
    ref[side - 1] = zero
    for r in range(1, side - 1):
        ref[r, 0] = zero[0]
        ref[r, side - 1] = zero[0]


def conv_tail(stride, hl, hg, weight, wf, tv, taps, ts, zv, z, zsem, stats):
    out = []
    for k in range(9):
        cols = pl.ds(k * 512, 512)
        tv[:, cols] = load_taps(hl, hg, k // 3, k % 3, stride).astype(BF)
        out.append(go(tv.at[:, cols], taps.at[:, cols], ts.at[k]))
        if k == 0:
            wait(weight)
            zv[...] = dot(tv[:, cols], wf[0:512, :])
        else:
            zv[...] += dot(tv[:, cols], wf[k * 512 : (k + 1) * 512, :])
    out.append(go(zv, z, zsem))
    put_stats(stats, moments(zv))
    wait(out)


def second_kernel(st, norms, z1, near, taps, z2, stats, sums, zin, hl, hg, w, tv, zv, xs, ws, ts, zsem):
    lines_in(z1, zin, xs)
    weight = bundle_in(near, 0, w, ws)
    total = added(st)
    sums[...] = total
    gb = mid_gb(norms, 0)
    cs = [coefs(total, k, M_IN[k], gb) for k in (0, 1)]
    clear_border(hl)
    clear_border(hg)

    def body(group, s, start, rows, carry):
        _, _, a, sh = cs[group]
        line_wait(z1, zin, xs, group, s, start, rows)
        i = lax.broadcasted_iota(jnp.int32, (rows, 512), 0)
        ok = (i & 15) < 12 if group == 0 else (i & 7) < 6
        h = jnp.where(ok, act(zin[pl.ds(start, rows), :] * a + sh), 0.0)
        if group == 0:
            hl[s + 1, 1:7] = h.reshape(6, 16, 512)
        else:
            hg[s + 1, 1:15] = h.reshape(14, 8, 512)
        return carry

    wide_sweep(body, 0)
    conv_tail(2, hl, hg, weight, w.reshape(4608, 512), tv, taps, ts, zv, z2, zsem.at[0], stats)


def fifth_kernel(st, norms, z4, late, taps, z5, stats, sums, zin, hl, hg, w, tv, zv, xs, ws, ts, zsem):
    cin = go(z4, zin, xs.at[0])
    weight = bundle_in(late, 0, w, ws)
    total = added(st)
    sums[...] = total
    gb = mid_gb(norms, 2)
    cs = [coefs(total, k, M_OUT[k], gb) for k in (0, 1)]
    clear_border(hl)
    clear_border(hg)
    cin.wait()
    for group, (first, side, rows) in enumerate(((0, 3, 48), (144, 7, 56))):
        _, _, a, sh = cs[group]
        i = lax.broadcasted_iota(jnp.int32, (rows, 512), 0)
        ok = (i & 15) < 12 if group == 0 else (i & 7) < 6

        def step(s, carry, group=group, first=first, rows=rows, a=a, sh=sh, ok=ok):
            v = zin[pl.ds(pl.multiple_of(first + s * rows, 8), rows), :]
            h = jnp.where(ok, act(v * a + sh), 0.0)
            if group == 0:
                hl[s + 1, 1:4] = h.reshape(3, 16, 512)
            else:
                hg[s + 1, 1:8] = h.reshape(7, 8, 512)
            return carry

        lax.fori_loop(0, side, step, 0)
    conv_tail(1, hl, hg, weight, w.reshape(4608, 512), tv, taps, ts, zv, z5, zsem.at[0], stats)


def conv_call(name, kernel, ins, rows, sides, n, flops):
    sl, sg = sides
    return launch(
        name,
        kernel,
        ins,
        [
            (shape((ROUT, 4608), BF), ANY),
            (shape((ROUT, 512)), ANY),
            (shape((32, 4, 512)), FAR),
            (shape((4, 512)), VM),
        ],
        [
            pltpu.VMEM((rows, 512), F32),
            pltpu.VMEM((sl, sl, 16, 512), F32),
            pltpu.VMEM((sg, sg, 8, 512), F32),
            pltpu.VMEM((32, 144, 512), BF),
            pltpu.VMEM((ROUT, 4608), BF),
            pltpu.VMEM((ROUT, 512), F32),
            sems(n),
            sems(13),
            sems(9),
            sems(1),
        ],
        (flops, 20_000_000),
    )


def expand_kernel(which, at, st, norms, z, bundle, h, zo, stats, sums, zin, hv, zv, w, wsem, hsem, zsem, isem):
    cin = go(z, zin, isem.at[0])
    weight = bundle_out_in(bundle, at, w.reshape(32, 16, 2048), wsem)
    total = added(st)
    sums[...] = total
    gb = mid_gb(norms, which)
    cs = [coefs(total, k, M_OUT[k], gb) for k in (0, 1)]
    cin.wait()

    def body(group, start, rows, carry):
        _, _, a, sh = cs[group]
        v = act(zin[pl.ds(start, rows), :] * a + sh)
        hv[pl.ds(start, rows), :] = jnp.where(keep(rows, 512, group, start), v, 0.0).astype(BF)
        return carry

    sweep(body, 0)
    out = [go(hv, h, hsem.at[0])]
    wait(weight)
    for n in range(4):
        cols = quarter(n)
        zv[:, cols] = dot(hv[...], w[:, cols])
        out.append(go(zv.at[:, cols], zo.at[:, cols], zsem.at[n]))
        put_stats(stats, moments(zv, cols), cols)
    wait(out)


def expand_call(name, which, at, st, norms, z, bundle):
    return launch(
        name,
        functools.partial(expand_kernel, which, at),
        [(st, NEAR), (norms, VM), (z, ANY), (bundle, ANY)],
        [
            (shape((ROUT, 512), BF), ANY),
            (shape((ROUT, 2048)), ANY),
            (shape((4, 2048)), VM),
            (shape((4, 512)), VM),
        ],
        [
            pltpu.VMEM((ROUT, 512), F32),
            pltpu.VMEM((ROUT, 512), BF),
            pltpu.VMEM((ROUT, 2048), F32),
            pltpu.VMEM((512, 2048), BF),
            sems(16),
            sems(1),
            sems(4),
            sems(1),
        ],
        (2 * 544 * 512 * 2048, 9_000_000),
    )


def skip_kernel(zi, *refs):
    x, srcs, rest = refs[:8], refs[8:21], refs[21:]
    xe, zs, stats, xv, ev, tmp, zv, w, xs, ws, es, os = rest
    xin = [
        [
            go(x[2 * k].at[pl.ds(0, TOP), :], xv.at[k, pl.ds(0, TOP), :], xs.at[k, 0]),
            go(x[2 * k + 1], xv.at[k, pl.ds(TOP, RIN - TOP), :], xs.at[k, 1]),
        ]
        for k in range(4)
    ]
    weight = halves_in(zi, srcs, w, ws)
    tmp[pl.ds(536, 8), :] = jnp.zeros((8, 256), F32)
    for k in range(4):
        wait(xin[k])
        for r in range(3):
            v = xv[k, pl.ds(r * 192, 96), :].astype(F32).reshape(3, 2, 16, 256)[:, 0]
            tmp[pl.ds(r * 48, 48), :] = v.reshape(48, 256)
        for r in range(7):
            v = xv[k, pl.ds(576 + r * 224, 112), :].astype(F32).reshape(7, 2, 8, 256)[:, 0]
            tmp[pl.ds(144 + r * 56, 56), :] = v.reshape(56, 256)
        at = pl.multiple_of(zi[k] * 256, 256)
        ev[:, pl.ds(at, 256)] = tmp[...].astype(BF)
    out = [go(ev, xe, es.at[0])]
    wait(weight)
    for n in range(4):
        cols = quarter(n)
        zv[:, cols] = dot(ev[...], w[:, cols])
        out.append(go(zv.at[:, cols], zs.at[:, cols], os.at[n]))
        put_stats(stats, moments(zv, cols), cols)
    wait(out)


def middle_kernel(st3, norms, z3, zs, late, mid, h3, z4, stats, sum3, sums, z3v, zsv, hv, zv, w, ins, ws, os, hs, zsem):
    cin = []
    for n in range(4):
        cols = quarter(n)
        cin.append(
            [go(z3.at[:, cols], z3v.at[:, cols], ins.at[0, n]), go(zs.at[:, cols], zsv.at[:, cols], ins.at[1, n])]
        )
    weight = bundle_in(late, 208, w, ws)
    wf = w.reshape(2048, 512)
    out = []
    for n in range(4):
        cols = quarter(n)
        both = added(st3, cols)
        s3, ss = both[0:4], both[4:8]
        sum3[:, cols] = s3
        sums[:, cols] = ss
        cs = []
        for k in (0, 1):
            _, _, a3, b3 = coefs(s3, k, M_OUT[k], out_gb(norms, 0, n))
            _, _, a5, b5 = coefs(ss, k, M_OUT[k], out_gb(norms, 1, n))
            cs.append((a3, a5, b3 + b5))
        wait(cin[n])

        def body(group, start, rows, carry, cols=cols, cs=cs):
            a3, a5, b = cs[group]
            here = (pl.ds(start, rows), cols)
            v = act(z3v[here] * a3 + zsv[here] * a5 + b)
            v = jnp.where(keep(rows, 512, group, start), v, 0.0)
            z3v[here] = v
            hv[here] = v.astype(BF)
            return carry

        sweep(body, 0)
        out.append(go(z3v.at[:, cols], mid.at[:, cols], os.at[n]))
        out.append(go(hv.at[:, cols], h3.at[:, cols], hs.at[n]))
        if n == 0:
            wait(weight)
            zv[...] = dot(hv[:, cols], wf[0:512, :])
        else:
            zv[...] += dot(hv[:, cols], wf[n * 512 : (n + 1) * 512, :])
    out.append(go(zv, z4, zsem.at[0]))
    put_stats(stats, moments(zv))
    wait(out)


def last_kernel(zi, st, norms, z6, mid, *refs):
    cots, rest = refs[:8], refs[8:]
    out, dv6, stats, sums, zv, mv, cv, ov, ins, os = rest
    cin = []
    for k in range(4):
        cols = pl.ds(pl.multiple_of(zi[k] * 512, 512), 512)
        cin.append(
            [
                go(z6.at[:, cols], zv.at[k], ins.at[0, k]),
                go(mid.at[:, cols], mv.at[k], ins.at[1, k]),
                go(cots[2 * k], cv.at[k, pl.ds(0, 272), :], ins.at[2, k]),
                go(cots[2 * k + 1], cv.at[k, pl.ds(272, 272), :], ins.at[3, k]),
            ]
        )
    sums[...] = added(st)
    done_out = []
    for k in range(4):
        cols = pl.ds(pl.multiple_of(zi[k] * 512, 512), 512)
        total = sums[:, cols]
        gb = out_gb(norms, 2, zi[k])
        cs = [coefs(total, j, M_OUT[j], gb) for j in (0, 1)]
        wait(cin[k])

        def body(group, start, rows, carry, cs=cs, k=k):
            m, _, a, sh = cs[group]
            here = pl.ds(start, rows)
            z = zv[k, here, :]
            v = z * a + sh + mv[k, here, :]
            if k == 0:
                ov[here, :] = act(v)
            d = slope(v) * cv[k, here, :].astype(F32)
            mv[k, here, :] = d
            return carry[0] + rows8(d), carry[1] + rows8(d * (z - m))

        done = sweep(body, two(512))
        done_out.append(go(mv.at[k], dv6.at[:, cols], os.at[k]))
        if k == 0:
            done_out.append(go(ov, out, os.at[4]))
        done = [(s, q * cs[j][1]) for j, (s, q) in enumerate(done)]
        put_stats(stats, done, cols)
    wait(done_out)


def grads_out(ref, grads, cols=slice(None)):
    ref[0:1, cols] = grads[0:1] + grads[2:3]
    ref[1:2, cols] = grads[1:2] + grads[3:4]


def slope_rows(dy, z, cs):
    def body(group, start, rows, carry):
        m, _, a, sh = cs[group]
        here = (pl.ds(start, rows), slice(None))
        v = z[here]
        d = jnp.where(keep(rows, 512, group, start), slope(v * a + sh) * dy[here], 0.0)
        dy[here] = d
        return carry[0] + rows8(d), carry[1] + rows8(d * (v - m))

    return [(s, q * cs[j][1]) for j, (s, q) in enumerate(sweep(body, two(512)))]


def norm_rows(dy, z, cs, cols, dz):
    def body(group, start, rows, carry):
        a, c1, c0 = cs[group]
        here = (pl.ds(start, rows), cols)
        d = a * dy[here] - c1 * z[here] - c0
        dz[here] = jnp.where(keep(rows, 512, group, start), d, 0.0).astype(dz.dtype)
        return carry

    sweep(body, 0)


def all_coefs(sums, gb):
    return [coefs(sums, k, M_OUT[k], gb) for k in (0, 1)]


def all_back(sums, grads, gb, members=M_OUT):
    return [back_coefs(sums, grads, k, members[k], gb) for k in (0, 1)]


def own_cols(dst, src, zi, width):
    at = pl.multiple_of(zi[0] * width, width)
    dst[...] = src[:, pl.ds(at, width)].astype(dst.dtype)


def back_six_kernel(zi, stb, norms, sum6, sum5, z6, dv6, z5, late, own, dv5, stats, grad, zv, dv, z5v, acc, dz, w, ins, i5, ws, os):
    cin = []
    for n in range(4):
        cols = quarter(n)
        cin.append(
            [go(z6.at[:, cols], zv.at[:, cols], ins.at[0, n]), go(dv6.at[:, cols], dv.at[:, cols], ins.at[1, n])]
        )
    weight = bundle_out_in(late, 144, w.reshape(32, 16, 2048), ws)
    c5 = go(z5, z5v, i5.at[0])
    for n in range(4):
        cols = quarter(n)
        grads = added(stb, cols)
        grads_out(grad, grads, cols)
        cs = all_back(sum6[:, cols], grads, out_gb(norms, 2, n))
        wait(cin[n])
        norm_rows(dv, zv, cs, cols, dz)
        if n == 0:
            wait(weight)
            acc[...] = dot_t(dz[:, cols], w[:, cols])
        else:
            acc[...] += dot_t(dz[:, cols], w[:, cols])
    own_cols(own, dz, zi, 512)
    c5.wait()
    done = slope_rows(acc, z5v, all_coefs(sum5[...], mid_gb(norms, 3)))
    out = go(acc, dv5, os.at[0])
    put_stats(stats, done)
    out.wait()


def pad_back(dzl, dzg, dz, at):
    dzl[...] = jnp.zeros_like(dzl)
    dzg[...] = jnp.zeros_like(dzg)
    for r in range(3):
        dzl[at + r, at : at + 3] = dz[pl.ds(48 * r, 48), :].reshape(3, 16, 512)
    for r in range(7):
        dzg[at + r, at : at + 7] = dz[pl.ds(144 + 56 * r, 56), :].reshape(7, 8, 512)


def back_five_kernel(zi, stb, norms, sum5, sum4, z5, dv5, z4, late, own, dv4, stats, grad, zv, dv, z4v, acc, dz, dzl, dzg, w, ins, ws, os):
    cin = [go(z5, zv, ins.at[0]), go(dv5, dv, ins.at[1])]
    weight = bundle_in(late, 0, w, ws)
    c4 = go(z4, z4v, ins.at[2])
    grads = added(stb)
    grads_out(grad, grads)
    cs = all_back(sum5[...], grads, mid_gb(norms, 3))
    wait(cin)
    norm_rows(dv, zv, cs, slice(None), dv)
    own_cols(own, dv, zi, 128)
    pad_back(dzl, dzg, dv, 1)
    wait(weight)
    wf = w.reshape(4608, 512)
    for k in range(9):
        dz[...] = load_taps(dzl, dzg, 2 - k // 3, 2 - k % 3, 1).astype(BF)
        part = dot_t(dz[...], wf[k * 512 : (k + 1) * 512, :])
        if k == 0:
            acc[...] = part
        else:
            acc[...] += part
    c4.wait()
    done = slope_rows(acc, z4v, all_coefs(sum4[...], mid_gb(norms, 2)))
    out = go(acc, dv4, os.at[0])
    put_stats(stats, done)
    out.wait()


def back_four_kernel(zi, stb, norms, sum4, sum3, sums, z4, dv4, dv6, z3, zs, late, own, dpre, stats, grad, zv, dv, d6, z3v, zsv, dz, w, in4, ins, ws, os):
    cin = [go(z4, zv, in4.at[0]), go(dv4, dv, in4.at[1])]
    weight = bundle_in(late, 208, w, ws)
    wide = []
    for n in range(4):
        cols = quarter(n)
        wide.append(
            [
                go(src.at[:, cols], dst.at[:, cols], ins.at[i, n])
                for i, (src, dst) in enumerate(((dv6, d6), (z3, z3v), (zs, zsv)))
            ]
        )
    grads = added(stb)
    grads_out(grad, grads)
    cs4 = all_back(sum4[...], grads, mid_gb(norms, 2))
    wait(cin)
    norm_rows(dv, zv, cs4, slice(None), dz)
    own_cols(own, dz, zi, 128)
    wait(weight)
    wf = w.reshape(2048, 512)
    z8 = jnp.zeros((8, 512), F32)
    out = []
    for n in range(4):
        cols = quarter(n)
        s3, ss = sum3[:, cols], sums[:, cols]
        cs = []
        for k in (0, 1):
            m3, i3, a3, b3 = coefs(s3, k, M_OUT[k], out_gb(norms, 0, n))
            ms, is_, a5, b5 = coefs(ss, k, M_OUT[k], out_gb(norms, 1, n))
            cs.append((a3, a5, b3 + b5, m3, ms, i3, is_))
        zv[...] = dot_t(dz[...], wf[n * 512 : (n + 1) * 512, :])
        wait(wide[n])

        def body(group, start, rows, carry, cols=cols, cs=cs):
            a3, a5, b, m3, ms, _, _ = cs[group]
            here = (pl.ds(start, rows), cols)
            u, v = z3v[here], zsv[here]
            d = slope(u * a3 + v * a5 + b) * (zv[pl.ds(start, rows), :] + d6[here])
            d = jnp.where(keep(rows, 512, group, start), d, 0.0)
            d6[here] = d
            return (
                carry[0] + rows8(d),
                carry[1] + rows8(d * (u - m3)),
                carry[2] + rows8(d * (v - ms)),
            )

        done = sweep(body, (z8, z8, z8))
        out.append(go(d6.at[:, cols], dpre.at[:, cols], os.at[n]))
        done = [(s, p * cs[j][5], q * cs[j][6]) for j, (s, p, q) in enumerate(done)]
        put_stats(stats, done, cols)
    wait(out)


def pick(grads, rows):
    return jnp.concatenate([grads[r : r + 1] for r in rows], axis=0)


def back_three_kernel(zi, stb, norms, sum3, sum2, z3, dpre, z2, bundle, own, dv2, stats, grad, gsum, zv, dv, z2v, acc, dz, w, ins, i2, ws, os):
    cin = []
    for n in range(4):
        cols = quarter(n)
        cin.append(
            [go(z3.at[:, cols], zv.at[:, cols], ins.at[0, n]), go(dpre.at[:, cols], dv.at[:, cols], ins.at[1, n])]
        )
    weight = bundle_out_in(bundle, 144, w.reshape(32, 16, 2048), ws)
    c2 = go(z2, z2v, i2.at[0])
    for n in range(4):
        cols = quarter(n)
        grads = added(stb, cols)
        gsum[:, cols] = pick(grads, (0, 2, 3, 5))
        grads = pick(grads, (0, 1, 3, 4))
        grads_out(grad, grads, cols)
        cs = all_back(sum3[:, cols], grads, out_gb(norms, 0, n))
        wait(cin[n])
        norm_rows(dv, zv, cs, cols, dz)
        if n == 0:
            wait(weight)
            acc[...] = dot_t(dz[:, cols], w[:, cols])
        else:
            acc[...] += dot_t(dz[:, cols], w[:, cols])
    own_cols(own, dz, zi, 512)
    c2.wait()
    done = slope_rows(acc, z2v, all_coefs(sum2[...], mid_gb(norms, 1)))
    out = go(acc, dv2, os.at[0])
    put_stats(stats, done)
    out.wait()


def back_skip_kernel(zi, norms, gsum, sums, zs, dpre, *refs):
    srcs, rest = refs[:13], refs[13:]
    own, skip, grad, zv, dv, dz, w, ins, ws = rest
    cin = []
    for n in range(4):
        cols = quarter(n)
        cin.append(
            [go(zs.at[:, cols], zv.at[:, cols], ins.at[0, n]), go(dpre.at[:, cols], dv.at[:, cols], ins.at[1, n])]
        )
    mine = pl.ds(pl.multiple_of(zi[0] * 256, 256), 256)
    cols = [pl.ds(pl.multiple_of(zi[k] * 512, 512), 512) for k in range(4)]
    weight = [go(srcs[0].at[mine, :], w.at[:, cols[0]], ws.at[0])]
    which = jnp.where(zi[0] // 2 == zi[4], 0, 2) + zi[0] % 2
    for v in range(4):

        @pl.when(which == v)
        def _(v=v):
            for k in (1, 2, 3):
                go(srcs[1 + 6 * (v // 2) + 2 * (k - 1) + v % 2], w.at[:, cols[k]], ws.at[k])

    for n in range(4):
        here = quarter(n)
        grads = gsum[:, here]
        grads_out(grad, grads, here)
        cs = all_back(sums[:, here], grads, out_gb(norms, 1, n))
        wait(cin[n])
        norm_rows(dv, zv, cs, here, dz)
    own_cols(own, dz, zi, 512)
    wait(weight)
    for k in (1, 2, 3):
        pltpu.make_async_copy(srcs[1], w.at[:, cols[k]], ws.at[k]).wait()
    skip[...] = dot_t(dz[...], w[...])


def back_two_kernel(zi, stb, norms, sum2, sum1, z2, dv2, z1, near, *refs):
    (own, dv1, stats, grad, zv, dv, dz, acc, dzl, dzg, w, z1v, ins, ws, os) = refs
    cin = [go(z2, zv, ins.at[0]), go(dv2, dv, ins.at[1])]
    weight = bundle_in(near, 0, w, ws)
    c1 = go(z1, z1v, ins.at[2])
    grads = added(stb)
    grads_out(grad, grads)
    cs = all_back(sum2[...], grads, mid_gb(norms, 1))
    wait(cin)
    norm_rows(dv, zv, cs, slice(None), dv)
    own_cols(own, dv, zi, 128)
    pad_back(dzl, dzg, dv, 0)
    wait(weight)
    wf = w.reshape(4608, 512)
    gb1 = mid_gb(norms, 0)
    c1s = [coefs(sum1[...], k, M_IN[k], gb1) for k in (0, 1)]
    reach = (((1, 0),), ((2, 0), (0, 1)))
    z8 = jnp.zeros((8, 512), F32)
    totals = [(z8, z8), (z8, z8)]
    out = []
    for p in (0, 1):
        for q in (0, 1):
            first = True
            for i, di in reach[p]:
                for j, dj in reach[q]:
                    k = 3 * i + j
                    dz[...] = load_taps(dzl, dzg, di, dj, 1).astype(BF)
                    part = dot_t(dz[...], wf[k * 512 : (k + 1) * 512, :])
                    if first:
                        acc[...] = part
                    else:
                        acc[...] += part
                    first = False
            if p == 0 and q == 0:
                c1.wait()
            for group, (base, side, n, from_row) in enumerate(((0, 3, 16, 0), (576, 7, 8, 144))):
                m, _, a, sh = c1s[group]
                rows = side * n
                i_ = lax.broadcasted_iota(jnp.int32, (rows, 512), 0)
                okay = (i_ & 15) < 12 if group == 0 else (i_ & 7) < 6
                cells = z1v.at[pl.ds(base, 4 * side * side * n), :]
                cells = cells.reshape(side, 2, side, 2, n, 512)

                def step(r, carry, n=n, side=side, rows=rows, from_row=from_row, m=m, a=a, sh=sh, okay=okay, cells=cells, p=p, q=q):
                    v = cells[r, p, :, q].reshape(rows, 512)
                    g = acc[pl.ds(pl.multiple_of(from_row + r * rows, 8), rows), :]
                    d = jnp.where(okay, slope(v * a + sh) * g, 0.0)
                    cells[r, p, :, q] = d.reshape(side, n, 512)
                    return carry[0] + rows8(d), carry[1] + rows8(d * (v - m))

                totals[group] = lax.fori_loop(0, side, step, totals[group])
        for group, (first_row, steps, rows) in enumerate(LINES):
            for s in range(p, steps, 2):
                here = pl.ds(first_row + s * rows, rows)
                out.append(go(z1v.at[here, :], dv1.at[here, :], os.at[6 * group + s]))
    put_stats(stats, [(s, t * c1s[j][1]) for j, (s, t) in enumerate(totals)])
    wait(out)


def back_one_kernel(zi, stb, norms, sum1, z1, dv1, own, dz1, grad, zv, dv, dzv, is0, is1, os):
    lines_in(z1, zv, is0)
    lines_in(dv1, dv, is1)
    grads = added(stb)
    grads_out(grad, grads)
    cs = all_back(sum1[...], grads, mid_gb(norms, 0), M_IN)

    def body(group, s, start, rows, carry):
        a, c1, c0 = cs[group]
        line_wait(z1, zv, is0, group, s, start, rows)
        line_wait(dv1, dv, is1, group, s, start, rows)
        here = (pl.ds(start, rows), slice(None))
        i = lax.broadcasted_iota(jnp.int32, (rows, 512), 0)
        ok = (i & 15) < 12 if group == 0 else (i & 7) < 6
        d = a * dv[here] - c1 * zv[here] - c0
        dzv[here] = jnp.where(ok, d, 0.0).astype(BF)
        return carry

    wide_sweep(body, 0)
    out = go(dzv, dz1, os.at[0])
    own_cols(own, dzv, zi, 128)
    out.wait()


def image_kernel(zi, dz1, t0, t1, t2, t3, skip, local, glob, img, w, ws):
    wait(riding_in(zi, (t0, t1, t2, t3), w, ws))
    mine = w[pl.ds(pl.multiple_of(zi[0] * 256, 256), 256), :]
    for lane in range(2):
        cols = slice(lane * 128, lane * 128 + 128)
        img[lane] = dot_t(dz1[...], mine[lane * 128 : lane * 128 + 128])
        lv = img.at[lane, pl.ds(0, LIN)].reshape(3, 2, 3, 2, 16, 128)
        gv = img.at[lane, pl.ds(LIN, GIN)].reshape(7, 2, 7, 2, 8, 128)
        lv[:, 0, :, 0] += skip[pl.ds(0, LOUT), cols].reshape(3, 3, 16, 128)
        gv[:, 0, :, 0] += skip[pl.ds(LOUT, GOUT), cols].reshape(7, 7, 8, 128)
    unpack_kernel((6, 14), img, local, glob)


def flipped(a, bt):
    return dot(bt, a).T.astype(BF)


def halves_out(zi, a, bt, width, held, give, at):
    for c, dst in enumerate((held, give)):
        half = zi[4] if c == 0 else 1 - zi[4]
        begin = pl.multiple_of(half * width, width)
        for k in range(0, width, 256):
            n = min(256, width - k)
            v = flipped(a[:, pl.ds(pl.multiple_of(begin + k, 128), n)], bt)
            for j in range(v.shape[1] // 128):
                row = at + j * width + k
                dst[row : row + n, :] = v[:, 128 * j : 128 * (j + 1)]


def grad_kernel(widths, zi, *refs):
    held, give = refs[-2:]
    at = 0
    for i, width in enumerate(widths):
        a, b = refs[2 * i], refs[2 * i + 1]
        bt = b[...].astype(F32).T.astype(BF)
        halves_out(zi, a, bt, width, held, give, at)
        at += width * b.shape[1] // 128


def grad_call(name, zi, pairs):
    widths = [a.shape[1] // 2 for a, _ in pairs]
    rows = sum(a.shape[1] * b.shape[1] // 256 for a, b in pairs)
    return launch(
        name,
        functools.partial(grad_kernel, widths),
        [(zi, SM)] + [(v, VM) for pair in pairs for v in pair],
        [(shape((rows, 128), BF), VM)] * 2,
        (),
        (4 * ROUT * rows * 128, 7_000_000),
    )


def first_grad_kernel(zi, *refs):
    xs, (o1, held, give) = refs[:8], refs[8:]
    bt = o1[...].astype(F32).T.astype(BF)
    for k in range(4):
        v = dot(bt[:, :768], xs[2 * k][0:768, :]) + dot(bt[:, 896:], xs[2 * k + 1][96:, :])
        edge = jnp.concatenate([xs[2 * k][768:800, :], xs[2 * k + 1][0:96, :]], axis=0)
        v = v + dot(bt[:, 768:896], edge)
        v = v.T.astype(BF)
        mine = zi[4] == k // 2
        rows = slice((k % 2) * 256, (k % 2) * 256 + 256)

        @pl.when(mine)
        def _():
            held[rows, :] = v

        @pl.when(jnp.logical_not(mine))
        def _():
            give[rows, :] = v


SPANS = (
    (6, 0, 1024),
    (5, 1024, 3328),
    (4, 3328, 4352),
    (2, 4352, 5376),
    (3, 5376, 7424),
), ((1, 0, 2304), (0, 2304, 2816))


def slice_kernel(at, some, rest, out):
    squares = [jnp.zeros((1, 128), F32)] * 8
    first = 0
    for src, spans in zip((some, rest), SPANS):
        n = src.shape[1]
        v = src[0].astype(F32)
        for p in range(1, 16):
            v = v + src[p].astype(F32)
        out[first : first + n, :] = v.astype(BF)
        first += n
        v = v * v
        row = lax.broadcasted_iota(jnp.int32, (n, 128), 0) + at[0] * n
        for i, lo, hi in spans:
            squares[i] = row1(jnp.where((row >= lo) & (row < hi), v, 0.0))
    left = jnp.concatenate(squares + squares, axis=0)
    for k in range(3):
        part = left.astype(BF)
        out[first + 16 * k : first + 16 * k + 16, :] = part
        left = left - part.astype(F32)


def spill_kernel(other, zi, src, *refs):
    refs = refs[7:] if other else refs
    outs, (v6, v5, v4, v3, vs, v2, v1, fa, fb, ins, sem) = refs[:7], refs[7:]
    cin = [
        go(src.at[:, pl.ds(0, 464), :], fa.reshape(16, 464, 128), ins.at[0]),
        go(src.at[:, pl.ds(464, 176), :], fb.reshape(16, 176, 128), ins.at[1]),
    ]
    c = 1 - zi[4] if other else zi[4]
    copies = []
    plan = (
        (v5, 1, fa, 1024, 2304, 1),
        (vs, 4, fa, 5376, 512, 4),
        (v6, 0, fa, 0, 256, 4),
        (v4, 2, fa, 3328, 1024, 1),
        (v3, 3, fa, 4352, 256, 4),
        (v2, 5, fb, 0, 2304, 1),
    )
    cin[0].wait()
    for dst, i, flat, at, n, blocks in plan:
        if i == 5:
            cin[1].wait()
        for j in range(blocks):
            dst[:, 128 * j : 128 * (j + 1)] = flat[at + j * n : at + (j + 1) * n, :].astype(F32)
        rows = pl.ds(pl.multiple_of(c * n, n), n)
        copies.append(go(dst, outs[i].at[rows, :], sem.at[i]))
    for k in range(2):
        v1[256 * k : 256 * (k + 1), :] = fb[2304 + 256 * k : 2560 + 256 * k, :].astype(F32)
        rows = pl.ds(pl.multiple_of(zi[2 * c + k] * 256, 256), 256)
        copies.append(go(v1.at[pl.ds(256 * k, 256), :], outs[6].at[rows, :], sem.at[6 + k]))
    wait(copies)


GRADS = ((512, 512), (4608, 128), (2048, 128), (512, 512), (1024, 512), (4608, 128), (1024, 128))


def spill(name, zi, src, before):
    other = bool(before)
    return pl.pallas_call(
        functools.partial(spill_kernel, other),
        name=name,
        out_shape=tuple(pltpu.HBM(d, F32) for d in GRADS),
        in_specs=[SM, ANY] + [ANY] * len(before),
        out_specs=tuple(ANY for _ in GRADS),
        scratch_shapes=[pltpu.VMEM((r // 2, c), F32) for r, c in GRADS]
        + [pltpu.VMEM((7424, 128), BF), pltpu.VMEM((2816, 128), BF), sems(2), sems(8)],
        input_output_aliases={2 + i: i for i in range(len(before))},
        compiler_params=pltpu.CompilerParams(vmem_limit_bytes=50 * 1024 * 1024),
        cost_estimate=pl.CostEstimate(flops=0, bytes_accessed=8_000_000, transcendentals=0),
    )(zi, src, *before)


def ring(n, k):
    return [(i, (i + k) % n) for i in range(n)]


def spread(v, axes, n):
    return lax.all_to_all(jnp.broadcast_to(v[None], (n,) + v.shape), axes, 0, 0)


def share(v):
    v = v + lax.ppermute(v, "c", ring(2, 1))
    return spread(v, PLANE, 16)


def tell(v):
    return lax.all_to_all(v, BATCH, 0, 0)


def tie(*vs):
    return lax.optimization_barrier(vs)


def plane_index():
    return lax.axis_index("y") * 4 + lax.axis_index("x")


def piece(shard, index):
    n = shard.shape[0] // 32
    return lax.dynamic_slice_in_dim(shard, index * n, n, 0)


def swap(v):
    return lax.ppermute(v, "c", ring(2, 1))


def around(parts):
    left = [lax.ppermute(v, "z", ring(4, 1)) for v in parts]
    right = [lax.ppermute(v, "z", ring(4, 3)) for v in parts]
    left[0], left[1], right[0], right[1] = tie(*left, *right)
    far = [lax.ppermute(left[0], "z", ring(4, 1)), lax.ppermute(right[1], "z", ring(4, 3))]
    return right, far, left


def after(v, *first):
    return tie(v, *first)[0]


def add_halves(held, give):
    return (held.astype(F32) + swap(give).astype(F32)).astype(BF)


def body(
    image_global,
    image_local,
    cotangent_global,
    cotangent_local,
    reduce_one,
    spatial_one,
    expand_one,
    shortcut,
    reduce_two,
    spatial_two,
    expand_two,
    factors_mid,
    factors_out,
    shifts_mid,
    shifts_out,
):
    zi = lax.axis_index("z")
    ci = lax.axis_index("c")
    where = jnp.stack([zi, (zi + 1) % 4, (zi + 2) % 4, (zi + 3) % 4, ci]).astype(jnp.int32)
    flat2, flat5 = spatial_one.reshape(-1, 128), spatial_two.reshape(-1, 128)
    own = [reduce_one, flat2, expand_one, shortcut, reduce_two, flat5, expand_two]

    x = pack(
        "pack_image", image_local, image_global, (6, 14), (TOP, RIN - TOP), (reduce_one,)
    )
    x_right, x_far, x_left = around(x)
    xs = tuple(x) + tuple(x_right) + tuple(x_far) + tuple(x_left)

    norms = jnp.concatenate(
        [factors_mid, shifts_mid, factors_out.reshape(12, 128), shifts_out.reshape(12, 128)]
    )
    norms = after(norms, x[0])
    high = lax.reduce_precision(norms, 8, 7)
    middle = lax.reduce_precision(norms - high, 8, 7)
    low = norms - high - middle
    norms = spread(jnp.concatenate([v.astype(BF) for v in (high, middle, low)]), "z", 4)
    norms = norms[:, 0:32].astype(F32) + norms[:, 32:64].astype(F32) + norms[:, 64:96].astype(F32)

    xs = tuple(after(v, norms) for v in xs)

    near, late = launch(
        "pieces",
        pieces_kernel,
        [((plane_index() * 2 + ci).reshape(1).astype(jnp.int32), SM)]
        + [(after(v, x[0]), ANY) for v in (flat2, expand_one, reduce_two, flat5, expand_two)],
        [(shape((272, 128), BF), VM), (shape((208, 128), BF), VM)],
        [sems(14)],
    )
    near = lax.all_gather(near, EVERY, axis=0).reshape(32, 4, 272, 128)
    late = lax.all_gather(late, EVERY, axis=0).reshape(32, 4, 208, 128)

    cot = pack("pack_cotangent", cotangent_local, cotangent_global, (3, 7), (272, 272))
    c_right, c_far, c_left = around(cot)
    cots = tuple(cot) + tuple(c_right) + tuple(c_far) + tuple(c_left)
    square = launch(
        "weight_squares",
        square_kernel,
        [(w, VM) for w in own],
        [(shape((7, 8, 128)), VM)],
        (),
        (0, 6_000_000),
    )[0]

    mid_stats = (shape((32, 4, 512)), FAR)
    out_stats = (shape((4, 2048)), VM)
    narrow, wide = (shape((ROUT, 512)), ANY), (shape((ROUT, 2048)), ANY)
    z1, s1 = launch(
        "reduce_one",
        first_kernel,
        [(where, SM)] + [(v, ANY) for v in xs],
        [(shape((RIN, 512)), ANY), mid_stats],
        [
            pltpu.VMEM((RIN, 1024), BF),
            pltpu.VMEM((RIN, 512), F32),
            pltpu.VMEM((1024, 512), BF),
            sems(4, 4),
            sems(4),
            sems(8),
        ],
        (2 * RIN * 1024 * 512, 10_000_000),
    )
    parts = [lax.dynamic_slice_in_dim(shortcut, ci * 512 + 256 * i, 256, 0) for i in (0, 1)]
    st1 = tell(s1)
    p_right, p_far, p_left = around([after(v, st1) for v in parts])
    skips = tuple(p_right) + tuple(p_far) + tuple(p_left)
    skips = (shortcut,) + skips + tuple(swap(v) for v in skips)
    t1, z2, s2, sum1 = conv_call(
        "spatial_one",
        second_kernel,
        [(st1, NEAR), (norms, VM), (z1, ANY), (near, ANY)],
        RIN,
        (8, 16),
        20,
        40_000_000_000,
    )
    st2 = tell(s2)
    xe, zs, ss = launch(
        "shortcut",
        skip_kernel,
        [(where, SM)] + [(v, ANY) for v in xs + skips],
        [(shape((ROUT, 1024), BF), ANY), wide, out_stats],
        [
            pltpu.VMEM((4, RIN, 256), BF),
            pltpu.VMEM((ROUT, 1024), BF),
            pltpu.VMEM((ROUT, 256), F32),
            pltpu.VMEM((ROUT, 2048), F32),
            pltpu.VMEM((1024, 2048), BF),
            sems(4, 2),
            sems(16),
            sems(1),
            sems(4),
        ],
        (2 * ROUT * 1024 * 2048, 14_000_000),
    )
    h2, z3, s3, sum2 = expand_call(
        "expand_one", 1, 144, st2, norms, z2, near
    )
    st3 = share(jnp.concatenate([s3, ss]))
    mid, h3, z4, s4, sum3, sums = launch(
        "reduce_two",
        middle_kernel,
        [(st3, NEAR), (norms, VM), (z3, ANY), (zs, ANY), (near, ANY)],
        [wide, (shape((ROUT, 2048), BF), ANY), narrow, mid_stats, out_stats, out_stats],
        [
            pltpu.VMEM((ROUT, 2048), F32),
            pltpu.VMEM((ROUT, 2048), F32),
            pltpu.VMEM((ROUT, 2048), BF),
            pltpu.VMEM((ROUT, 512), F32),
            pltpu.VMEM((32, 64, 512), BF),
            sems(2, 4),
            sems(4),
            sems(4),
            sems(4),
            sems(1),
        ],
        (2 * ROUT * 2048 * 512, 20_000_000),
    )
    st4 = tell(s4)
    st4, square = tie(st4, square)
    t4, z5, s5, sum4 = conv_call(
        "spatial_two",
        fifth_kernel,
        [(st4, NEAR), (norms, VM), (z4, ANY), (late, ANY)],
        ROUT,
        (5, 9),
        1,
        2 * 544 * 4608 * 512,
    )
    st5 = tell(s5)
    h5, z6, s6, sum5 = expand_call("expand_two", 3, 144, st5, norms, z5, late)
    st6 = share(s6)
    out, dv6, b6, sum6 = launch(
        "output",
        last_kernel,
        [(where, SM), (st6, NEAR), (norms, VM)] + [(v, ANY) for v in (z6, mid) + cots],
        [narrow, wide, out_stats, out_stats],
        [
            pltpu.VMEM((4, ROUT, 512), F32),
            pltpu.VMEM((4, ROUT, 512), F32),
            pltpu.VMEM((4, ROUT, 512), BF),
            pltpu.VMEM((ROUT, 512), F32),
            sems(4, 4),
            sems(5),
        ],
        (0, 20_000_000),
    )
    output_local, output_global = unpack("unpack_output", out, (3, 7))
    bt6 = share(b6)
    bt6, output_local, output_global = tie(bt6, output_local, output_global)

    wide_in = [pltpu.VMEM((ROUT, 2048), F32), pltpu.VMEM((ROUT, 2048), F32)]
    flat = [pltpu.VMEM((ROUT, 512), F32)]
    mid_grad, out_grad = (shape((2, 512)), VM), (shape((2, 2048)), VM)
    own_mid, own_out = (shape((ROUT, 128), BF), VM), (shape((ROUT, 512), BF), VM)
    o6, dv5, b5, gr6 = launch(
        "back_expand_two",
        back_six_kernel,
        [(where, SM), (bt6, NEAR), (norms, VM), (sum6, VM), (sum5, VM)]
        + [(v, ANY) for v in (z6, dv6, z5, late)],
        [own_out, narrow, mid_stats, out_grad],
        wide_in
        + flat * 2
        + [
            pltpu.VMEM((ROUT, 2048), BF),
            pltpu.VMEM((512, 2048), BF),
            sems(2, 4),
            sems(1),
            sems(16),
            sems(1),
        ],
        (2 * ROUT * 2048 * 512, 14_000_000),
    )
    bt5 = tell(b5)
    gw6 = grad_call("grad_expand_two", where, [(h5, o6)])
    bt5, *gw6 = tie(bt5, *gw6)
    conv_weight = [pltpu.VMEM((32, 144, 512), BF)]
    o5, dv4, b4, gr5 = launch(
        "back_spatial_two",
        back_five_kernel,
        [(where, SM), (bt5, NEAR), (norms, VM), (sum5, VM), (sum4, VM)]
        + [(v, ANY) for v in (z5, dv5, z4, late)],
        [own_mid, narrow, mid_stats, mid_grad],
        flat * 4
        + [
            pltpu.VMEM((ROUT, 512), BF),
            pltpu.VMEM((5, 5, 16, 512), F32),
            pltpu.VMEM((9, 9, 8, 512), F32),
        ]
        + conv_weight
        + [sems(3), sems(4), sems(1)],
        (2 * ROUT * 4608 * 512, 10_000_000),
    )
    bt4 = tell(b4)
    gw5 = grad_call("grad_spatial_two", where, [(t4, o5)])
    bt4, *gw5 = tie(bt4, *gw5)
    o4, dpre, b3, gr4 = launch(
        "back_reduce_two",
        back_four_kernel,
        [(where, SM), (bt4, NEAR), (norms, VM), (sum4, VM), (sum3, VM), (sums, VM)]
        + [(v, ANY) for v in (z4, dv4, dv6, z3, zs, near)],
        [own_mid, wide, (shape((6, 2048)), VM), mid_grad],
        flat * 2
        + wide_in
        + wide_in[:1]
        + [
            pltpu.VMEM((ROUT, 512), BF),
            pltpu.VMEM((32, 64, 512), BF),
            sems(2),
            sems(3, 4),
            sems(4),
            sems(4),
        ],
        (2 * ROUT * 2048 * 512, 22_000_000),
    )
    bt3 = share(b3)
    gw4 = grad_call("grad_reduce_two", where, [(h3, o4)])
    bt3, *gw4 = tie(bt3, *gw4)
    o3, dv2, b2, gr3, gsum = launch(
        "back_expand_one",
        back_three_kernel,
        [(where, SM), (bt3, NEAR), (norms, VM), (sum3, VM), (sum2, VM)]
        + [(v, ANY) for v in (z3, dpre, z2, near)],
        [own_out, narrow, mid_stats, out_grad, out_stats],
        wide_in
        + flat * 2
        + [
            pltpu.VMEM((ROUT, 2048), BF),
            pltpu.VMEM((512, 2048), BF),
            sems(2, 4),
            sems(1),
            sems(16),
            sems(1),
        ],
        (2 * ROUT * 2048 * 512, 16_000_000),
    )
    bt2 = tell(b2)
    o_s, skip, grs = launch(
        "back_shortcut",
        back_skip_kernel,
        [(where, SM), (norms, VM), (gsum, VM), (sums, VM)]
        + [(v, ANY) for v in (zs, dpre) + skips],
        [own_out, (shape((ROUT, 256)), VM), out_grad],
        wide_in
        + [pltpu.VMEM((ROUT, 2048), BF), pltpu.VMEM((256, 2048), BF), sems(2, 4), sems(16)],
        (2 * ROUT * 2048 * 256, 10_000_000),
    )
    pair = grad_call("grad_pair", where, [(h2, o3), (xe, o_s)])
    bt2, skip, *pair = tie(bt2, skip, *pair)
    o2, dv1, b1, gr2 = launch(
        "back_spatial_one",
        back_two_kernel,
        [(where, SM), (bt2, NEAR), (norms, VM), (sum2, VM), (sum1, VM)]
        + [(v, ANY) for v in (z2, dv2, z1, near)],
        [own_mid, (shape((RIN, 512)), ANY), mid_stats, mid_grad],
        flat * 2
        + [
            pltpu.VMEM((ROUT, 512), BF),
            pltpu.VMEM((ROUT, 512), F32),
            pltpu.VMEM((4, 4, 16, 512), F32),
            pltpu.VMEM((8, 8, 8, 512), F32),
        ]
        + conv_weight
        + [pltpu.VMEM((RIN, 512), F32), sems(3), sems(4), sems(20)],
        (2 * ROUT * 4608 * 512, 20_000_000),
    )
    bt1 = tell(b1)
    conv = grad_call("grad_spatial_one", where, [(t1, o2)])
    some = jnp.concatenate([add_halves(*v) for v in (gw6, gw5, gw4, pair)]).reshape(16, 464, 128)
    bt1, some, *conv = tie(bt1, some, *conv)
    some = lax.all_to_all(some, PLANE, 0, 0)
    o1, dz1, gr1 = launch(
        "back_reduce_one",
        back_one_kernel,
        [(where, SM), (bt1, NEAR), (norms, VM), (sum1, VM), (z1, ANY), (dv1, ANY)],
        [(shape((RIN, 128), BF), VM), (shape((RIN, 512), BF), ANY), mid_grad],
        [
            pltpu.VMEM((RIN, 512), F32),
            pltpu.VMEM((RIN, 512), F32),
            pltpu.VMEM((RIN, 512), BF),
            sems(20),
            sems(20),
            sems(1),
        ],
        (0, 12_000_000),
    )
    first = launch(
        "grad_reduce_one",
        first_grad_kernel,
        [(where, SM)] + [(v, VM) for v in xs + (o1,)],
        [(shape((512, 128), BF), VM)] * 2,
        (),
        (2 * RIN * 1024 * 128, 6_000_000),
    )
    rest = jnp.concatenate([add_halves(*conv), add_halves(*first)]).reshape(16, 176, 128)
    some, rest = tie(some, rest)
    rest = lax.all_to_all(rest, PLANE, 0, 0)
    slice_ = launch(
        "slice",
        slice_kernel,
        [(plane_index().reshape(1).astype(jnp.int32), SM), (some, VM), (rest, VM)],
        [(shape((688, 128), BF), VM)],
        (),
        (0, 3_000_000),
    )[0]
    dimage_local, dimage_global = launch(
        "image_grad",
        image_kernel,
        [(where, SM), (dz1, VM)] + [(v, ANY) for v in xs[::2]] + [(skip, VM)],
        [(shape((12, 6, 6, 256)), VM), (shape((6, 14, 14, 256)), VM)],
        [pltpu.VMEM((2, RIN, 128), F32), pltpu.VMEM((1024, 512), BF), sems(8)],
        (2 * RIN * 512 * 256, 8_000_000),
    )
    slice_, dimage_local, dimage_global = tie(slice_, dimage_local, dimage_global)
    held = spread(slice_, PLANE, 16)
    given = swap(held)
    grads = spill("grads_kept", where, held, ())
    given, *grads = tie(given, *grads)
    t6, t5, t4w, t3, ts, t2, t1w = spill("grads_given", where, given, grads)

    def squares(v):
        v = v[:, 640:688].astype(F32).reshape(16, 3, 16, 128)[:, :, :8]
        return jnp.sum(v, axis=(0, 1, 3))

    grad_sq = squares(held) + squares(given)
    weight_sq = jnp.pad(jnp.sum(square, axis=(1, 2)), (0, 1))
    sq = jnp.concatenate([weight_sq[None], grad_sq[None]])
    sq = sq + lax.ppermute(sq, "z", ring(4, 2))
    sq = (sq + lax.ppermute(sq, "z", ring(4, 1)))[:, :7]
    weight_norm = jnp.sqrt(sq[0])
    ratios = weight_norm / (jnp.sqrt(sq[1]) / 12864.0 + DECAY * weight_norm)

    def cut_own(v, n):
        return lax.dynamic_slice_in_dim(v, zi * n, n, 2)

    mids = cut_own(jnp.stack([gr1, gr2, gr4, gr5]), 128)
    wides = cut_own(jnp.stack([gr3, grs, gr6]), 512)
    return (
        output_global,
        output_local,
        dimage_global,
        dimage_local,
        t1w,
        t2.reshape(spatial_one.shape),
        t3,
        ts,
        t4w,
        t5.reshape(spatial_two.shape),
        t6,
        mids[:, 1],
        wides[:, 1],
        mids[:, 0],
        wides[:, 0],
        ratios,
    )


def solution(mesh):
    fine = Mesh(np.asarray(mesh.devices).reshape(4, 4, 2, 4), EVERY)
    crops = P(BATCH, None, None, "z")
    mat = P(None, "z")
    conv = P(None, None, None, "z")
    weights = (mat, conv, mat, mat, mat, conv, mat)
    return jax.shard_map(
        body,
        mesh=fine,
        in_specs=(crops,) * 4 + weights + (mat,) * 4,
        out_specs=(crops,) * 4 + weights + (mat,) * 4 + (P(),),
        check_vma=False,
    )
```

time: 690 us -> 550 us (0.80)
  waiting for transfers between devices: 226 us -> 156 us
  blocking collectives: 8.75 us -> 61.2 us
  local copies, waits for them, and re-layouts: 57.7 us -> 19.8 us
  starting transfers between devices: 145 us -> 112 us
  other arithmetic: 40.9 us -> 8.02 us
  matrix products: 23.2 us -> 0 us
  Pallas kernels: 161 us -> 168 us
    all_to_all x0 -> x2, blocking collectives: none -> 61.2 us  [spread(): return lax.all_to_all(jnp.broadcast_to(v[None], (n,) + v.shape), axes, 0, 0)]
    all_to_all x11 -> x4, waiting for transfers between devices: 80.2 us -> 37.2 us  [spread(): return lax.all_to_all(jnp.broadcast_to(v[None], (n,) + v.shape), axes, 0, 0)]
    all_to_all x11 -> x4, starting transfers between devices: 59.1 us -> 17.4 us  [spread(): return lax.all_to_all(jnp.broadcast_to(v[None], (n,) + v.shape), axes, 0, 0)]
    dot_general x14 -> x0, matrix products: 23.2 us -> none  [the longest x10 21 us: dot_w(): lax.dot_general(a, b, (((0,), (0,)), ((), ())), preferred_element_type=F32)]
    reduce_sum x14 -> x2, other arithmetic: 19.7 us -> 0.32 us  [the longest x1 0.19 us: squares(): return jnp.sum(v, axis=(0, 1, 3))]
    all_to_all x2, waiting for transfers between devices: 33.8 us -> 20.6 us  [the longest x1 15.6 us: body(): some = lax.all_to_all(some, PLANE, 0, 0)]
    another operation x2 -> x0, local copies, waits for them, and re-layouts: 9.11 us -> none  [the longest x1 4.61 us: body(): weight_sq = jnp.stack([jnp.sum(jnp.square(w.astype(F32))) for w in own])]
    broadcast_in_dim x11 -> x6, local copies, waits for them, and re-layouts: 13.1 us -> 3.97 us  [spread(): return lax.all_to_all(jnp.broadcast_to(v[None], (n,) + v.shape), axes, 0, 0)]
  transfers between devices with their start and end apart: 44 -> 53, of which waited for: 28 -> 30; matrix products, arithmetic and copies ran while one was open for 12% -> 2% of each run, Pallas kernels for 13% -> 22%
where the time goes in v1:
time: 550 us; the launch traced here: 541 us
  Pallas kernels  168 us (31%)
  waiting for transfers between devices  156 us (28%)
  starting transfers between devices  112 us (20%)
  blocking collectives  61.2 us (11%)
  local copies, waits for them, and re-layouts  19.8 us (4%)
  between operations  15.8 us (3%)
  other arithmetic  8.02 us (1%)
    pallas_call x28, Pallas kernels, launch(): pl.pallas_call(body, name=name, out_shape=tuple((pltpu.HBM(o.shape, o.dty...  160 us
    all_to_all x2, blocking collectives, spread(): return lax.all_to_all(jnp.broadcast_to(v[None], (n,) + v.shape), axes, 0, 0)  61.2 us
    all_to_all x8, starting transfers between devices, tell(): return lax.all_to_all(v, BATCH, 0, 0)  50.9 us
    all_to_all x4, waiting for transfers between devices, spread(): return lax.all_to_all(jnp.broadcast_to(v[None], (n,) + v.shape), axes, 0, 0)  37.2 us
    ppermute x6, waiting for transfers between devices, around(): right = [lax.ppermute(v, 'z', ring(4, 3)) for v in parts]  32.1 us
    all_to_all x8, waiting for transfers between devices, tell(): return lax.all_to_all(v, BATCH, 0, 0)  30.2 us
    all_to_all x4, starting transfers between devices, spread(): return lax.all_to_all(jnp.broadcast_to(v[None], (n,) + v.shape), axes, 0, 0)  17.4 us
    all_to_all x1, waiting for transfers between devices, body(): some = lax.all_to_all(some, PLANE, 0, 0)  15.6 us
  transfers between devices with their start and end apart: 53, of which 30 were waited for; matrix products, arithmetic and copies ran while one was open for 2% of the time, Pallas kernels for 22%

profile of v1, /device:TPU:1, one launch (start us, length us, event | category | flops | bytes accessed | tf_op | source)
XLA Modules:
  0.0 540.7 jit_solution(1346375274566914139)
XLA Ops:
  21.4 26.5 %collective-permute-done.2.refs_2_.t1 = bf16[1312,256]{1,0:T(8,128)(2,1)S(1)} collective-permute-done((bf16[1312,256]{1,0:T(8,128)(2,1)S(1)}, bf16[1312,256]{1,0:T(8,128)(2,1)S(1)}, u32[]{:S(2)}, u32[]{:S(2)}) %collective-permute-start.2) | collective-permute-done | bytes 671776 | tf_op jit(solution)/shard_map/ppermute | solution.py:1192
  57.9 12.1 %all-to-all-done = bf16[4,96,128]{2,1,0:T(8,128)(2,1)S(1)} async-done(((bf16[4,96,128]{2,1,0:T(8,128)(2,1)}), bf16[4,96,128]{2,1,0:T(8,128)(2,1)S(1)}, u32[]{:S(2)}, u32[]{:S(2)}) %all-to-all-start) | async-done | bytes 98336 | tf_op jit(solution)/shard_map/all_to_all | solution.py:1161
  70.1 8.0 %reduce_one.1 = (f32[2144,512]{1,0:T(8,128)}, f32[32,4,512]{2,1,0:T(4,128)}) custom-call(s32[5]{0:T(128)S(1)} %stack.50.zi, bf16[1312,256]{1,0:T(8,128)(2,1)} %copy-done.2, bf16[1344,256]{1,0:T(8,128)(2,1)} %copy-done.9, bf16[1312,256]{1,0:T(8,128)(2,1)} %copy-done.4, bf16[1344,256]{1,0:T(8,128)(2,1)} %collective-permute-done.3.refs_3_, ...), custom_call_target="tpu_custom_call" | custom-call | flops 2248146944 | bytes 10000000 | tf_op jit(solution)/shard_map/reduce_one/pallas_call | solution.py:43
  78.1 14.2 %all-to-all-start.1 = ((f32[32,4,512]{2,1,0:T(4,128)}), f32[32,4,512]{2,1,0:T(4,128)S(1)}, u32[]{:S(2)}, u32[]{:S(2)}) async-start(f32[32,4,512]{2,1,0:T(4,128)} %get-tuple-element.188), calls=%async_computation.1 | async-start | bytes 524288 | tf_op jit(solution)/shard_map/all_to_all | solution.py:1170
  92.4 8.8 %all-to-all-done.1.st = f32[32,4,512]{2,1,0:T(4,128)S(1)} async-done(((f32[32,4,512]{2,1,0:T(4,128)}), f32[32,4,512]{2,1,0:T(4,128)S(1)}, u32[]{:S(2)}, u32[]{:S(2)}) %all-to-all-start.1) | async-done | bytes 262176 | tf_op jit(solution)/shard_map/all_to_all | solution.py:1170
  123.0 6.9 %collective-permute-done.11.refs_12_.refs_4_ = bf16[256,512]{1,0:T(8,128)(2,1)S(1)} collective-permute-done((bf16[256,512]{1,0:T(8,128)(2,1)S(1)}, bf16[256,512]{1,0:T(8,128)(2,1)S(1)}, u32[]{:S(2)}, u32[]{:S(2)}) %collective-permute-start.11) | collective-permute-done | bytes 262176 | tf_op jit(solution)/shard_map/ppermute | solution.py:1194
  132.3 8.6 %spatial_one.1 = (bf16[544,4608]{1,0:T(8,128)(2,1)}, f32[544,512]{1,0:T(8,128)}, f32[32,4,512]{2,1,0:T(4,128)}, f32[4,512]{1,0:T(4,128)S(1)}) custom-call(f32[32,4,512]{2,1,0:T(4,128)S(1)} %all-to-all-done.1.st, f32[4,32,128]{2,1,0:T(8,128)S(1)} %convert_add_fusion.norms, f32[2144,512]{1,0:T(8,128)} %get-tuple-element.189.z1, bf16[32,4,272,128]{3,2,1,0:T(8,128)(2,1)} %bitcast.52), custom_call_target="tpu_custom_call" | custom-call | flops 40000000000 | bytes 20000000 | tf_op jit(solution)/shard_map/spatial_one/pallas_call | solution.py:43
  145.5 9.2 %shortcut.1 = (bf16[544,1024]{1,0:T(8,128)(2,1)}, f32[544,2048]{1,0:T(8,128)}, f32[4,2048]{1,0:T(4,128)S(1)}) custom-call(s32[5]{0:T(128)S(1)} %stack.50.zi, bf16[1312,256]{1,0:T(8,128)(2,1)} %copy-done.2, bf16[1344,256]{1,0:T(8,128)(2,1)} %copy-done.9, bf16[1312,256]{1,0:T(8,128)(2,1)} %copy-done.4, bf16[1344,256]{1,0:T(8,128)(2,1)} %collective-permute-done.3.refs_3_, ...), custom_call_target="tpu_custom_call" | custom-call | flops 2281701376 | bytes 14000000 | tf_op jit(solution)/shard_map/shortcut/pallas_call | solution.py:43
  154.8 5.4 %expand_one.2 = (bf16[544,512]{1,0:T(8,128)(2,1)}, f32[544,2048]{1,0:T(8,128)}, f32[4,2048]{1,0:T(4,128)S(1)}, f32[4,512]{1,0:T(4,128)S(1)}) custom-call(f32[32,4,512]{2,1,0:T(4,128)S(1)} %all-to-all-done.2.st, f32[4,32,128]{2,1,0:T(8,128)S(1)} %convert_add_fusion.norms, f32[544,512]{1,0:T(8,128)} %get-tuple-element.197.z.z2, bf16[32,4,272,128]{3,2,1,0:T(8,128)(2,1)} %bitcast.53), custom_call_target="tpu_custom_call" | custom-call | flops 1140850688 | bytes 9000000 | tf_op jit(solution)/shard_map/expand_one/pallas_call | solution.py:43
  161.7 23.0 %all_to_all.80.st3 = f32[16,8,2048]{2,1,0:T(8,128)S(1)} all-to-all(f32[16,8,2048]{2,1,0:T(8,128)S(1)} %broadcast_in_dim.15), channel_id=1, replica_groups=mesh['y'=4,'x'=4,'c'=2,'z'=4] {'y','x'}, dimensions={0} | all-to-all | bytes 2097152 | tf_op jit(solution)/shard_map/all_to_all | solution.py:1161
  184.7 10.1 %reduce_two.2 = (f32[544,2048]{1,0:T(8,128)}, bf16[544,2048]{1,0:T(8,128)(2,1)}, f32[544,512]{1,0:T(8,128)}, f32[32,4,512]{2,1,0:T(4,128)}, f32[4,2048]{1,0:T(4,128)S(1)}, /*index=5*/f32[4,2048]{1,0:T(4,128)S(1)}) custom-call(f32[16,8,2048]{2,1,0:T(8,128)S(1)} %all_to_all.80.st3, f32[4,32,128]{2,1,0:T(8,128)S(1)} %convert_add_fusion.norms, ...), custom_call_target="tpu_custom_call" | custom-call | flops 1140850688 | bytes 20000000 | tf_op jit(solution)/shard_map/reduce_two/pallas_call | solution.py:43
  194.7 6.4 %all-to-all-start.4 = ((f32[32,4,512]{2,1,0:T(4,128)}), f32[32,4,512]{2,1,0:T(4,128)}, u32[]{:S(2)}, u32[]{:S(2)}) async-start(f32[32,4,512]{2,1,0:T(4,128)} %get-tuple-element.208), calls=%async_computation.4 | async-start | bytes 524288 | tf_op jit(solution)/shard_map/all_to_all | solution.py:1170
  210.1 8.4 %spatial_two.1 = (bf16[544,4608]{1,0:T(8,128)(2,1)}, f32[544,512]{1,0:T(8,128)}, f32[32,4,512]{2,1,0:T(4,128)}, f32[4,512]{1,0:T(4,128)S(1)}) custom-call(f32[32,4,512]{2,1,0:T(4,128)} %all-to-all-done.4.st, f32[4,32,128]{2,1,0:T(8,128)S(1)} %convert_add_fusion.norms, f32[544,512]{1,0:T(8,128)} %get-tuple-element.210.z4, bf16[32,4,208,128]{3,2,1,0:T(8,128)(2,1)} %bitcast.58), custom_call_target="tpu_custom_call" | custom-call | flops 2566914048 | bytes 20000000 | tf_op jit(solution)/shard_map/spatial_two/pallas_call | solution.py:43
  227.1 5.4 all-to-all-done.5.st
  232.5 5.3 expand_two.2
  245.3 6.5 %collective-permute-done.25.refs_5_ = bf16[272,512]{1,0:T(8,128)(2,1)S(1)} collective-permute-done((bf16[272,512]{1,0:T(8,128)(2,1)S(1)}, bf16[272,512]{1,0:T(8,128)(2,1)S(1)}, u32[]{:S(2)}, u32[]{:S(2)}) %collective-permute-start.25) | collective-permute-done | bytes 278560 | tf_op jit(solution)/shard_map/ppermute | solution.py:1194
  254.8 8.0 %output.1 = (f32[544,512]{1,0:T(8,128)}, f32[544,2048]{1,0:T(8,128)}, f32[4,2048]{1,0:T(4,128)S(1)}, f32[4,2048]{1,0:T(4,128)S(1)}) custom-call(s32[5]{0:T(128)S(1)} %stack.50.zi, f32[16,4,2048]{2,1,0:T(4,128)S(1)} %all-to-all-done.6.st, f32[4,32,128]{2,1,0:T(8,128)S(1)} %convert_add_fusion.norms, f32[544,2048]{1,0:T(8,128)} %get-tuple-element.215.z6, ...), custom_call_target="tpu_custom_call" | custom-call | bytes 20000000 | tf_op jit(solution)/shard_map/output/pallas_call | solution.py:43
  266.2 6.8 %all-to-all-start.7 = ((f32[16,4,2048]{2,1,0:T(4,128)}), f32[16,4,2048]{2,1,0:T(4,128)S(1)}, u32[]{:S(2)}, u32[]{:S(2)}) async-start(f32[16,4,2048]{2,1,0:T(4,128)} %broadcast_in_dim.17), calls=%async_computation.7 | async-start | bytes 1048576 | tf_op jit(solution)/shard_map/all_to_all | solution.py:1161
  274.3 9.5 %all-to-all-done.7.stb = f32[16,4,2048]{2,1,0:T(4,128)S(1)} async-done(((f32[16,4,2048]{2,1,0:T(4,128)}), f32[16,4,2048]{2,1,0:T(4,128)S(1)}, u32[]{:S(2)}, u32[]{:S(2)}) %all-to-all-start.7) | async-done | bytes 524320 | tf_op jit(solution)/shard_map/all_to_all | solution.py:1161
  283.7 10.0 %back_expand_two.1 = (bf16[544,512]{1,0:T(8,128)(2,1)S(1)}, f32[544,512]{1,0:T(8,128)}, f32[32,4,512]{2,1,0:T(4,128)}, f32[2,2048]{1,0:T(2,128)S(1)}) custom-call(s32[5]{0:T(128)S(1)} %stack.50.zi, f32[16,4,2048]{2,1,0:T(4,128)S(1)} %all-to-all-done.7.stb, f32[4,32,128]{2,1,0:T(8,128)S(1)} %convert_add_fusion.norms, f32[4,2048]{1,0:T(4,128)S(1)} %get-tuple-element.230.sum6, ...), custom_call_target="tpu_custom_call" | custom-call | flops 1140850688 | bytes 14000000 | tf_op jit(solution)/shard_map/back_expand_two/pallas_call | solution.py:43
  300.3 7.7 %all-to-all-done.8.stb = f32[32,4,512]{2,1,0:T(4,128)S(1)} async-done(((f32[32,4,512]{2,1,0:T(4,128)}), f32[32,4,512]{2,1,0:T(4,128)S(1)}, u32[]{:S(2)}, u32[]{:S(2)}) %all-to-all-start.8) | async-done | bytes 262176 | tf_op jit(solution)/shard_map/all_to_all | solution.py:1170
  308.0 9.0 %back_spatial_two.1 = (bf16[544,128]{1,0:T(8,128)(2,1)S(1)}, f32[544,512]{1,0:T(8,128)}, f32[32,4,512]{2,1,0:T(4,128)}, f32[2,512]{1,0:T(2,128)S(1)}) custom-call(s32[5]{0:T(128)S(1)} %stack.50.zi, f32[32,4,512]{2,1,0:T(4,128)S(1)} %all-to-all-done.8.stb, f32[4,32,128]{2,1,0:T(8,128)S(1)} %convert_add_fusion.norms, f32[4,512]{1,0:T(4,128)S(1)} %get-tuple-element.231.sum5, ...), custom_call_target="tpu_custom_call" | custom-call | flops 2566914048 | bytes 10000000 | tf_op jit(solution)/shard_map/back_spatial_two/pallas_call | solution.py:43
  329.9 11.2 %back_reduce_two.1 = (bf16[544,128]{1,0:T(8,128)(2,1)S(1)}, f32[544,2048]{1,0:T(8,128)}, f32[6,2048]{1,0:T(8,128)S(1)}, f32[2,512]{1,0:T(2,128)S(1)}) custom-call(s32[5]{0:T(128)S(1)} %stack.50.zi, f32[32,4,512]{2,1,0:T(4,128)S(1)} %all-to-all-done.9.stb, f32[4,32,128]{2,1,0:T(8,128)S(1)} %convert_add_fusion.norms, f32[4,512]{1,0:T(4,128)S(1)} %get-tuple-element.239.sum4, ...), custom_call_target="tpu_custom_call" | custom-call | flops 1140850688 | bytes 22000000 | tf_op jit(solution)/shard_map/back_reduce_two/pallas_call | solution.py:43
  350.6 14.6 %all-to-all-done.10.stb = f32[16,6,2048]{2,1,0:T(8,128)S(1)} async-done(((f32[16,6,2048]{2,1,0:T(8,128)}), f32[16,6,2048]{2,1,0:T(8,128)S(1)}, u32[]{:S(2)}, u32[]{:S(2)}) %all-to-all-start.10) | async-done | bytes 786464 | tf_op jit(solution)/shard_map/all_to_all | solution.py:1161
  365.9 10.1 %back_expand_one.1 = (bf16[544,512]{1,0:T(8,128)(2,1)S(1)}, f32[544,512]{1,0:T(8,128)}, f32[32,4,512]{2,1,0:T(4,128)}, f32[2,2048]{1,0:T(2,128)S(1)}, f32[4,2048]{1,0:T(4,128)S(1)}) custom-call(s32[5]{0:T(128)S(1)} %stack.50.zi, f32[16,6,2048]{2,1,0:T(8,128)S(1)} %all-to-all-done.10.stb, f32[4,32,128]{2,1,0:T(8,128)S(1)} %convert_add_fusion.norms, ...), custom_call_target="tpu_custom_call" | custom-call | flops 1140850688 | bytes 16000000 | tf_op jit(solution)/shard_map/back_expand_one/pallas_call | solution.py:43
  382.3 5.7 %back_shortcut.1 = (bf16[544,512]{1,0:T(8,128)(2,1)S(1)}, f32[544,256]{1,0:T(8,128)S(1)}, f32[2,2048]{1,0:T(2,128)S(1)}) custom-call(s32[5]{0:T(128)S(1)} %stack.50.zi, f32[4,32,128]{2,1,0:T(8,128)S(1)} %convert_add_fusion.norms, f32[4,2048]{1,0:T(4,128)S(1)} %get-tuple-element.259.gsum, f32[4,2048]{1,0:T(4,128)S(1)} %get-tuple-element.248.sums, ...), custom_call_target="tpu_custom_call" | custom-call | flops 570425344 | bytes 10000000 | tf_op jit(solution)/shard_map/back_shortcut/pallas_call | solution.py:43
  394.9 13.8 %back_spatial_one.1 = (bf16[544,128]{1,0:T(8,128)(2,1)S(1)}, f32[2144,512]{1,0:T(8,128)}, f32[32,4,512]{2,1,0:T(4,128)}, f32[2,512]{1,0:T(2,128)S(1)}) custom-call(s32[5]{0:T(128)S(1)} %stack.50.zi, f32[32,4,512]{2,1,0:T(4,128)S(1)} %all-to-all-done.11.stb, f32[4,32,128]{2,1,0:T(8,128)S(1)} %convert_add_fusion.norms, f32[4,512]{1,0:T(4,128)S(1)} %copy-done.38, ...), custom_call_target="tpu_custom_call" | custom-call | flops 2566914048 | bytes 20000000 | tf_op jit(solution)/shard_map/back_spatial_one/pallas_call | solution.py:43
  408.7 7.9 %all-to-all-start.12 = ((f32[32,4,512]{2,1,0:T(4,128)}), f32[32,4,512]{2,1,0:T(4,128)S(1)}, u32[]{:S(2)}, u32[]{:S(2)}) async-start(f32[32,4,512]{2,1,0:T(4,128)} %get-tuple-element.270), calls=%async_computation.12 | async-start | bytes 524288 | tf_op jit(solution)/shard_map/all_to_all | solution.py:1170
  425.4 5.5 %all-to-all-start.13 = ((bf16[16,464,128]{2,1,0:T(8,128)(2,1)}), bf16[16,464,128]{2,1,0:T(8,128)(2,1)S(1)}, u32[]{:S(2)}, u32[]{:S(2)}) async-start(bf16[16,464,128]{2,1,0:T(8,128)(2,1)} %bitcast.62), calls=%async_computation.13 | async-start | bytes 3801088 | tf_op jit(solution)/shard_map/all_to_all | solution.py:1496
  431.6 5.9 %back_reduce_one.1 = (bf16[2144,128]{1,0:T(8,128)(2,1)S(1)}, bf16[2144,512]{1,0:T(8,128)(2,1)}, f32[2,512]{1,0:T(2,128)S(1)}) custom-call(s32[5]{0:T(128)S(1)} %stack.50.zi, f32[32,4,512]{2,1,0:T(4,128)S(1)} %all-to-all-done.12.stb, f32[4,32,128]{2,1,0:T(8,128)S(1)} %convert_add_fusion.norms, f32[4,512]{1,0:T(4,128)S(1)} %copy-done.40, ...), custom_call_target="tpu_custom_call" | custom-call | bytes 12000000 | tf_op jit(solution)/shard_map/back_reduce_one/pallas_call | solution.py:43
  444.3 15.6 %all-to-all-done.13.some = bf16[16,464,128]{2,1,0:T(8,128)(2,1)S(1)} async-done(((bf16[16,464,128]{2,1,0:T(8,128)(2,1)}), bf16[16,464,128]{2,1,0:T(8,128)(2,1)S(1)}, u32[]{:S(2)}, u32[]{:S(2)}) %all-to-all-start.13) | async-done | bytes 1900576 | tf_op jit(solution)/shard_map/all_to_all | solution.py:1496
  476.5 38.2 %all_to_all.81.src = bf16[16,688,128]{2,1,0:T(8,128)(2,1)S(1)} all-to-all(bf16[16,688,128]{2,1,0:T(8,128)(2,1)S(1)} %broadcast_in_dim.19), channel_id=1, replica_groups=mesh['y'=4,'x'=4,'c'=2,'z'=4] {'y','x'}, dimensions={0} | all-to-all | bytes 5636096 | tf_op jit(solution)/shard_map/all_to_all | solution.py:1161
  (292 shorter events, 180.6 us)
Async XLA Ops:
  7.2 125.1 %all-gather.5.cloned.1.call-start = ((), (), s32[]{:S(2)}) async-start(), calls=%async_computation.16 | async-start | bytes 8982528 | tf_op jit(solution)/shard_map/all_gather | solution.py:1255
  13.3 196.8 %all-gather.7.cloned.1.call-start = ((), (), s32[]{:S(2)}) async-start(), calls=%async_computation.17 | async-start | bytes 6868992 | tf_op jit(solution)/shard_map/all_gather | solution.py:1256
  14.0 37.0 %collective-permute-start.3 = (bf16[1344,256]{1,0:T(8,128)(2,1)S(1)}, bf16[1344,256]{1,0:T(8,128)(2,1)}, u32[]{:S(2)}, u32[]{:S(2)}) collective-permute-start(bf16[1344,256]{1,0:T(8,128)(2,1)S(1)} %get-tuple-element.177.refs_1_), channel_id=1, source_target_pairs={{0,3},{1,0},{2,1},{3,2},{4,7},{5,4},{6,5},{7,6},{8,11},{9,8},{10,9... | collective-permute-start | bytes 2064392 | tf_op jit(solution)/shard_map/ppermute | solution.py:1192
  18.7 32.3 %collective-permute-start.1 = (bf16[1344,256]{1,0:T(8,128)(2,1)S(1)}, bf16[1344,256]{1,0:T(8,128)(2,1)}, u32[]{:S(2)}, u32[]{:S(2)}) collective-permute-start(bf16[1344,256]{1,0:T(8,128)(2,1)S(1)} %get-tuple-element.177.refs_1_), channel_id=1, source_target_pairs={{0,1},{1,2},{2,3},{3,0},{4,5},{5,6},{6,7},{7,4},{8,9},{9,10},{10,1... | collective-permute-start | bytes 2064392 | tf_op jit(solution)/shard_map/ppermute | solution.py:1191
  18.7 29.2 %collective-permute-start.2 = (bf16[1312,256]{1,0:T(8,128)(2,1)S(1)}, bf16[1312,256]{1,0:T(8,128)(2,1)S(1)}, u32[]{:S(2)}, u32[]{:S(2)}) collective-permute-start(bf16[1312,256]{1,0:T(8,128)(2,1)S(1)} %get-tuple-element.175.refs_0_.t0), channel_id=1, source_target_pairs={{0,3},{1,0},{2,1},{3,2},{4,7},{5,4},{6,5},{7,6},{8,11},{9,8},{10,9... | collective-permute-start | bytes 2015240 | tf_op jit(solution)/shard_map/ppermute | solution.py:1192
  21.4 29.6 %collective-permute-start = (bf16[1312,256]{1,0:T(8,128)(2,1)S(1)}, bf16[1312,256]{1,0:T(8,128)(2,1)S(1)}, u32[]{:S(2)}, u32[]{:S(2)}) collective-permute-start(bf16[1312,256]{1,0:T(8,128)(2,1)S(1)} %get-tuple-element.175.refs_0_.t0), channel_id=1, source_target_pairs={{0,1},{1,2},{2,3},{3,0},{4,5},{5,6},{6,7},{7,4},{8,9},{9,10},{10,1... | collective-permute-start | bytes 2015240 | tf_op jit(solution)/shard_map/ppermute | solution.py:1191
  51.0 19.1 %collective-permute-start.4 = (bf16[1312,256]{1,0:T(8,128)(2,1)S(1)}, bf16[1312,256]{1,0:T(8,128)(2,1)}, u32[]{:S(2)}, u32[]{:S(2)}) collective-permute-start(bf16[1312,256]{1,0:T(8,128)(2,1)S(1)} %collective-permute-done.refs_6_.t3), channel_id=1, source_target_pairs={{0,1},{1,2},{2,3},{3,0},{4,5},{5,6},{6,7},{7,4},{8,9},{9,10},{10,1... | collective-permute-start | bytes 2015240 | tf_op jit(solution)/shard_map/ppermute | solution.py:1194
  51.1 19.0 %collective-permute-start.5 = (bf16[1344,256]{1,0:T(8,128)(2,1)}, bf16[1344,256]{1,0:T(8,128)(2,1)}, u32[]{:S(2)}, u32[]{:S(2)}) collective-permute-start(bf16[1344,256]{1,0:T(8,128)(2,1)} %collective-permute-done.3.refs_3_), channel_id=1, source_target_pairs={{0,3},{1,0},{2,1},{3,2},{4,7},{5,4},{6,5},{7,6},{8,11},{9,8},{10,9... | collective-permute-start | bytes 2064392 | tf_op jit(solution)/shard_map/ppermute | solution.py:1194
  54.5 15.6 %all-to-all-start = ((bf16[4,96,128]{2,1,0:T(8,128)(2,1)}), bf16[4,96,128]{2,1,0:T(8,128)(2,1)S(1)}, u32[]{:S(2)}, u32[]{:S(2)}) async-start(bf16[4,96,128]{2,1,0:T(8,128)(2,1)} %broadcast_in_dim.14), calls=%async_computation | async-start | bytes 196608 | tf_op jit(solution)/shard_map/all_to_all | solution.py:1161
  78.1 23.1 %all-to-all-start.1 = ((f32[32,4,512]{2,1,0:T(4,128)}), f32[32,4,512]{2,1,0:T(4,128)S(1)}, u32[]{:S(2)}, u32[]{:S(2)}) async-start(f32[32,4,512]{2,1,0:T(4,128)} %get-tuple-element.188), calls=%async_computation.1 | async-start | bytes 524288 | tf_op jit(solution)/shard_map/all_to_all | solution.py:1170
  122.0 22.7 %collective-permute-start.13 = (bf16[256,512]{1,0:T(8,128)(2,1)S(1)}, bf16[256,512]{1,0:T(8,128)(2,1)S(1)}, u32[]{:S(2)}, u32[]{:S(2)}) collective-permute-start(bf16[256,512]{1,0:T(8,128)(2,1)S(1)} %collective-permute-done.9.refs_10_.refs_2_), channel_id=1, source_target_pairs={{0,4},{4,0},{1,5},{5,1},{2,6},{6,2},{3,7},{7,3},{8,12},{12,8},{9,1... | collective-permute-start | bytes 786440 | tf_op jit(solution)/shard_map/ppermute | solution.py:1187
  122.5 22.2 %collective-permute-start.16 = (bf16[256,512]{1,0:T(8,128)(2,1)S(1)}, bf16[256,512]{1,0:T(8,128)(2,1)S(1)}, u32[]{:S(2)}, u32[]{:S(2)}) collective-permute-start(bf16[256,512]{1,0:T(8,128)(2,1)S(1)} %collective-permute-done.6.refs_13_.refs_5_), channel_id=1, source_target_pairs={{0,4},{4,0},{1,5},{5,1},{2,6},{6,2},{3,7},{7,3},{8,12},{12,8},{9,1... | collective-permute-start | bytes 786440 | tf_op jit(solution)/shard_map/ppermute | solution.py:1187
  122.5 22.1 %collective-permute-start.17 = (bf16[256,512]{1,0:T(8,128)(2,1)S(1)}, bf16[256,512]{1,0:T(8,128)(2,1)}, u32[]{:S(2)}, u32[]{:S(2)}) collective-permute-start(bf16[256,512]{1,0:T(8,128)(2,1)S(1)} %collective-permute-done.7.refs_14_.refs_6_), channel_id=1, source_target_pairs={{0,4},{4,0},{1,5},{5,1},{2,6},{6,2},{3,7},{7,3},{8,12},{12,8},{9,1... | collective-permute-start | bytes 786440 | tf_op jit(solution)/shard_map/ppermute | solution.py:1187
  130.0 14.7 %collective-permute-start.15 = (bf16[256,512]{1,0:T(8,128)(2,1)S(1)}, bf16[256,512]{1,0:T(8,128)(2,1)}, u32[]{:S(2)}, u32[]{:S(2)}) collective-permute-start(bf16[256,512]{1,0:T(8,128)(2,1)S(1)} %collective-permute-done.11.refs_12_.refs_4_), channel_id=1, source_target_pairs={{0,4},{4,0},{1,5},{5,1},{2,6},{6,2},{3,7},{7,3},{8,12},{12,8},{9,1... | collective-permute-start | bytes 786440 | tf_op jit(solution)/shard_map/ppermute | solution.py:1187
  194.7 15.3 %all-to-all-start.4 = ((f32[32,4,512]{2,1,0:T(4,128)}), f32[32,4,512]{2,1,0:T(4,128)}, u32[]{:S(2)}, u32[]{:S(2)}) async-start(f32[32,4,512]{2,1,0:T(4,128)} %get-tuple-element.208), calls=%async_computation.4 | async-start | bytes 524288 | tf_op jit(solution)/shard_map/all_to_all | solution.py:1170
  218.4 14.0 %all-to-all-start.5 = ((f32[32,4,512]{2,1,0:T(4,128)}), f32[32,4,512]{2,1,0:T(4,128)S(1)}, u32[]{:S(2)}, u32[]{:S(2)}) async-start(f32[32,4,512]{2,1,0:T(4,128)} %get-tuple-element.212), calls=%async_computation.5 | async-start | bytes 524288 | tf_op jit(solution)/shard_map/all_to_all | solution.py:1170
  224.0 19.6 %collective-permute-start.22 = (bf16[272,512]{1,0:T(8,128)(2,1)S(1)}, bf16[272,512]{1,0:T(8,128)(2,1)S(1)}, u32[]{:S(2)}, u32[]{:S(2)}) collective-permute-start(bf16[272,512]{1,0:T(8,128)(2,1)S(1)} %get-tuple-element.217.refs_0_), channel_id=1, source_target_pairs={{0,3},{1,0},{2,1},{3,2},{4,7},{5,4},{6,5},{7,6},{8,11},{9,8},{10,9... | collective-permute-start | bytes 835592 | tf_op jit(solution)/shard_map/ppermute | solution.py:1192
  224.4 19.3 %collective-permute-start.20 = (bf16[272,512]{1,0:T(8,128)(2,1)S(1)}, bf16[272,512]{1,0:T(8,128)(2,1)S(1)}, u32[]{:S(2)}, u32[]{:S(2)}) collective-permute-start(bf16[272,512]{1,0:T(8,128)(2,1)S(1)} %get-tuple-element.217.refs_0_), channel_id=1, source_target_pairs={{0,1},{1,2},{2,3},{3,0},{4,5},{5,6},{6,7},{7,4},{8,9},{9,10},{10,1... | collective-permute-start | bytes 835592 | tf_op jit(solution)/shard_map/ppermute | solution.py:1191
  225.5 18.1 %collective-permute-start.23 = (bf16[272,512]{1,0:T(8,128)(2,1)S(1)}, bf16[272,512]{1,0:T(8,128)(2,1)S(1)}, u32[]{:S(2)}, u32[]{:S(2)}) collective-permute-start(bf16[272,512]{1,0:T(8,128)(2,1)S(1)} %get-tuple-element.218.refs_1_), channel_id=1, source_target_pairs={{0,3},{1,0},{2,1},{3,2},{4,7},{5,4},{6,5},{7,6},{8,11},{9,8},{10,9... | collective-permute-start | bytes 835592 | tf_op jit(solution)/shard_map/ppermute | solution.py:1192
  227.1 16.6 %collective-permute-start.21 = (bf16[272,512]{1,0:T(8,128)(2,1)S(1)}, bf16[272,512]{1,0:T(8,128)(2,1)S(1)}, u32[]{:S(2)}, u32[]{:S(2)}) collective-permute-start(bf16[272,512]{1,0:T(8,128)(2,1)S(1)} %get-tuple-element.218.refs_1_), channel_id=1, source_target_pairs={{0,1},{1,2},{2,3},{3,0},{4,5},{5,6},{6,7},{7,4},{8,9},{9,10},{10,1... | collective-permute-start | bytes 835592 | tf_op jit(solution)/shard_map/ppermute | solution.py:1191
  240.0 14.7 %all-to-all-start.6 = ((f32[16,4,2048]{2,1,0:T(4,128)}), f32[16,4,2048]{2,1,0:T(4,128)S(1)}, u32[]{:S(2)}, u32[]{:S(2)}) async-start(f32[16,4,2048]{2,1,0:T(4,128)} %broadcast_in_dim.16), calls=%async_computation.6 | async-start | bytes 1048576 | tf_op jit(solution)/shard_map/all_to_all | solution.py:1161
  266.2 17.6 %all-to-all-start.7 = ((f32[16,4,2048]{2,1,0:T(4,128)}), f32[16,4,2048]{2,1,0:T(4,128)S(1)}, u32[]{:S(2)}, u32[]{:S(2)}) async-start(f32[16,4,2048]{2,1,0:T(4,128)} %broadcast_in_dim.17), calls=%async_computation.7 | async-start | bytes 1048576 | tf_op jit(solution)/shard_map/all_to_all | solution.py:1161
  293.7 14.3 %all-to-all-start.8 = ((f32[32,4,512]{2,1,0:T(4,128)}), f32[32,4,512]{2,1,0:T(4,128)S(1)}, u32[]{:S(2)}, u32[]{:S(2)}) async-start(f32[32,4,512]{2,1,0:T(4,128)} %get-tuple-element.233), calls=%async_computation.8 | async-start | bytes 524288 | tf_op jit(solution)/shard_map/all_to_all | solution.py:1170
  343.5 21.7 %all-to-all-start.10 = ((f32[16,6,2048]{2,1,0:T(8,128)}), f32[16,6,2048]{2,1,0:T(8,128)S(1)}, u32[]{:S(2)}, u32[]{:S(2)}) async-start(f32[16,6,2048]{2,1,0:T(8,128)} %broadcast_in_dim.18), calls=%async_computation.10 | async-start | bytes 2097152 | tf_op jit(solution)/shard_map/all_to_all | solution.py:1161
  347.1 33.4 %collective-permute-start.28 = (bf16[1024,128]{1,0:T(8,128)(2,1)}, bf16[1024,128]{1,0:T(8,128)(2,1)}, u32[]{:S(2)}, u32[]{:S(2)}) collective-permute-start(bf16[1024,128]{1,0:T(8,128)(2,1)} %copy-done.50), channel_id=1, source_target_pairs={{0,4},{4,0},{1,5},{5,1},{2,6},{6,2},{3,7},{7,3},{8,12},{12,8},{9,1... | collective-permute-start | bytes 786440 | tf_op jit(solution)/shard_map/ppermute | solution.py:1187
  347.5 46.0 %collective-permute-start.29 = (bf16[2304,128]{1,0:T(8,128)(2,1)}, bf16[2304,128]{1,0:T(8,128)(2,1)}, u32[]{:S(2)}, u32[]{:S(2)}) collective-permute-start(bf16[2304,128]{1,0:T(8,128)(2,1)} %copy-done.45), channel_id=1, source_target_pairs={{0,4},{4,0},{1,5},{5,1},{2,6},{6,2},{3,7},{7,3},{8,12},{12,8},{9,1... | collective-permute-start | bytes 1769480 | tf_op jit(solution)/shard_map/ppermute | solution.py:1187
  376.0 17.0 %all-to-all-start.11 = ((f32[32,4,512]{2,1,0:T(4,128)}), f32[32,4,512]{2,1,0:T(4,128)S(1)}, u32[]{:S(2)}, u32[]{:S(2)}) async-start(f32[32,4,512]{2,1,0:T(4,128)} %get-tuple-element.258), calls=%async_computation.11 | async-start | bytes 524288 | tf_op jit(solution)/shard_map/all_to_all | solution.py:1170
  393.0 28.2 %collective-permute-start.31 = (bf16[3072,128]{1,0:T(8,128)(2,1)S(1)}, bf16[3072,128]{1,0:T(8,128)(2,1)}, u32[]{:S(2)}, u32[]{:S(2)}) collective-permute-start(bf16[3072,128]{1,0:T(8,128)(2,1)S(1)} %get-tuple-element.278), channel_id=1, source_target_pairs={{0,4},{4,0},{1,5},{5,1},{2,6},{6,2},{3,7},{7,3},{8,12},{12,8},{9,1... | collective-permute-start | bytes 2359304 | tf_op jit(solution)/shard_map/ppermute | solution.py:1187
  394.7 26.5 %collective-permute-start.30 = (bf16[1024,128]{1,0:T(8,128)(2,1)}, bf16[1024,128]{1,0:T(8,128)(2,1)S(1)}, u32[]{:S(2)}, u32[]{:S(2)}) collective-permute-start(bf16[1024,128]{1,0:T(8,128)(2,1)} %copy-done.49), channel_id=1, source_target_pairs={{0,4},{4,0},{1,5},{5,1},{2,6},{6,2},{3,7},{7,3},{8,12},{12,8},{9,1... | collective-permute-start | bytes 786440 | tf_op jit(solution)/shard_map/ppermute | solution.py:1187
  408.7 16.6 %all-to-all-start.12 = ((f32[32,4,512]{2,1,0:T(4,128)}), f32[32,4,512]{2,1,0:T(4,128)S(1)}, u32[]{:S(2)}, u32[]{:S(2)}) async-start(f32[32,4,512]{2,1,0:T(4,128)} %get-tuple-element.270), calls=%async_computation.12 | async-start | bytes 524288 | tf_op jit(solution)/shard_map/all_to_all | solution.py:1170
  425.4 34.5 %all-to-all-start.13 = ((bf16[16,464,128]{2,1,0:T(8,128)(2,1)}), bf16[16,464,128]{2,1,0:T(8,128)(2,1)S(1)}, u32[]{:S(2)}, u32[]{:S(2)}) async-start(bf16[16,464,128]{2,1,0:T(8,128)(2,1)} %bitcast.62), calls=%async_computation.13 | async-start | bytes 3801088 | tf_op jit(solution)/shard_map/all_to_all | solution.py:1496
  459.9 15.7 %all-to-all-start.14 = ((bf16[16,176,128]{2,1,0:T(8,128)(2,1)}), bf16[16,176,128]{2,1,0:T(8,128)(2,1)S(1)}, u32[]{:S(2)}, u32[]{:S(2)}) async-start(bf16[16,176,128]{2,1,0:T(8,128)(2,1)} %bitcast.65), calls=%async_computation.14 | async-start | bytes 1441792 | tf_op jit(solution)/shard_map/all_to_all | solution.py:1522
  (92 other events, 1076.3 us)
Sparse Core Ops, SparseCore 0:
  13.4 75.3 all-gather.4
  92.3 69.7 all-gather.6

commit v2 on v1

--- a/solution.py
+++ b/solution.py
@@ -228,17 +228,6 @@
         for z in range(4)
         for j in range(4)
     ]
-
-
-def halves_in(zi, srcs, w, sem):
-    copies = [go(srcs[0], w.at[:, pl.ds(pl.multiple_of(zi[0] * 512, 512), 512)], sem.at[0])]
-    for c in (0, 1):
-        r = zi[4] * 512 if c == 0 else 512 - zi[4] * 512
-        for i in range(6):
-            cols = pl.ds(pl.multiple_of(zi[1 + i // 2] * 512, 512), 512)
-            dst = w.at[pl.ds(pl.multiple_of(r + 256 * (i % 2), 256), 256), cols]
-            copies.append(go(srcs[1 + 6 * c + i], dst, sem.at[1 + 6 * c + i]))
-    return copies
 
 
 def pack_kernel(side, cuts, local, glob, *refs):
@@ -313,7 +302,7 @@
     )
 
 
-def pieces_kernel(at, spatial_one, expand_one, reduce_two, spatial_two, expand_two, near, late, sem):
+def pieces_kernel(at, spatial_one, expand_one, shortcut, reduce_two, spatial_two, expand_two, near, late, sem):
     copies = []
 
     def take(src, dst, first):
@@ -326,7 +315,8 @@
 
     take(spatial_one, near, 0)
     take(expand_one, near, 144)
-    take(reduce_two, near, 208)
+    take(shortcut, near, 208)
+    take(reduce_two, near, 336)
     take(spatial_two, late, 0)
     take(expand_two, late, 144)
     wait(copies)
@@ -570,7 +560,7 @@
 
 
 def skip_kernel(zi, *refs):
-    x, srcs, rest = refs[:8], refs[8:21], refs[21:]
+    x, bundle, rest = refs[:8], refs[8], refs[9:]
     xe, zs, stats, xv, ev, tmp, zv, w, xs, ws, es, os = rest
     xin = [
         [
@@ -579,7 +569,7 @@
         ]
         for k in range(4)
     ]
-    weight = halves_in(zi, srcs, w, ws)
+    weight = bundle_out_in(bundle, 208, w.reshape(32, 32, 2048), ws)
     tmp[pl.ds(536, 8), :] = jnp.zeros((8, 256), F32)
     for k in range(4):
         wait(xin[k])
@@ -608,7 +598,7 @@
         cin.append(
             [go(z3.at[:, cols], z3v.at[:, cols], ins.at[0, n]), go(zs.at[:, cols], zsv.at[:, cols], ins.at[1, n])]
         )
-    weight = bundle_in(late, 208, w, ws)
+    weight = bundle_in(late, 336, w, ws)
     wf = w.reshape(2048, 512)
     out = []
     for n in range(4):
@@ -797,7 +787,7 @@
 
 def back_four_kernel(zi, stb, norms, sum4, sum3, sums, z4, dv4, dv6, z3, zs, late, own, dpre, stats, grad, zv, dv, d6, z3v, zsv, dz, w, in4, ins, ws, os):
     cin = [go(z4, zv, in4.at[0]), go(dv4, dv, in4.at[1])]
-    weight = bundle_in(late, 208, w, ws)
+    weight = bundle_in(late, 336, w, ws)
     wide = []
     for n in range(4):
         cols = quarter(n)
@@ -883,26 +873,23 @@
     out.wait()
 
 
-def back_skip_kernel(zi, norms, gsum, sums, zs, dpre, *refs):
-    srcs, rest = refs[:13], refs[13:]
-    own, skip, grad, zv, dv, dz, w, ins, ws = rest
+def back_skip_kernel(zi, norms, gsum, sums, zs, dpre, bundle, own, skip, grad, zv, dv, dz, w, ins, ws):
     cin = []
     for n in range(4):
         cols = quarter(n)
         cin.append(
             [go(zs.at[:, cols], zv.at[:, cols], ins.at[0, n]), go(dpre.at[:, cols], dv.at[:, cols], ins.at[1, n])]
         )
-    mine = pl.ds(pl.multiple_of(zi[0] * 256, 256), 256)
-    cols = [pl.ds(pl.multiple_of(zi[k] * 512, 512), 512) for k in range(4)]
-    weight = [go(srcs[0].at[mine, :], w.at[:, cols[0]], ws.at[0])]
-    which = jnp.where(zi[0] // 2 == zi[4], 0, 2) + zi[0] % 2
-    for v in range(4):
-
-        @pl.when(which == v)
-        def _(v=v):
-            for k in (1, 2, 3):
-                go(srcs[1 + 6 * (v // 2) + 2 * (k - 1) + v % 2], w.at[:, cols[k]], ws.at[k])
-
+    wv = w.reshape(8, 32, 2048)
+    weight = [
+        go(
+            bundle.at[pl.ds(zi[0] * 8, 8), z, pl.ds(208 + 32 * j, 32), :],
+            wv.at[:, :, pl.ds(z * 512 + j * 128, 128)],
+            ws.at[4 * z + j],
+        )
+        for z in range(4)
+        for j in range(4)
+    ]
     for n in range(4):
         here = quarter(n)
         grads = gsum[:, here]
@@ -912,8 +899,6 @@
         norm_rows(dv, zv, cs, here, dz)
     own_cols(own, dz, zi, 512)
     wait(weight)
-    for k in (1, 2, 3):
-        pltpu.make_async_copy(srcs[1], w.at[:, cols[k]], ws.at[k]).wait()
     skip[...] = dot_t(dz[...], w[...])
 
 
@@ -929,6 +914,8 @@
     norm_rows(dv, zv, cs, slice(None), dv)
     own_cols(own, dv, zi, 128)
     pad_back(dzl, dzg, dv, 0)
+    for i in range(4):
+        dz[i] = load_taps(dzl, dzg, i // 2, i % 2, 1).astype(BF)
     wait(weight)
     wf = w.reshape(4608, 512)
     gb1 = mid_gb(norms, 0)
@@ -943,8 +930,7 @@
             for i, di in reach[p]:
                 for j, dj in reach[q]:
                     k = 3 * i + j
-                    dz[...] = load_taps(dzl, dzg, di, dj, 1).astype(BF)
-                    part = dot_t(dz[...], wf[k * 512 : (k + 1) * 512, :])
+                    part = dot_t(dz[2 * di + dj], wf[k * 512 : (k + 1) * 512, :])
                     if first:
                         acc[...] = part
                     else:
@@ -1081,34 +1067,39 @@
 ), ((1, 0, 2304), (0, 2304, 2816))
 
 
-def slice_kernel(at, some, rest, out):
+def slice_kernel(spans, at, src, *refs):
+    out = refs[0] if spans is SPANS[0] else refs[1]
     squares = [jnp.zeros((1, 128), F32)] * 8
-    first = 0
-    for src, spans in zip((some, rest), SPANS):
-        n = src.shape[1]
-        v = src[0].astype(F32)
-        for p in range(1, 16):
-            v = v + src[p].astype(F32)
-        out[first : first + n, :] = v.astype(BF)
-        first += n
-        v = v * v
-        row = lax.broadcasted_iota(jnp.int32, (n, 128), 0) + at[0] * n
-        for i, lo, hi in spans:
-            squares[i] = row1(jnp.where((row >= lo) & (row < hi), v, 0.0))
-    left = jnp.concatenate(squares + squares, axis=0)
+    n = src.shape[1]
+    v = src[0].astype(F32)
+    for p in range(1, 16):
+        v = v + src[p].astype(F32)
+    out[0:n, :] = v.astype(BF)
+    v = v * v
+    row = lax.broadcasted_iota(jnp.int32, (n, 128), 0) + at[0] * n
+    for i, lo, hi in spans:
+        squares[i] = row1(jnp.where((row >= lo) & (row < hi), v, 0.0))
+    left = jnp.concatenate(squares, axis=0)
+    if spans is SPANS[0]:
+        refs[1][...] = left
+        return
+    left = left + refs[0][...]
+    left = jnp.concatenate([left, left], axis=0)
     for k in range(3):
         part = left.astype(BF)
-        out[first + 16 * k : first + 16 * k + 16, :] = part
+        out[n + 16 * k : n + 16 * k + 16, :] = part
         left = left - part.astype(F32)
 
 
-def spill_kernel(other, zi, src, *refs):
+def spill_kernel(other, zi, places, a0, a1, a2, a3, b, *refs):
     refs = refs[7:] if other else refs
     outs, (v6, v5, v4, v3, vs, v2, v1, fa, fb, ins, sem) = refs[:7], refs[7:]
-    cin = [
-        go(src.at[:, pl.ds(0, 464), :], fa.reshape(16, 464, 128), ins.at[0]),
-        go(src.at[:, pl.ds(464, 176), :], fb.reshape(16, 176, 128), ins.at[1]),
-    ]
+    cin = []
+    for j, a in enumerate((a0, a1, a2, a3)):
+        for k in range(4):
+            dst = fa.at[pl.ds(pl.multiple_of(places[4 * j + k] * 464, 16), 464), :]
+            cin.append(go(a.at[pl.ds(464 * k, 464), :], dst, ins.at[4 * j + k]))
+    last = go(b.at[:, pl.ds(0, 176), :], fb.reshape(16, 176, 128), ins.at[16])
     c = 1 - zi[4] if other else zi[4]
     copies = []
     plan = (
@@ -1119,10 +1110,10 @@
         (v3, 3, fa, 4352, 256, 4),
         (v2, 5, fb, 0, 2304, 1),
     )
-    cin[0].wait()
+    wait(cin)
     for dst, i, flat, at, n, blocks in plan:
         if i == 5:
-            cin[1].wait()
+            last.wait()
         for j in range(blocks):
             dst[:, 128 * j : 128 * (j + 1)] = flat[at + j * n : at + (j + 1) * n, :].astype(F32)
         rows = pl.ds(pl.multiple_of(c * n, n), n)
@@ -1137,20 +1128,20 @@
 GRADS = ((512, 512), (4608, 128), (2048, 128), (512, 512), (1024, 512), (4608, 128), (1024, 128))
 
 
-def spill(name, zi, src, before):
+def spill(name, zi, places, srcs, before):
     other = bool(before)
     return pl.pallas_call(
         functools.partial(spill_kernel, other),
         name=name,
         out_shape=tuple(pltpu.HBM(d, F32) for d in GRADS),
-        in_specs=[SM, ANY] + [ANY] * len(before),
+        in_specs=[SM, SM] + [ANY] * (5 + len(before)),
         out_specs=tuple(ANY for _ in GRADS),
         scratch_shapes=[pltpu.VMEM((r // 2, c), F32) for r, c in GRADS]
-        + [pltpu.VMEM((7424, 128), BF), pltpu.VMEM((2816, 128), BF), sems(2), sems(8)],
-        input_output_aliases={2 + i: i for i in range(len(before))},
+        + [pltpu.VMEM((7424, 128), BF), pltpu.VMEM((2816, 128), BF), sems(17), sems(8)],
+        input_output_aliases={7 + i: i for i in range(len(before))},
         compiler_params=pltpu.CompilerParams(vmem_limit_bytes=50 * 1024 * 1024),
         cost_estimate=pl.CostEstimate(flops=0, bytes_accessed=8_000_000, transcendentals=0),
-    )(zi, src, *before)
+    )(zi, places, *srcs, *before)
 
 
 def ring(n, k):
@@ -1248,11 +1239,11 @@
         "pieces",
         pieces_kernel,
         [((plane_index() * 2 + ci).reshape(1).astype(jnp.int32), SM)]
-        + [(after(v, x[0]), ANY) for v in (flat2, expand_one, reduce_two, flat5, expand_two)],
-        [(shape((272, 128), BF), VM), (shape((208, 128), BF), VM)],
-        [sems(14)],
-    )
-    near = lax.all_gather(near, EVERY, axis=0).reshape(32, 4, 272, 128)
+        + [(after(v, x[0]), ANY) for v in (flat2, expand_one, shortcut, reduce_two, flat5, expand_two)],
+        [(shape((400, 128), BF), VM), (shape((208, 128), BF), VM)],
+        [sems(15)],
+    )
+    near = lax.all_gather(near, EVERY, axis=0).reshape(32, 4, 400, 128)
     late = lax.all_gather(late, EVERY, axis=0).reshape(32, 4, 208, 128)
 
     cot = pack("pack_cotangent", cotangent_local, cotangent_global, (3, 7), (272, 272))
@@ -1285,11 +1276,7 @@
         ],
         (2 * RIN * 1024 * 512, 10_000_000),
     )
-    parts = [lax.dynamic_slice_in_dim(shortcut, ci * 512 + 256 * i, 256, 0) for i in (0, 1)]
     st1 = tell(s1)
-    p_right, p_far, p_left = around([after(v, st1) for v in parts])
-    skips = tuple(p_right) + tuple(p_far) + tuple(p_left)
-    skips = (shortcut,) + skips + tuple(swap(v) for v in skips)
     t1, z2, s2, sum1 = conv_call(
         "spatial_one",
         second_kernel,
@@ -1303,7 +1290,7 @@
     xe, zs, ss = launch(
         "shortcut",
         skip_kernel,
-        [(where, SM)] + [(v, ANY) for v in xs + skips],
+        [(where, SM)] + [(v, ANY) for v in xs + (near,)],
         [(shape((ROUT, 1024), BF), ANY), wide, out_stats],
         [
             pltpu.VMEM((4, RIN, 256), BF),
@@ -1464,7 +1451,7 @@
         "back_shortcut",
         back_skip_kernel,
         [(where, SM), (norms, VM), (gsum, VM), (sums, VM)]
-        + [(v, ANY) for v in (zs, dpre) + skips],
+        + [(v, ANY) for v in (zs, dpre, near)],
         [own_out, (shape((ROUT, 256)), VM), out_grad],
         wide_in
         + [pltpu.VMEM((ROUT, 2048), BF), pltpu.VMEM((256, 2048), BF), sems(2, 4), sems(16)],
@@ -1480,7 +1467,7 @@
         [own_mid, (shape((RIN, 512)), ANY), mid_stats, mid_grad],
         flat * 2
         + [
-            pltpu.VMEM((ROUT, 512), BF),
+            pltpu.VMEM((4, ROUT, 512), BF),
             pltpu.VMEM((ROUT, 512), F32),
             pltpu.VMEM((4, 4, 16, 512), F32),
             pltpu.VMEM((8, 8, 8, 512), F32),
@@ -1520,13 +1507,24 @@
     rest = jnp.concatenate([add_halves(*conv), add_halves(*first)]).reshape(16, 176, 128)
     some, rest = tie(some, rest)
     rest = lax.all_to_all(rest, PLANE, 0, 0)
-    slice_ = launch(
-        "slice",
-        slice_kernel,
-        [(plane_index().reshape(1).astype(jnp.int32), SM), (some, VM), (rest, VM)],
-        [(shape((688, 128), BF), VM)],
+    here = plane_index().reshape(1).astype(jnp.int32)
+    some, squares_ = launch(
+        "slice_some",
+        functools.partial(slice_kernel, SPANS[0]),
+        [(here, SM), (some, VM)],
+        [(shape((464, 128), BF), VM), (shape((8, 128)), VM)],
         (),
-        (0, 3_000_000),
+        (0, 2_000_000),
+    )
+    some = [some] + [lax.ppermute(some, "x", ring(4, k)) for k in (1, 2, 3)]
+    rest, *some = tie(rest, *some)
+    rest = launch(
+        "slice_rest",
+        functools.partial(slice_kernel, SPANS[1]),
+        [(here, SM), (rest, VM), (squares_, VM)],
+        [(shape((224, 128), BF), VM)],
+        (),
+        (0, 1_000_000),
     )[0]
     dimage_local, dimage_global = launch(
         "image_grad",
@@ -1536,18 +1534,24 @@
         [pltpu.VMEM((2, RIN, 128), F32), pltpu.VMEM((1024, 512), BF), sems(8)],
         (2 * RIN * 512 * 256, 8_000_000),
     )
-    slice_, dimage_local, dimage_global = tie(slice_, dimage_local, dimage_global)
-    held = spread(slice_, PLANE, 16)
-    given = swap(held)
-    grads = spill("grads_kept", where, held, ())
-    given, *grads = tie(given, *grads)
-    t6, t5, t4w, t3, ts, t2, t1w = spill("grads_given", where, given, grads)
+    rest, dimage_local, dimage_global = tie(rest, dimage_local, dimage_global)
+    some = jnp.concatenate(some)
+    some = [some] + [lax.ppermute(some, "y", ring(4, k)) for k in (1, 2, 3)]
+    yi, xi = lax.axis_index("y"), lax.axis_index("x")
+    places = jnp.stack([(yi - j) % 4 * 4 + (xi - k) % 4 for j in range(4) for k in range(4)])
+    places = places.astype(jnp.int32)
+    rest = spread(rest, PLANE, 16)
+    rest, *some = tie(rest, *some)
+    grads = spill("grads_kept", where, places, (*some, rest), ())
+    given = swap(rest)
+    others = [swap(v) for v in some]
+    t6, t5, t4w, t3, ts, t2, t1w = spill("grads_given", where, places, (*others, given), grads)
 
     def squares(v):
-        v = v[:, 640:688].astype(F32).reshape(16, 3, 16, 128)[:, :, :8]
+        v = v[:, 176:224].astype(F32).reshape(16, 3, 16, 128)[:, :, :8]
         return jnp.sum(v, axis=(0, 1, 3))
 
-    grad_sq = squares(held) + squares(given)
+    grad_sq = squares(rest) + squares(given)
     weight_sq = jnp.pad(jnp.sum(square, axis=(1, 2)), (0, 1))
     sq = jnp.concatenate([weight_sq[None], grad_sq[None]])
     sq = sq + lax.ppermute(sq, "z", ring(4, 2))

time: 550 us -> 528 us (0.960)
  blocking collectives: 61.2 us -> 45 us
  starting transfers between devices: 112 us -> 104 us
    all_to_all x2 -> x1, blocking collectives: 61.2 us -> 23 us  [spread(): return lax.all_to_all(jnp.broadcast_to(v[None], (n,) + v.shape), axes, 0, 0)]
    ppermute x0 -> x6, waiting for transfers between devices: none -> 36.4 us  [the longest x3 30.6 us: body(): some = [some] + [lax.ppermute(some, 'y', ring(4, k)) for k in (1, 2, 3)]]
    all_to_all x0 -> x1, blocking collectives: none -> 22.1 us  [tell(): return lax.all_to_all(v, BATCH, 0, 0)]
    all_to_all x8 -> x7, starting transfers between devices: 50.9 us -> 36.6 us  [tell(): return lax.all_to_all(v, BATCH, 0, 0)]
    all_to_all x8 -> x7, waiting for transfers between devices: 30.2 us -> 18 us  [tell(): return lax.all_to_all(v, BATCH, 0, 0)]
    ppermute x3 -> x2, waiting for transfers between devices: 13.4 us -> 5.37 us  [around(): lax.ppermute(right[1], 'z', ring(4, 3))]
    ppermute x0 -> x6, starting transfers between devices: none -> 7.78 us  [the longest x3 3.98 us: body(): some = [some] + [lax.ppermute(some, 'x', ring(4, k)) for k in (1, 2, 3)]]
    ppermute x6 -> x4, waiting for transfers between devices: 9.39 us -> 2.68 us  [around(): left = [lax.ppermute(v, 'z', ring(4, 1)) for v in parts]]
  transfers between devices with their start and end apart: 53 -> 51, of which waited for: 30 -> 24; matrix products, arithmetic and copies ran while one was open for 2% -> 2% of each run, Pallas kernels for 22% -> 24%
where the time goes in v2:
time: 528 us; the launch traced here: 519 us
  Pallas kernels  172 us (33%)
  waiting for transfers between devices  151 us (29%)
  starting transfers between devices  104 us (20%)
  blocking collectives  45 us (9%)
  local copies, waits for them, and re-layouts  22.4 us (4%)
  between operations  15.8 us (3%)
  other arithmetic  8.93 us (2%)
    pallas_call x29, Pallas kernels, launch(): pl.pallas_call(body, name=name, out_shape=tuple((pltpu.HBM(o.shape, o.dty...  160 us
    all_to_all x5, waiting for transfers between devices, spread(): return lax.all_to_all(jnp.broadcast_to(v[None], (n,) + v.shape), axes, 0, 0)  37.2 us
    all_to_all x7, starting transfers between devices, tell(): return lax.all_to_all(v, BATCH, 0, 0)  36.6 us
    ppermute x3, waiting for transfers between devices, body(): some = [some] + [lax.ppermute(some, 'y', ring(4, k)) for k in (1, 2, 3)]  30.6 us
    ppermute x4, waiting for transfers between devices, around(): right = [lax.ppermute(v, 'z', ring(4, 3)) for v in parts]  27.3 us
    all_to_all x5, starting transfers between devices, spread(): return lax.all_to_all(jnp.broadcast_to(v[None], (n,) + v.shape), axes, 0, 0)  23.6 us
    all_to_all x1, blocking collectives, spread(): return lax.all_to_all(jnp.broadcast_to(v[None], (n,) + v.shape), axes, 0, 0)  23 us
    all_to_all x1, blocking collectives, tell(): return lax.all_to_all(v, BATCH, 0, 0)  22.1 us
  transfers between devices with their start and end apart: 51, of which 24 were waited for; matrix products, arithmetic and copies ran while one was open for 2% of the time, Pallas kernels for 24%

profile of v2, /device:TPU:1, one launch (start us, length us, event | category | flops | bytes accessed | tf_op | source)
XLA Modules:
  0.0 519.4 jit_solution(16339870381138671944)
XLA Ops:
  21.5 27.3 %collective-permute-done.2.refs_2_.t1 = bf16[1312,256]{1,0:T(8,128)(2,1)S(1)} collective-permute-done((bf16[1312,256]{1,0:T(8,128)(2,1)S(1)}, bf16[1312,256]{1,0:T(8,128)(2,1)S(1)}, u32[]{:S(2)}, u32[]{:S(2)}) %collective-permute-start.2) | collective-permute-done | bytes 671776 | tf_op jit(solution)/shard_map/ppermute | solution.py:1183
  58.3 12.9 %all-to-all-done = bf16[4,96,128]{2,1,0:T(8,128)(2,1)S(1)} async-done(((bf16[4,96,128]{2,1,0:T(8,128)(2,1)}), bf16[4,96,128]{2,1,0:T(8,128)(2,1)S(1)}, u32[]{:S(2)}, u32[]{:S(2)}) %all-to-all-start) | async-done | bytes 98336 | tf_op jit(solution)/shard_map/all_to_all | solution.py:1152
  73.0 8.0 %reduce_one.1 = (f32[2144,512]{1,0:T(8,128)}, f32[32,4,512]{2,1,0:T(4,128)}) custom-call(s32[5]{0:T(128)S(1)} %stack.101.zi, bf16[1312,256]{1,0:T(8,128)(2,1)} %copy-done, bf16[1344,256]{1,0:T(8,128)(2,1)} %copy-done.10, bf16[1312,256]{1,0:T(8,128)(2,1)} %copy-done.2, bf16[1344,256]{1,0:T(8,128)(2,1)} %collective-permute-done.3.refs_3_, ...), custom_call_target="tpu_custom_call" | custom-call | flops 2248146944 | bytes 10000000 | tf_op jit(solution)/shard_map/reduce_one/pallas_call | solution.py:43
  81.0 22.1 %all_to_all.80.st = f32[32,4,512]{2,1,0:T(4,128)S(1)} all-to-all(f32[32,4,512]{2,1,0:T(4,128)} %get-tuple-element.187), channel_id=1, replica_groups=mesh['y'=4,'x'=4,'c'=2,'z'=4] {'y','x','c'}, dimensions={0} | all-to-all | bytes 524288 | tf_op jit(solution)/shard_map/all_to_all | solution.py:1161
  103.1 8.6 %spatial_one.1 = (bf16[544,4608]{1,0:T(8,128)(2,1)}, f32[544,512]{1,0:T(8,128)}, f32[32,4,512]{2,1,0:T(4,128)}, f32[4,512]{1,0:T(4,128)S(1)}) custom-call(f32[32,4,512]{2,1,0:T(4,128)S(1)} %all_to_all.80.st, f32[4,32,128]{2,1,0:T(8,128)S(1)} %convert_add_fusion.norms, f32[2144,512]{1,0:T(8,128)} %get-tuple-element.188.z1, bf16[32,4,400,128]{3,2,1,0:T(8,128)(2,1)} %bitcast.68), custom_call_target="tpu_custom_call" | custom-call | flops 40000000000 | bytes 20000000 | tf_op jit(solution)/shard_map/spatial_one/pallas_call | solution.py:43
  116.4 9.1 %shortcut.2 = (bf16[544,1024]{1,0:T(8,128)(2,1)}, f32[544,2048]{1,0:T(8,128)}, f32[4,2048]{1,0:T(4,128)S(1)}) custom-call(s32[5]{0:T(128)S(1)} %stack.101.zi, bf16[1312,256]{1,0:T(8,128)(2,1)} %copy-done, bf16[1344,256]{1,0:T(8,128)(2,1)} %copy-done.10, bf16[1312,256]{1,0:T(8,128)(2,1)} %copy-done.2, bf16[1344,256]{1,0:T(8,128)(2,1)} %collective-permute-done.3.refs_3_, ...), custom_call_target="tpu_custom_call" | custom-call | flops 2281701376 | bytes 14000000 | tf_op jit(solution)/shard_map/shortcut/pallas_call | solution.py:43
  125.5 5.3 %expand_one.2 = (bf16[544,512]{1,0:T(8,128)(2,1)}, f32[544,2048]{1,0:T(8,128)}, f32[4,2048]{1,0:T(4,128)S(1)}, f32[4,512]{1,0:T(4,128)S(1)}) custom-call(f32[32,4,512]{2,1,0:T(4,128)S(1)} %all-to-all-done.2.st, f32[4,32,128]{2,1,0:T(8,128)S(1)} %convert_add_fusion.norms, f32[544,512]{1,0:T(8,128)} %get-tuple-element.197.z.z2, bf16[32,4,400,128]{3,2,1,0:T(8,128)(2,1)} %bitcast.70), custom_call_target="tpu_custom_call" | custom-call | flops 1140850688 | bytes 9000000 | tf_op jit(solution)/shard_map/expand_one/pallas_call | solution.py:43
  132.3 23.0 %all_to_all.81.st3 = f32[16,8,2048]{2,1,0:T(8,128)S(1)} all-to-all(f32[16,8,2048]{2,1,0:T(8,128)S(1)} %broadcast_in_dim.15), channel_id=1, replica_groups=mesh['y'=4,'x'=4,'c'=2,'z'=4] {'y','x'}, dimensions={0} | all-to-all | bytes 2097152 | tf_op jit(solution)/shard_map/all_to_all | solution.py:1152
  155.3 10.6 %reduce_two.2 = (f32[544,2048]{1,0:T(8,128)}, bf16[544,2048]{1,0:T(8,128)(2,1)}, f32[544,512]{1,0:T(8,128)}, f32[32,4,512]{2,1,0:T(4,128)}, f32[4,2048]{1,0:T(4,128)S(1)}, /*index=5*/f32[4,2048]{1,0:T(4,128)S(1)}) custom-call(f32[16,8,2048]{2,1,0:T(8,128)S(1)} %all_to_all.81.st3, f32[4,32,128]{2,1,0:T(8,128)S(1)} %convert_add_fusion.norms, ...), custom_call_target="tpu_custom_call" | custom-call | flops 1140850688 | bytes 20000000 | tf_op jit(solution)/shard_map/reduce_two/pallas_call | solution.py:43
  165.8 6.0 %all-to-all-start.4 = ((f32[32,4,512]{2,1,0:T(4,128)}), f32[32,4,512]{2,1,0:T(4,128)}, u32[]{:S(2)}, u32[]{:S(2)}) async-start(f32[32,4,512]{2,1,0:T(4,128)} %get-tuple-element.202), calls=%async_computation.4 | async-start | bytes 524288 | tf_op jit(solution)/shard_map/all_to_all | solution.py:1161
  180.9 8.4 %spatial_two.1 = (bf16[544,4608]{1,0:T(8,128)(2,1)}, f32[544,512]{1,0:T(8,128)}, f32[32,4,512]{2,1,0:T(4,128)}, f32[4,512]{1,0:T(4,128)S(1)}) custom-call(f32[32,4,512]{2,1,0:T(4,128)} %all-to-all-done.4.st, f32[4,32,128]{2,1,0:T(8,128)S(1)} %convert_add_fusion.norms, f32[544,512]{1,0:T(8,128)} %get-tuple-element.204.z4, bf16[32,4,208,128]{3,2,1,0:T(8,128)(2,1)} %bitcast.76), custom_call_target="tpu_custom_call" | custom-call | flops 2566914048 | bytes 20000000 | tf_op jit(solution)/shard_map/spatial_two/pallas_call | solution.py:43
  210.7 5.7 %all-to-all-start.6 = ((f32[16,4,2048]{2,1,0:T(4,128)}), f32[16,4,2048]{2,1,0:T(4,128)S(1)}, u32[]{:S(2)}, u32[]{:S(2)}) async-start(f32[16,4,2048]{2,1,0:T(4,128)} %broadcast_in_dim.16), calls=%async_computation.6 | async-start | bytes 1048576 | tf_op jit(solution)/shard_map/all_to_all | solution.py:1152
  219.4 5.4 %collective-permute-done.13.refs_5_ = bf16[272,512]{1,0:T(8,128)(2,1)S(1)} collective-permute-done((bf16[272,512]{1,0:T(8,128)(2,1)S(1)}, bf16[272,512]{1,0:T(8,128)(2,1)S(1)}, u32[]{:S(2)}, u32[]{:S(2)}) %collective-permute-start.13) | collective-permute-done | bytes 278560 | tf_op jit(solution)/shard_map/ppermute | solution.py:1185
  228.6 8.1 %output.1 = (f32[544,512]{1,0:T(8,128)}, f32[544,2048]{1,0:T(8,128)}, f32[4,2048]{1,0:T(4,128)S(1)}, f32[4,2048]{1,0:T(4,128)S(1)}) custom-call(s32[5]{0:T(128)S(1)} %stack.101.zi, f32[16,4,2048]{2,1,0:T(4,128)S(1)} %all-to-all-done.6.st, f32[4,32,128]{2,1,0:T(8,128)S(1)} %convert_add_fusion.norms, f32[544,2048]{1,0:T(8,128)} %get-tuple-element.209.z6, ...), custom_call_target="tpu_custom_call" | custom-call | bytes 20000000 | tf_op jit(solution)/shard_map/output/pallas_call | solution.py:43
  240.4 6.7 %all-to-all-start.7 = ((f32[16,4,2048]{2,1,0:T(4,128)}), f32[16,4,2048]{2,1,0:T(4,128)S(1)}, u32[]{:S(2)}, u32[]{:S(2)}) async-start(f32[16,4,2048]{2,1,0:T(4,128)} %broadcast_in_dim.17), calls=%async_computation.7 | async-start | bytes 1048576 | tf_op jit(solution)/shard_map/all_to_all | solution.py:1152
  248.3 9.5 %all-to-all-done.7.stb = f32[16,4,2048]{2,1,0:T(4,128)S(1)} async-done(((f32[16,4,2048]{2,1,0:T(4,128)}), f32[16,4,2048]{2,1,0:T(4,128)S(1)}, u32[]{:S(2)}, u32[]{:S(2)}) %all-to-all-start.7) | async-done | bytes 524320 | tf_op jit(solution)/shard_map/all_to_all | solution.py:1152
  257.8 10.0 %back_expand_two.1 = (bf16[544,512]{1,0:T(8,128)(2,1)S(1)}, f32[544,512]{1,0:T(8,128)}, f32[32,4,512]{2,1,0:T(4,128)}, f32[2,2048]{1,0:T(2,128)S(1)}) custom-call(s32[5]{0:T(128)S(1)} %stack.101.zi, f32[16,4,2048]{2,1,0:T(4,128)S(1)} %all-to-all-done.7.stb, f32[4,32,128]{2,1,0:T(8,128)S(1)} %convert_add_fusion.norms, f32[4,2048]{1,0:T(4,128)S(1)} %get-tuple-element.224.sum6, ...), custom_call_target="tpu_custom_call" | custom-call | flops 1140850688 | bytes 14000000 | tf_op jit(solution)/shard_map/back_expand_two/pallas_call | solution.py:43
  274.3 7.7 %all-to-all-done.8.stb = f32[32,4,512]{2,1,0:T(4,128)S(1)} async-done(((f32[32,4,512]{2,1,0:T(4,128)}), f32[32,4,512]{2,1,0:T(4,128)S(1)}, u32[]{:S(2)}, u32[]{:S(2)}) %all-to-all-start.8) | async-done | bytes 262176 | tf_op jit(solution)/shard_map/all_to_all | solution.py:1161
  282.0 9.0 %back_spatial_two.1 = (bf16[544,128]{1,0:T(8,128)(2,1)S(1)}, f32[544,512]{1,0:T(8,128)}, f32[32,4,512]{2,1,0:T(4,128)}, f32[2,512]{1,0:T(2,128)S(1)}) custom-call(s32[5]{0:T(128)S(1)} %stack.101.zi, f32[32,4,512]{2,1,0:T(4,128)S(1)} %all-to-all-done.8.stb, f32[4,32,128]{2,1,0:T(8,128)S(1)} %convert_add_fusion.norms, f32[4,512]{1,0:T(4,128)S(1)} %get-tuple-element.225.sum5, ...), custom_call_target="tpu_custom_call" | custom-call | flops 2566914048 | bytes 10000000 | tf_op jit(solution)/shard_map/back_spatial_two/pallas_call | solution.py:43
  304.1 11.1 %back_reduce_two.1 = (bf16[544,128]{1,0:T(8,128)(2,1)S(1)}, f32[544,2048]{1,0:T(8,128)}, f32[6,2048]{1,0:T(8,128)S(1)}, f32[2,512]{1,0:T(2,128)S(1)}) custom-call(s32[5]{0:T(128)S(1)} %stack.101.zi, f32[32,4,512]{2,1,0:T(4,128)S(1)} %all-to-all-done.9.stb, f32[4,32,128]{2,1,0:T(8,128)S(1)} %convert_add_fusion.norms, f32[4,512]{1,0:T(4,128)S(1)} %get-tuple-element.233.sum4, ...), custom_call_target="tpu_custom_call" | custom-call | flops 1140850688 | bytes 22000000 | tf_op jit(solution)/shard_map/back_reduce_two/pallas_call | solution.py:43
  324.5 14.8 %all-to-all-done.10.stb = f32[16,6,2048]{2,1,0:T(8,128)S(1)} async-done(((f32[16,6,2048]{2,1,0:T(8,128)}), f32[16,6,2048]{2,1,0:T(8,128)S(1)}, u32[]{:S(2)}, u32[]{:S(2)}) %all-to-all-start.10) | async-done | bytes 786464 | tf_op jit(solution)/shard_map/all_to_all | solution.py:1152
  340.0 10.0 %back_expand_one.1 = (bf16[544,512]{1,0:T(8,128)(2,1)S(1)}, f32[544,512]{1,0:T(8,128)}, f32[32,4,512]{2,1,0:T(4,128)}, f32[2,2048]{1,0:T(2,128)S(1)}, f32[4,2048]{1,0:T(4,128)S(1)}) custom-call(s32[5]{0:T(128)S(1)} %stack.101.zi, f32[16,6,2048]{2,1,0:T(8,128)S(1)} %all-to-all-done.10.stb, f32[4,32,128]{2,1,0:T(8,128)S(1)} %convert_add_fusion.norms, ...), custom_call_target="tpu_custom_call" | custom-call | flops 1140850688 | bytes 16000000 | tf_op jit(solution)/shard_map/back_expand_one/pallas_call | solution.py:43
  356.7 5.4 %back_shortcut.1 = (bf16[544,512]{1,0:T(8,128)(2,1)S(1)}, f32[544,256]{1,0:T(8,128)S(1)}, f32[2,2048]{1,0:T(2,128)S(1)}) custom-call(s32[5]{0:T(128)S(1)} %stack.101.zi, f32[4,32,128]{2,1,0:T(8,128)S(1)} %convert_add_fusion.norms, f32[4,2048]{1,0:T(4,128)S(1)} %get-tuple-element.253.gsum, f32[4,2048]{1,0:T(4,128)S(1)} %get-tuple-element.242.sums, ...), custom_call_target="tpu_custom_call" | custom-call | flops 570425344 | bytes 10000000 | tf_op jit(solution)/shard_map/back_shortcut/pallas_call | solution.py:43
  369.7 13.8 %back_spatial_one.1 = (bf16[544,128]{1,0:T(8,128)(2,1)S(1)}, f32[2144,512]{1,0:T(8,128)}, f32[32,4,512]{2,1,0:T(4,128)}, f32[2,512]{1,0:T(2,128)S(1)}) custom-call(s32[5]{0:T(128)S(1)} %stack.101.zi, f32[32,4,512]{2,1,0:T(4,128)S(1)} %all-to-all-done.11.stb, f32[4,32,128]{2,1,0:T(8,128)S(1)} %convert_add_fusion.norms, f32[4,512]{1,0:T(4,128)S(1)} %copy-done.41, ...), custom_call_target="tpu_custom_call" | custom-call | flops 2566914048 | bytes 20000000 | tf_op jit(solution)/shard_map/back_spatial_one/pallas_call | solution.py:43
  383.5 7.5 %all-to-all-start.12 = ((f32[32,4,512]{2,1,0:T(4,128)}), f32[32,4,512]{2,1,0:T(4,128)S(1)}, u32[]{:S(2)}, u32[]{:S(2)}) async-start(f32[32,4,512]{2,1,0:T(4,128)} %get-tuple-element.264), calls=%async_computation.12 | async-start | bytes 524288 | tf_op jit(solution)/shard_map/all_to_all | solution.py:1161
  400.6 5.4 %all-to-all-start.13 = ((bf16[16,464,128]{2,1,0:T(8,128)(2,1)}), bf16[16,464,128]{2,1,0:T(8,128)(2,1)S(1)}, u32[]{:S(2)}, u32[]{:S(2)}) async-start(bf16[16,464,128]{2,1,0:T(8,128)(2,1)} %bitcast.80), calls=%async_computation.13 | async-start | bytes 3801088 | tf_op jit(solution)/shard_map/all_to_all | solution.py:1483
  407.7 6.1 %back_reduce_one.1 = (bf16[2144,128]{1,0:T(8,128)(2,1)S(1)}, bf16[2144,512]{1,0:T(8,128)(2,1)}, f32[2,512]{1,0:T(2,128)S(1)}) custom-call(s32[5]{0:T(128)S(1)} %stack.101.zi, f32[32,4,512]{2,1,0:T(4,128)S(1)} %copy-done.20, f32[4,32,128]{2,1,0:T(8,128)S(1)} %convert_add_fusion.norms, f32[4,512]{1,0:T(4,128)S(1)} %copy-done.43, ...), custom_call_target="tpu_custom_call" | custom-call | bytes 12000000 | tf_op jit(solution)/shard_map/back_reduce_one/pallas_call | solution.py:43
  420.4 14.6 %all-to-all-done.13.src = bf16[16,464,128]{2,1,0:T(8,128)(2,1)S(1)} async-done(((bf16[16,464,128]{2,1,0:T(8,128)(2,1)}), bf16[16,464,128]{2,1,0:T(8,128)(2,1)S(1)}, u32[]{:S(2)}, u32[]{:S(2)}) %all-to-all-start.13) | async-done | bytes 1900576 | tf_op jit(solution)/shard_map/all_to_all | solution.py:1483
  464.6 17.1 %collective-permute-done.27.a3 = bf16[1856,128]{1,0:T(8,128)(2,1)S(1)} collective-permute-done((bf16[1856,128]{1,0:T(8,128)(2,1)S(1)}, bf16[1856,128]{1,0:T(8,128)(2,1)S(1)}, u32[]{:S(2)}, u32[]{:S(2)}) %collective-permute-start.27) | collective-permute-done | bytes 475168 | tf_op jit(solution)/shard_map/ppermute | solution.py:1539
  484.5 10.8 %collective-permute-done.25.a1 = bf16[1856,128]{1,0:T(8,128)(2,1)S(1)} collective-permute-done((bf16[1856,128]{1,0:T(8,128)(2,1)S(1)}, bf16[1856,128]{1,0:T(8,128)(2,1)S(1)}, u32[]{:S(2)}, u32[]{:S(2)}) %collective-permute-start.25) | collective-permute-done | bytes 475168 | tf_op jit(solution)/shard_map/ppermute | solution.py:1539
  498.7 5.8 %grads_kept.1 = (f32[512,512]{1,0:T(8,128)}, f32[4608,128]{1,0:T(8,128)}, f32[2048,128]{1,0:T(8,128)}, f32[512,512]{1,0:T(8,128)}, f32[1024,512]{1,0:T(8,128)}, ...) custom-call(s32[5]{0:T(128)S(1)} %stack.101.zi, s32[16]{0:T(128)S(1)} %stack.118.places, ...), custom_call_target="tpu_custom_call" | custom-call | bytes 8000000 | tf_op jit(solution)/shard_map/grads_kept/pallas_call | solution.py:1133
  505.4 6.2 %grads_given.1 = (f32[512,512]{1,0:T(8,128)}, f32[4608,128]{1,0:T(8,128)}, f32[2048,128]{1,0:T(8,128)}, f32[512,512]{1,0:T(8,128)}, f32[1024,512]{1,0:T(8,128)},...) custom-call(s32[5]{0:T(128)S(1)} %stack.101.zi, ...), custom_call_target="tpu_custom_call", output_to_operand_aliasing={{0}: (7, {}), {1}: (8, {}), {2}: (9, {}), {3}: (10, {}), {4... | custom-call | bytes 8000000 | tf_op jit(solution)/shard_map/grads_given/pallas_call | solution.py:1133
  (287 shorter events, 172.1 us)
Async XLA Ops:
  7.2 95.9 %all-gather.5.cloned.1.call-start = ((), (), s32[]{:S(2)}) async-start(), calls=%async_computation.16 | async-start | bytes 13209600 | tf_op jit(solution)/shard_map/all_gather | solution.py:1246
  13.3 167.5 %all-gather.7.cloned.1.call-start = ((), (), s32[]{:S(2)}) async-start(), calls=%async_computation.17 | async-start | bytes 6868992 | tf_op jit(solution)/shard_map/all_gather | solution.py:1247
  14.1 37.3 %collective-permute-start.3 = (bf16[1344,256]{1,0:T(8,128)(2,1)S(1)}, bf16[1344,256]{1,0:T(8,128)(2,1)}, u32[]{:S(2)}, u32[]{:S(2)}) collective-permute-start(bf16[1344,256]{1,0:T(8,128)(2,1)S(1)} %get-tuple-element.176.refs_1_), channel_id=1, source_target_pairs={{0,3},{1,0},{2,1},{3,2},{4,7},{5,4},{6,5},{7,6},{8,11},{9,8},{10,9... | collective-permute-start | bytes 2064392 | tf_op jit(solution)/shard_map/ppermute | solution.py:1183
  18.8 32.7 %collective-permute-start.1 = (bf16[1344,256]{1,0:T(8,128)(2,1)S(1)}, bf16[1344,256]{1,0:T(8,128)(2,1)}, u32[]{:S(2)}, u32[]{:S(2)}) collective-permute-start(bf16[1344,256]{1,0:T(8,128)(2,1)S(1)} %get-tuple-element.176.refs_1_), channel_id=1, source_target_pairs={{0,1},{1,2},{2,3},{3,0},{4,5},{5,6},{6,7},{7,4},{8,9},{9,10},{10,1... | collective-permute-start | bytes 2064392 | tf_op jit(solution)/shard_map/ppermute | solution.py:1182
  18.8 30.0 %collective-permute-start.2 = (bf16[1312,256]{1,0:T(8,128)(2,1)S(1)}, bf16[1312,256]{1,0:T(8,128)(2,1)S(1)}, u32[]{:S(2)}, u32[]{:S(2)}) collective-permute-start(bf16[1312,256]{1,0:T(8,128)(2,1)S(1)} %get-tuple-element.174.refs_0_.t0), channel_id=1, source_target_pairs={{0,3},{1,0},{2,1},{3,2},{4,7},{5,4},{6,5},{7,6},{8,11},{9,8},{10,9... | collective-permute-start | bytes 2015240 | tf_op jit(solution)/shard_map/ppermute | solution.py:1183
  21.4 30.0 %collective-permute-start = (bf16[1312,256]{1,0:T(8,128)(2,1)S(1)}, bf16[1312,256]{1,0:T(8,128)(2,1)S(1)}, u32[]{:S(2)}, u32[]{:S(2)}) collective-permute-start(bf16[1312,256]{1,0:T(8,128)(2,1)S(1)} %get-tuple-element.174.refs_0_.t0), channel_id=1, source_target_pairs={{0,1},{1,2},{2,3},{3,0},{4,5},{5,6},{6,7},{7,4},{8,9},{9,10},{10,1... | collective-permute-start | bytes 2015240 | tf_op jit(solution)/shard_map/ppermute | solution.py:1182
  51.4 19.8 %collective-permute-start.4 = (bf16[1312,256]{1,0:T(8,128)(2,1)S(1)}, bf16[1312,256]{1,0:T(8,128)(2,1)S(1)}, u32[]{:S(2)}, u32[]{:S(2)}) collective-permute-start(bf16[1312,256]{1,0:T(8,128)(2,1)S(1)} %collective-permute-done.refs_6_.t3), channel_id=1, source_target_pairs={{0,1},{1,2},{2,3},{3,0},{4,5},{5,6},{6,7},{7,4},{8,9},{9,10},{10,1... | collective-permute-start | bytes 2015240 | tf_op jit(solution)/shard_map/ppermute | solution.py:1185
  51.5 19.8 %collective-permute-start.5 = (bf16[1344,256]{1,0:T(8,128)(2,1)}, bf16[1344,256]{1,0:T(8,128)(2,1)S(1)}, u32[]{:S(2)}, u32[]{:S(2)}) collective-permute-start(bf16[1344,256]{1,0:T(8,128)(2,1)} %collective-permute-done.3.refs_3_), channel_id=1, source_target_pairs={{0,3},{1,0},{2,1},{3,2},{4,7},{5,4},{6,5},{7,6},{8,11},{9,8},{10,9... | collective-permute-start | bytes 2064392 | tf_op jit(solution)/shard_map/ppermute | solution.py:1185
  54.9 16.4 %all-to-all-start = ((bf16[4,96,128]{2,1,0:T(8,128)(2,1)}), bf16[4,96,128]{2,1,0:T(8,128)(2,1)S(1)}, u32[]{:S(2)}, u32[]{:S(2)}) async-start(bf16[4,96,128]{2,1,0:T(8,128)(2,1)} %broadcast_in_dim.14), calls=%async_computation | async-start | bytes 196608 | tf_op jit(solution)/shard_map/all_to_all | solution.py:1152
  165.8 15.1 %all-to-all-start.4 = ((f32[32,4,512]{2,1,0:T(4,128)}), f32[32,4,512]{2,1,0:T(4,128)}, u32[]{:S(2)}, u32[]{:S(2)}) async-start(f32[32,4,512]{2,1,0:T(4,128)} %get-tuple-element.202), calls=%async_computation.4 | async-start | bytes 524288 | tf_op jit(solution)/shard_map/all_to_all | solution.py:1161
  189.3 13.8 %all-to-all-start.5 = ((f32[32,4,512]{2,1,0:T(4,128)}), f32[32,4,512]{2,1,0:T(4,128)S(1)}, u32[]{:S(2)}, u32[]{:S(2)}) async-start(f32[32,4,512]{2,1,0:T(4,128)} %get-tuple-element.206), calls=%async_computation.5 | async-start | bytes 524288 | tf_op jit(solution)/shard_map/all_to_all | solution.py:1161
  194.7 21.7 %collective-permute-start.10 = (bf16[272,512]{1,0:T(8,128)(2,1)S(1)}, bf16[272,512]{1,0:T(8,128)(2,1)S(1)}, u32[]{:S(2)}, u32[]{:S(2)}) collective-permute-start(bf16[272,512]{1,0:T(8,128)(2,1)S(1)} %get-tuple-element.211.refs_0_), channel_id=1, source_target_pairs={{0,3},{1,0},{2,1},{3,2},{4,7},{5,4},{6,5},{7,6},{8,11},{9,8},{10,9... | collective-permute-start | bytes 835592 | tf_op jit(solution)/shard_map/ppermute | solution.py:1183
  198.2 18.2 %collective-permute-start.8 = (bf16[272,512]{1,0:T(8,128)(2,1)S(1)}, bf16[272,512]{1,0:T(8,128)(2,1)S(1)}, u32[]{:S(2)}, u32[]{:S(2)}) collective-permute-start(bf16[272,512]{1,0:T(8,128)(2,1)S(1)} %get-tuple-element.211.refs_0_), channel_id=1, source_target_pairs={{0,1},{1,2},{2,3},{3,0},{4,5},{5,6},{6,7},{7,4},{8,9},{9,10},{10,1... | collective-permute-start | bytes 835592 | tf_op jit(solution)/shard_map/ppermute | solution.py:1182
  198.2 18.2 %collective-permute-start.11 = (bf16[272,512]{1,0:T(8,128)(2,1)S(1)}, bf16[272,512]{1,0:T(8,128)(2,1)S(1)}, u32[]{:S(2)}, u32[]{:S(2)}) collective-permute-start(bf16[272,512]{1,0:T(8,128)(2,1)S(1)} %get-tuple-element.212.refs_1_), channel_id=1, source_target_pairs={{0,3},{1,0},{2,1},{3,2},{4,7},{5,4},{6,5},{7,6},{8,11},{9,8},{10,9... | collective-permute-start | bytes 835592 | tf_op jit(solution)/shard_map/ppermute | solution.py:1183
  201.2 15.2 %collective-permute-start.9 = (bf16[272,512]{1,0:T(8,128)(2,1)S(1)}, bf16[272,512]{1,0:T(8,128)(2,1)S(1)}, u32[]{:S(2)}, u32[]{:S(2)}) collective-permute-start(bf16[272,512]{1,0:T(8,128)(2,1)S(1)} %get-tuple-element.212.refs_1_), channel_id=1, source_target_pairs={{0,1},{1,2},{2,3},{3,0},{4,5},{5,6},{6,7},{7,4},{8,9},{9,10},{10,1... | collective-permute-start | bytes 835592 | tf_op jit(solution)/shard_map/ppermute | solution.py:1182
  210.7 17.2 %all-to-all-start.6 = ((f32[16,4,2048]{2,1,0:T(4,128)}), f32[16,4,2048]{2,1,0:T(4,128)S(1)}, u32[]{:S(2)}, u32[]{:S(2)}) async-start(f32[16,4,2048]{2,1,0:T(4,128)} %broadcast_in_dim.16), calls=%async_computation.6 | async-start | bytes 1048576 | tf_op jit(solution)/shard_map/all_to_all | solution.py:1152
  240.4 17.4 %all-to-all-start.7 = ((f32[16,4,2048]{2,1,0:T(4,128)}), f32[16,4,2048]{2,1,0:T(4,128)S(1)}, u32[]{:S(2)}, u32[]{:S(2)}) async-start(f32[16,4,2048]{2,1,0:T(4,128)} %broadcast_in_dim.17), calls=%async_computation.7 | async-start | bytes 1048576 | tf_op jit(solution)/shard_map/all_to_all | solution.py:1152
  267.7 14.3 %all-to-all-start.8 = ((f32[32,4,512]{2,1,0:T(4,128)}), f32[32,4,512]{2,1,0:T(4,128)S(1)}, u32[]{:S(2)}, u32[]{:S(2)}) async-start(f32[32,4,512]{2,1,0:T(4,128)} %get-tuple-element.227), calls=%async_computation.8 | async-start | bytes 524288 | tf_op jit(solution)/shard_map/all_to_all | solution.py:1161
  317.6 21.7 %all-to-all-start.10 = ((f32[16,6,2048]{2,1,0:T(8,128)}), f32[16,6,2048]{2,1,0:T(8,128)S(1)}, u32[]{:S(2)}, u32[]{:S(2)}) async-start(f32[16,6,2048]{2,1,0:T(8,128)} %broadcast_in_dim.18), calls=%async_computation.10 | async-start | bytes 2097152 | tf_op jit(solution)/shard_map/all_to_all | solution.py:1152
  321.3 33.7 %collective-permute-start.16 = (bf16[1024,128]{1,0:T(8,128)(2,1)}, bf16[1024,128]{1,0:T(8,128)(2,1)}, u32[]{:S(2)}, u32[]{:S(2)}) collective-permute-start(bf16[1024,128]{1,0:T(8,128)(2,1)} %copy-done.52), channel_id=1, source_target_pairs={{0,4},{4,0},{1,5},{5,1},{2,6},{6,2},{3,7},{7,3},{8,12},{12,8},{9,1... | collective-permute-start | bytes 786440 | tf_op jit(solution)/shard_map/ppermute | solution.py:1178
  321.6 45.8 %collective-permute-start.17 = (bf16[2304,128]{1,0:T(8,128)(2,1)}, bf16[2304,128]{1,0:T(8,128)(2,1)}, u32[]{:S(2)}, u32[]{:S(2)}) collective-permute-start(bf16[2304,128]{1,0:T(8,128)(2,1)} %copy-done.48), channel_id=1, source_target_pairs={{0,4},{4,0},{1,5},{5,1},{2,6},{6,2},{3,7},{7,3},{8,12},{12,8},{9,1... | collective-permute-start | bytes 1769480 | tf_op jit(solution)/shard_map/ppermute | solution.py:1178
  350.0 17.1 %all-to-all-start.11 = ((f32[32,4,512]{2,1,0:T(4,128)}), f32[32,4,512]{2,1,0:T(4,128)S(1)}, u32[]{:S(2)}, u32[]{:S(2)}) async-start(f32[32,4,512]{2,1,0:T(4,128)} %get-tuple-element.252), calls=%async_computation.11 | async-start | bytes 524288 | tf_op jit(solution)/shard_map/all_to_all | solution.py:1161
  367.1 28.5 %collective-permute-start.19 = (bf16[3072,128]{1,0:T(8,128)(2,1)S(1)}, bf16[3072,128]{1,0:T(8,128)(2,1)}, u32[]{:S(2)}, u32[]{:S(2)}) collective-permute-start(bf16[3072,128]{1,0:T(8,128)(2,1)S(1)} %get-tuple-element.272), channel_id=1, source_target_pairs={{0,4},{4,0},{1,5},{5,1},{2,6},{6,2},{3,7},{7,3},{8,12},{12,8},{9,1... | collective-permute-start | bytes 2359304 | tf_op jit(solution)/shard_map/ppermute | solution.py:1178
  369.4 26.1 %collective-permute-start.18 = (bf16[1024,128]{1,0:T(8,128)(2,1)S(1)}, bf16[1024,128]{1,0:T(8,128)(2,1)S(1)}, u32[]{:S(2)}, u32[]{:S(2)}) collective-permute-start(bf16[1024,128]{1,0:T(8,128)(2,1)S(1)} %copy-done.54), channel_id=1, source_target_pairs={{0,4},{4,0},{1,5},{5,1},{2,6},{6,2},{3,7},{7,3},{8,12},{12,8},{9,1... | collective-permute-start | bytes 786440 | tf_op jit(solution)/shard_map/ppermute | solution.py:1178
  383.5 16.4 %all-to-all-start.12 = ((f32[32,4,512]{2,1,0:T(4,128)}), f32[32,4,512]{2,1,0:T(4,128)S(1)}, u32[]{:S(2)}, u32[]{:S(2)}) async-start(f32[32,4,512]{2,1,0:T(4,128)} %get-tuple-element.264), calls=%async_computation.12 | async-start | bytes 524288 | tf_op jit(solution)/shard_map/all_to_all | solution.py:1161
  400.6 34.4 %all-to-all-start.13 = ((bf16[16,464,128]{2,1,0:T(8,128)(2,1)}), bf16[16,464,128]{2,1,0:T(8,128)(2,1)S(1)}, u32[]{:S(2)}, u32[]{:S(2)}) async-start(bf16[16,464,128]{2,1,0:T(8,128)(2,1)} %bitcast.80), calls=%async_computation.13 | async-start | bytes 3801088 | tf_op jit(solution)/shard_map/all_to_all | solution.py:1483
  406.0 13.3 %collective-permute-start.20 = (bf16[2304,128]{1,0:T(8,128)(2,1)}, bf16[2304,128]{1,0:T(8,128)(2,1)S(1)}, u32[]{:S(2)}, u32[]{:S(2)}) collective-permute-start(bf16[2304,128]{1,0:T(8,128)(2,1)} %get-tuple-element.279), channel_id=1, source_target_pairs={{0,4},{4,0},{1,5},{5,1},{2,6},{6,2},{3,7},{7,3},{8,12},{12,8},{9,1... | collective-permute-start | bytes 1769480 | tf_op jit(solution)/shard_map/ppermute | solution.py:1178
  435.0 19.9 %all-to-all-start.14 = ((bf16[16,176,128]{2,1,0:T(8,128)(2,1)}), bf16[16,176,128]{2,1,0:T(8,128)(2,1)S(1)}, u32[]{:S(2)}, u32[]{:S(2)}) async-start(bf16[16,176,128]{2,1,0:T(8,128)(2,1)} %bitcast.83), calls=%async_computation.14 | async-start | bytes 1441792 | tf_op jit(solution)/shard_map/all_to_all | solution.py:1509
  456.2 39.1 %all-to-all-start.15 = ((bf16[16,224,128]{2,1,0:T(8,128)(2,1)}), bf16[16,224,128]{2,1,0:T(8,128)(2,1)S(1)}, u32[]{:S(2)}, u32[]{:S(2)}) async-start(bf16[16,224,128]{2,1,0:T(8,128)(2,1)} %broadcast_in_dim.19), calls=%async_computation.15 | async-start | bytes 1835008 | tf_op jit(solution)/shard_map/all_to_all | solution.py:1152
  460.6 21.1 %collective-permute-start.27 = (bf16[1856,128]{1,0:T(8,128)(2,1)S(1)}, bf16[1856,128]{1,0:T(8,128)(2,1)S(1)}, u32[]{:S(2)}, u32[]{:S(2)}) collective-permute-start(bf16[1856,128]{1,0:T(8,128)(2,1)S(1)} %constant_dynamic-update-slice_fusion.a0), channel_id=1, source_target_pairs={{0,96},{32,0},{64,32},{96,64},{1,97},{33,1},{65,33},{97,65},{2,98}... | collective-permute-start | bytes 1425416 | tf_op jit(solution)/shard_map/ppermute | solution.py:1539
  463.2 21.3 %collective-permute-start.26 = (bf16[1856,128]{1,0:T(8,128)(2,1)S(1)}, bf16[1856,128]{1,0:T(8,128)(2,1)S(1)}, u32[]{:S(2)}, u32[]{:S(2)}) collective-permute-start(bf16[1856,128]{1,0:T(8,128)(2,1)S(1)} %constant_dynamic-update-slice_fusion.a0), channel_id=1, source_target_pairs={{0,64},{32,96},{64,0},{96,32},{1,65},{33,97},{65,1},{97,33},{2,66}... | collective-permute-start | bytes 1425416 | tf_op jit(solution)/shard_map/ppermute | solution.py:1539
  463.8 31.5 %collective-permute-start.25 = (bf16[1856,128]{1,0:T(8,128)(2,1)S(1)}, bf16[1856,128]{1,0:T(8,128)(2,1)S(1)}, u32[]{:S(2)}, u32[]{:S(2)}) collective-permute-start(bf16[1856,128]{1,0:T(8,128)(2,1)S(1)} %constant_dynamic-update-slice_fusion.a0), channel_id=1, source_target_pairs={{0,32},{32,64},{64,96},{96,0},{1,33},{33,65},{65,97},{97,1},{2,34}... | collective-permute-start | bytes 1425416 | tf_op jit(solution)/shard_map/ppermute | solution.py:1539
  (87 other events, 820.5 us)
Sparse Core Ops, SparseCore 0:
  13.5 80.4 all-gather.4
  97.5 73.1 all-gather.6

commit v3 on v2

--- a/solution.py
+++ b/solution.py
@@ -1091,15 +1091,17 @@
         left = left - part.astype(F32)
 
 
-def spill_kernel(other, zi, places, a0, a1, a2, a3, b, *refs):
+def spill_kernel(other, zi, places, *refs):
+    parts, b, refs = refs[:8], refs[8], refs[9:]
     refs = refs[7:] if other else refs
     outs, (v6, v5, v4, v3, vs, v2, v1, fa, fb, ins, sem) = refs[:7], refs[7:]
     cin = []
-    for j, a in enumerate((a0, a1, a2, a3)):
+    for j, part in enumerate(parts):
+        first, n = (0, 224) if j < 4 else (224, 240)
         for k in range(4):
-            dst = fa.at[pl.ds(pl.multiple_of(places[4 * j + k] * 464, 16), 464), :]
-            cin.append(go(a.at[pl.ds(464 * k, 464), :], dst, ins.at[4 * j + k]))
-    last = go(b.at[:, pl.ds(0, 176), :], fb.reshape(16, 176, 128), ins.at[16])
+            row = pl.multiple_of(places[4 * j + k] * 464 + first, 16)
+            cin.append(go(part.at[pl.ds(n * k, n), :], fa.at[pl.ds(row, n), :], ins.at[4 * j + k]))
+    last = go(b.at[:, pl.ds(0, 176), :], fb.reshape(16, 176, 128), ins.at[32])
     c = 1 - zi[4] if other else zi[4]
     copies = []
     plan = (
@@ -1134,11 +1136,11 @@
         functools.partial(spill_kernel, other),
         name=name,
         out_shape=tuple(pltpu.HBM(d, F32) for d in GRADS),
-        in_specs=[SM, SM] + [ANY] * (5 + len(before)),
+        in_specs=[SM, SM] + [ANY] * (9 + len(before)),
         out_specs=tuple(ANY for _ in GRADS),
         scratch_shapes=[pltpu.VMEM((r // 2, c), F32) for r, c in GRADS]
-        + [pltpu.VMEM((7424, 128), BF), pltpu.VMEM((2816, 128), BF), sems(17), sems(8)],
-        input_output_aliases={7 + i: i for i in range(len(before))},
+        + [pltpu.VMEM((7424, 128), BF), pltpu.VMEM((2816, 128), BF), sems(33), sems(8)],
+        input_output_aliases={11 + i: i for i in range(len(before))},
         compiler_params=pltpu.CompilerParams(vmem_limit_bytes=50 * 1024 * 1024),
         cost_estimate=pl.CostEstimate(flops=0, bytes_accessed=8_000_000, transcendentals=0),
     )(zi, places, *srcs, *before)
@@ -1516,8 +1518,11 @@
         (),
         (0, 2_000_000),
     )
-    some = [some] + [lax.ppermute(some, "x", ring(4, k)) for k in (1, 2, 3)]
-    rest, *some = tie(rest, *some)
+    parts = [
+        [v] + [lax.ppermute(v, axis, ring(4, k)) for k in (1, 2, 3)]
+        for v, axis in ((some[:224], "x"), (some[224:], "y"))
+    ]
+    rest, *some = tie(rest, *parts[0], *parts[1])
     rest = launch(
         "slice_rest",
         functools.partial(slice_kernel, SPANS[1]),
@@ -1535,10 +1540,16 @@
         (2 * RIN * 512 * 256, 8_000_000),
     )
     rest, dimage_local, dimage_global = tie(rest, dimage_local, dimage_global)
-    some = jnp.concatenate(some)
-    some = [some] + [lax.ppermute(some, "y", ring(4, k)) for k in (1, 2, 3)]
+    some = [
+        w
+        for v, axis in ((jnp.concatenate(some[:4]), "y"), (jnp.concatenate(some[4:]), "x"))
+        for w in [v] + [lax.ppermute(v, axis, ring(4, k)) for k in (1, 2, 3)]
+    ]
     yi, xi = lax.axis_index("y"), lax.axis_index("x")
-    places = jnp.stack([(yi - j) % 4 * 4 + (xi - k) % 4 for j in range(4) for k in range(4)])
+    places = jnp.stack(
+        [(yi - j) % 4 * 4 + (xi - k) % 4 for j in range(4) for k in range(4)]
+        + [(yi - k) % 4 * 4 + (xi - j) % 4 for j in range(4) for k in range(4)]
+    )
     places = places.astype(jnp.int32)
     rest = spread(rest, PLANE, 16)
     rest, *some = tie(rest, *some)

time: 528 us -> 541 us (1.025)
  starting transfers between devices: 104 us -> 123 us
  waiting for transfers between devices: 151 us -> 135 us
  local copies, waits for them, and re-layouts: 22.4 us -> 29.3 us
    ppermute x6 -> x12, waiting for transfers between devices: 36.4 us -> 19.1 us  [body(): lax.ppermute(v, axis, ring(4, k))]
    ppermute x6 -> x12, starting transfers between devices: 7.78 us -> 15.6 us  [body(): lax.ppermute(v, axis, ring(4, k))]
    ppermute x11 -> x15, starting transfers between devices: 3.82 us -> 11.2 us  [swap(): return lax.ppermute(v, 'c', ring(2, 1))]
    unnamed x140 -> x157, local copies, waits for them, and re-layouts: 16.9 us -> 22.6 us
  transfers between devices with their start and end apart: 51 -> 61, of which waited for: 24 -> 26; matrix products, arithmetic and copies ran while one was open for 2% -> 3% of each run, Pallas kernels for 24% -> 23%
where the time goes in v3:
time: 541 us; the launch traced here: 532 us
  Pallas kernels  172 us (32%)
  waiting for transfers between devices  135 us (25%)
  starting transfers between devices  123 us (23%)
  blocking collectives  44.8 us (8%)
  local copies, waits for them, and re-layouts  29.3 us (5%)
  between operations  15.9 us (3%)
  other arithmetic  11.7 us (2%)
    pallas_call x29, Pallas kernels, launch(): pl.pallas_call(body, name=name, out_shape=tuple((pltpu.HBM(o.shape, o.dty...  160 us
    all_to_all x7, starting transfers between devices, tell(): return lax.all_to_all(v, BATCH, 0, 0)  37.3 us
    all_to_all x5, waiting for transfers between devices, spread(): return lax.all_to_all(jnp.broadcast_to(v[None], (n,) + v.shape), axes, 0, 0)  36.6 us
    ppermute x4, waiting for transfers between devices, around(): right = [lax.ppermute(v, 'z', ring(4, 3)) for v in parts]  27.3 us
    all_to_all x5, starting transfers between devices, spread(): return lax.all_to_all(jnp.broadcast_to(v[None], (n,) + v.shape), axes, 0, 0)  25.9 us
    all_to_all x1, blocking collectives, spread(): return lax.all_to_all(jnp.broadcast_to(v[None], (n,) + v.shape), axes, 0, 0)  23 us
    unnamed x157, local copies, waits for them, and re-layouts  22.6 us
    all_to_all x1, blocking collectives, tell(): return lax.all_to_all(v, BATCH, 0, 0)  21.8 us
  transfers between devices with their start and end apart: 61, of which 26 were waited for; matrix products, arithmetic and copies ran while one was open for 3% of the time, Pallas kernels for 23%

profile of v3, /device:TPU:1, one launch (start us, length us, event | category | flops | bytes accessed | tf_op | source)
XLA Modules:
  0.0 532.0 jit_solution(14422213457051131123)
XLA Ops:
  21.5 27.3 %collective-permute-done.2.refs_2_.t1 = bf16[1312,256]{1,0:T(8,128)(2,1)S(1)} collective-permute-done((bf16[1312,256]{1,0:T(8,128)(2,1)S(1)}, bf16[1312,256]{1,0:T(8,128)(2,1)S(1)}, u32[]{:S(2)}, u32[]{:S(2)}) %collective-permute-start.2) | collective-permute-done | bytes 671776 | tf_op jit(solution)/shard_map/ppermute | solution.py:1185
  58.9 12.3 %all-to-all-done = bf16[4,96,128]{2,1,0:T(8,128)(2,1)} async-done(((bf16[4,96,128]{2,1,0:T(8,128)(2,1)}), bf16[4,96,128]{2,1,0:T(8,128)(2,1)}, u32[]{:S(2)}, u32[]{:S(2)}) %all-to-all-start) | async-done | bytes 98336 | tf_op jit(solution)/shard_map/all_to_all | solution.py:1154
  73.8 8.1 %reduce_one.1 = (f32[2144,512]{1,0:T(8,128)}, f32[32,4,512]{2,1,0:T(4,128)}) custom-call(s32[5]{0:T(128)S(1)} %stack.117.zi, bf16[1312,256]{1,0:T(8,128)(2,1)} %copy-done, bf16[1344,256]{1,0:T(8,128)(2,1)} %copy-done.10, bf16[1312,256]{1,0:T(8,128)(2,1)} %copy-done.2, bf16[1344,256]{1,0:T(8,128)(2,1)} %copy-done.61, bf16[1312,256]{1,0:T(8,128)(2,1)} %copy-done.6, ...), custom_call_target="tpu_custom_call" | custom-call | flops 2248146944 | bytes 10000000 | tf_op jit(solution)/shard_map/reduce_one/pallas_call | solution.py:43
  81.8 21.8 %all_to_all.80.st = f32[32,4,512]{2,1,0:T(4,128)S(1)} all-to-all(f32[32,4,512]{2,1,0:T(4,128)} %get-tuple-element.195), channel_id=1, replica_groups=mesh['y'=4,'x'=4,'c'=2,'z'=4] {'y','x','c'}, dimensions={0} | all-to-all | bytes 524288 | tf_op jit(solution)/shard_map/all_to_all | solution.py:1163
  103.6 8.6 %spatial_one.1 = (bf16[544,4608]{1,0:T(8,128)(2,1)}, f32[544,512]{1,0:T(8,128)}, f32[32,4,512]{2,1,0:T(4,128)}, f32[4,512]{1,0:T(4,128)S(1)}) custom-call(f32[32,4,512]{2,1,0:T(4,128)S(1)} %all_to_all.80.st, f32[4,32,128]{2,1,0:T(8,128)S(1)} %convert_add_fusion.norms, f32[2144,512]{1,0:T(8,128)} %get-tuple-element.196.z1, bf16[32,4,400,128]{3,2,1,0:T(8,128)(2,1)} %bitcast.68), custom_call_target="tpu_custom_call" | custom-call | flops 40000000000 | bytes 20000000 | tf_op jit(solution)/shard_map/spatial_one/pallas_call | solution.py:43
  116.3 9.1 %shortcut.2 = (bf16[544,1024]{1,0:T(8,128)(2,1)}, f32[544,2048]{1,0:T(8,128)}, f32[4,2048]{1,0:T(4,128)S(1)}) custom-call(s32[5]{0:T(128)S(1)} %stack.117.zi, bf16[1312,256]{1,0:T(8,128)(2,1)} %copy-done, bf16[1344,256]{1,0:T(8,128)(2,1)} %copy-done.10, bf16[1312,256]{1,0:T(8,128)(2,1)} %copy-done.2, bf16[1344,256]{1,0:T(8,128)(2,1)} %copy-done.61, ...), custom_call_target="tpu_custom_call" | custom-call | flops 2281701376 | bytes 14000000 | tf_op jit(solution)/shard_map/shortcut/pallas_call | solution.py:43
  132.2 23.0 %all_to_all.81.st3 = f32[16,8,2048]{2,1,0:T(8,128)S(1)} all-to-all(f32[16,8,2048]{2,1,0:T(8,128)S(1)} %broadcast_in_dim.15), channel_id=1, replica_groups=mesh['y'=4,'x'=4,'c'=2,'z'=4] {'y','x'}, dimensions={0} | all-to-all | bytes 2097152 | tf_op jit(solution)/shard_map/all_to_all | solution.py:1154
  155.2 10.6 %reduce_two.2 = (f32[544,2048]{1,0:T(8,128)}, bf16[544,2048]{1,0:T(8,128)(2,1)}, f32[544,512]{1,0:T(8,128)}, f32[32,4,512]{2,1,0:T(4,128)}, f32[4,2048]{1,0:T(4,128)S(1)}, /*index=5*/f32[4,2048]{1,0:T(4,128)S(1)}) custom-call(f32[16,8,2048]{2,1,0:T(8,128)S(1)} %all_to_all.81.st3, f32[4,32,128]{2,1,0:T(8,128)S(1)} %convert_add_fusion.norms, ...), custom_call_target="tpu_custom_call" | custom-call | flops 1140850688 | bytes 20000000 | tf_op jit(solution)/shard_map/reduce_two/pallas_call | solution.py:43
  165.8 6.7 %all-to-all-start.4 = ((f32[32,4,512]{2,1,0:T(4,128)}), f32[32,4,512]{2,1,0:T(4,128)}, u32[]{:S(2)}, u32[]{:S(2)}) async-start(f32[32,4,512]{2,1,0:T(4,128)} %get-tuple-element.210), calls=%async_computation.4 | async-start | bytes 524288 | tf_op jit(solution)/shard_map/all_to_all | solution.py:1163
  181.6 8.4 %spatial_two.1 = (bf16[544,4608]{1,0:T(8,128)(2,1)}, f32[544,512]{1,0:T(8,128)}, f32[32,4,512]{2,1,0:T(4,128)}, f32[4,512]{1,0:T(4,128)S(1)}) custom-call(f32[32,4,512]{2,1,0:T(4,128)} %all-to-all-done.4.st, f32[4,32,128]{2,1,0:T(8,128)S(1)} %convert_add_fusion.norms, f32[544,512]{1,0:T(8,128)} %get-tuple-element.212.z4, bf16[32,4,208,128]{3,2,1,0:T(8,128)(2,1)} %bitcast.76), custom_call_target="tpu_custom_call" | custom-call | flops 2566914048 | bytes 20000000 | tf_op jit(solution)/shard_map/spatial_two/pallas_call | solution.py:43
  203.9 5.4 %expand_two.2 = (bf16[544,512]{1,0:T(8,128)(2,1)}, f32[544,2048]{1,0:T(8,128)}, f32[4,2048]{1,0:T(4,128)S(1)}, f32[4,512]{1,0:T(4,128)S(1)}) custom-call(f32[32,4,512]{2,1,0:T(4,128)S(1)} %all-to-all-done.5.st, f32[4,32,128]{2,1,0:T(8,128)S(1)} %convert_add_fusion.norms, f32[544,512]{1,0:T(8,128)} %get-tuple-element.215.z.z5, bf16[32,4,208,128]{3,2,1,0:T(8,128)(2,1)} %bitcast.77), custom_call_target="tpu_custom_call" | custom-call | flops 1140850688 | bytes 9000000 | tf_op jit(solution)/shard_map/expand_two/pallas_call | solution.py:43
  212.0 6.8 %all-to-all-start.6 = ((f32[16,4,2048]{2,1,0:T(4,128)}), f32[16,4,2048]{2,1,0:T(4,128)S(1)}, u32[]{:S(2)}, u32[]{:S(2)}) async-start(f32[16,4,2048]{2,1,0:T(4,128)} %broadcast_in_dim.16), calls=%async_computation.6 | async-start | bytes 1048576 | tf_op jit(solution)/shard_map/all_to_all | solution.py:1154
  221.9 5.4 %collective-permute-done.13.refs_5_ = bf16[272,512]{1,0:T(8,128)(2,1)S(1)} collective-permute-done((bf16[272,512]{1,0:T(8,128)(2,1)S(1)}, bf16[272,512]{1,0:T(8,128)(2,1)S(1)}, u32[]{:S(2)}, u32[]{:S(2)}) %collective-permute-start.13) | collective-permute-done | bytes 278560 | tf_op jit(solution)/shard_map/ppermute | solution.py:1187
  231.1 8.0 %output.1 = (f32[544,512]{1,0:T(8,128)}, f32[544,2048]{1,0:T(8,128)}, f32[4,2048]{1,0:T(4,128)S(1)}, f32[4,2048]{1,0:T(4,128)S(1)}) custom-call(s32[5]{0:T(128)S(1)} %stack.117.zi, f32[16,4,2048]{2,1,0:T(4,128)S(1)} %all-to-all-done.6.st, f32[4,32,128]{2,1,0:T(8,128)S(1)} %convert_add_fusion.norms, f32[544,2048]{1,0:T(8,128)} %get-tuple-element.217.z6, ...), custom_call_target="tpu_custom_call" | custom-call | bytes 20000000 | tf_op jit(solution)/shard_map/output/pallas_call | solution.py:43
  242.8 6.7 %all-to-all-start.7 = ((f32[16,4,2048]{2,1,0:T(4,128)}), f32[16,4,2048]{2,1,0:T(4,128)S(1)}, u32[]{:S(2)}, u32[]{:S(2)}) async-start(f32[16,4,2048]{2,1,0:T(4,128)} %broadcast_in_dim.17), calls=%async_computation.7 | async-start | bytes 1048576 | tf_op jit(solution)/shard_map/all_to_all | solution.py:1154
  250.7 9.5 %all-to-all-done.7.stb = f32[16,4,2048]{2,1,0:T(4,128)S(1)} async-done(((f32[16,4,2048]{2,1,0:T(4,128)}), f32[16,4,2048]{2,1,0:T(4,128)S(1)}, u32[]{:S(2)}, u32[]{:S(2)}) %all-to-all-start.7) | async-done | bytes 524320 | tf_op jit(solution)/shard_map/all_to_all | solution.py:1154
  260.2 10.0 %back_expand_two.1 = (bf16[544,512]{1,0:T(8,128)(2,1)S(1)}, f32[544,512]{1,0:T(8,128)}, f32[32,4,512]{2,1,0:T(4,128)}, f32[2,2048]{1,0:T(2,128)S(1)}) custom-call(s32[5]{0:T(128)S(1)} %stack.117.zi, f32[16,4,2048]{2,1,0:T(4,128)S(1)} %all-to-all-done.7.stb, f32[4,32,128]{2,1,0:T(8,128)S(1)} %convert_add_fusion.norms, f32[4,2048]{1,0:T(4,128)S(1)} %get-tuple-element.232.sum6, ...), custom_call_target="tpu_custom_call" | custom-call | flops 1140850688 | bytes 14000000 | tf_op jit(solution)/shard_map/back_expand_two/pallas_call | solution.py:43
  277.4 7.7 %all-to-all-done.8.stb = f32[32,4,512]{2,1,0:T(4,128)S(1)} async-done(((f32[32,4,512]{2,1,0:T(4,128)}), f32[32,4,512]{2,1,0:T(4,128)S(1)}, u32[]{:S(2)}, u32[]{:S(2)}) %all-to-all-start.8) | async-done | bytes 262176 | tf_op jit(solution)/shard_map/all_to_all | solution.py:1163
  285.1 9.0 %back_spatial_two.1 = (bf16[544,128]{1,0:T(8,128)(2,1)S(1)}, f32[544,512]{1,0:T(8,128)}, f32[32,4,512]{2,1,0:T(4,128)}, f32[2,512]{1,0:T(2,128)S(1)}) custom-call(s32[5]{0:T(128)S(1)} %stack.117.zi, f32[32,4,512]{2,1,0:T(4,128)S(1)} %all-to-all-done.8.stb, f32[4,32,128]{2,1,0:T(8,128)S(1)} %convert_add_fusion.norms, f32[4,512]{1,0:T(4,128)S(1)} %get-tuple-element.233.sum5, ...), custom_call_target="tpu_custom_call" | custom-call | flops 2566914048 | bytes 10000000 | tf_op jit(solution)/shard_map/back_spatial_two/pallas_call | solution.py:43
  307.7 11.2 %back_reduce_two.1 = (bf16[544,128]{1,0:T(8,128)(2,1)S(1)}, f32[544,2048]{1,0:T(8,128)}, f32[6,2048]{1,0:T(8,128)S(1)}, f32[2,512]{1,0:T(2,128)S(1)}) custom-call(s32[5]{0:T(128)S(1)} %stack.117.zi, f32[32,4,512]{2,1,0:T(4,128)S(1)} %all-to-all-done.9.stb, f32[4,32,128]{2,1,0:T(8,128)S(1)} %convert_add_fusion.norms, f32[4,512]{1,0:T(4,128)S(1)} %get-tuple-element.241.sum4, ...), custom_call_target="tpu_custom_call" | custom-call | flops 1140850688 | bytes 22000000 | tf_op jit(solution)/shard_map/back_reduce_two/pallas_call | solution.py:43
  328.7 14.8 %all-to-all-done.10.stb = f32[16,6,2048]{2,1,0:T(8,128)S(1)} async-done(((f32[16,6,2048]{2,1,0:T(8,128)}), f32[16,6,2048]{2,1,0:T(8,128)S(1)}, u32[]{:S(2)}, u32[]{:S(2)}) %all-to-all-start.10) | async-done | bytes 786464 | tf_op jit(solution)/shard_map/all_to_all | solution.py:1154
  344.3 10.0 %back_expand_one.1 = (bf16[544,512]{1,0:T(8,128)(2,1)S(1)}, f32[544,512]{1,0:T(8,128)}, f32[32,4,512]{2,1,0:T(4,128)}, f32[2,2048]{1,0:T(2,128)S(1)}, f32[4,2048]{1,0:T(4,128)S(1)}) custom-call(s32[5]{0:T(128)S(1)} %stack.117.zi, f32[16,6,2048]{2,1,0:T(8,128)S(1)} %all-to-all-done.10.stb, f32[4,32,128]{2,1,0:T(8,128)S(1)} %convert_add_fusion.norms, ...), custom_call_target="tpu_custom_call" | custom-call | flops 1140850688 | bytes 16000000 | tf_op jit(solution)/shard_map/back_expand_one/pallas_call | solution.py:43
  362.4 5.4 %back_shortcut.1 = (bf16[544,512]{1,0:T(8,128)(2,1)S(1)}, f32[544,256]{1,0:T(8,128)S(1)}, f32[2,2048]{1,0:T(2,128)S(1)}) custom-call(s32[5]{0:T(128)S(1)} %stack.117.zi, f32[4,32,128]{2,1,0:T(8,128)S(1)} %convert_add_fusion.norms, f32[4,2048]{1,0:T(4,128)S(1)} %get-tuple-element.261.gsum, f32[4,2048]{1,0:T(4,128)S(1)} %get-tuple-element.250.sums, ...), custom_call_target="tpu_custom_call" | custom-call | flops 570425344 | bytes 10000000 | tf_op jit(solution)/shard_map/back_shortcut/pallas_call | solution.py:43
  375.0 13.7 %back_spatial_one.1 = (bf16[544,128]{1,0:T(8,128)(2,1)S(1)}, f32[2144,512]{1,0:T(8,128)}, f32[32,4,512]{2,1,0:T(4,128)}, f32[2,512]{1,0:T(2,128)S(1)}) custom-call(s32[5]{0:T(128)S(1)} %stack.117.zi, f32[32,4,512]{2,1,0:T(4,128)S(1)} %all-to-all-done.11.stb, f32[4,32,128]{2,1,0:T(8,128)S(1)} %convert_add_fusion.norms, f32[4,512]{1,0:T(4,128)S(1)} %get-tuple-element.258.sum2, ...), custom_call_target="tpu_custom_call" | custom-call | flops 2566914048 | bytes 20000000 | tf_op jit(solution)/shard_map/back_spatial_one/pallas_call | solution.py:43
  389.3 7.5 %all-to-all-start.12 = ((f32[32,4,512]{2,1,0:T(4,128)}), f32[32,4,512]{2,1,0:T(4,128)S(1)}, u32[]{:S(2)}, u32[]{:S(2)}) async-start(f32[32,4,512]{2,1,0:T(4,128)} %get-tuple-element.272), calls=%async_computation.12 | async-start | bytes 524288 | tf_op jit(solution)/shard_map/all_to_all | solution.py:1163
  412.8 6.1 %back_reduce_one.1 = (bf16[2144,128]{1,0:T(8,128)(2,1)S(1)}, bf16[2144,512]{1,0:T(8,128)(2,1)}, f32[2,512]{1,0:T(2,128)S(1)}) custom-call(s32[5]{0:T(128)S(1)} %stack.117.zi, f32[32,4,512]{2,1,0:T(4,128)S(1)} %copy-done.20, f32[4,32,128]{2,1,0:T(8,128)S(1)} %convert_add_fusion.norms, f32[4,512]{1,0:T(4,128)S(1)} %get-tuple-element.270.sum1, ...), custom_call_target="tpu_custom_call" | custom-call | bytes 12000000 | tf_op jit(solution)/shard_map/back_reduce_one/pallas_call | solution.py:43
  425.5 14.6 %all-to-all-done.13.src = bf16[16,464,128]{2,1,0:T(8,128)(2,1)S(1)} async-done(((bf16[16,464,128]{2,1,0:T(8,128)(2,1)}), bf16[16,464,128]{2,1,0:T(8,128)(2,1)S(1)}, u32[]{:S(2)}, u32[]{:S(2)}) %all-to-all-start.13) | async-done | bytes 1900576 | tf_op jit(solution)/shard_map/all_to_all | solution.py:1485
  474.5 9.3 %collective-permute-done.30.refs_3_ = bf16[896,128]{1,0:T(8,128)(2,1)S(1)} collective-permute-done((bf16[896,128]{1,0:T(8,128)(2,1)S(1)}, bf16[896,128]{1,0:T(8,128)(2,1)S(1)}, u32[]{:S(2)}, u32[]{:S(2)}) %collective-permute-start.30) | collective-permute-done | bytes 229408 | tf_op jit(solution)/shard_map/ppermute | solution.py:1546
  485.2 6.0 %collective-permute-done.28.refs_1_ = bf16[896,128]{1,0:T(8,128)(2,1)S(1)} collective-permute-done((bf16[896,128]{1,0:T(8,128)(2,1)S(1)}, bf16[896,128]{1,0:T(8,128)(2,1)S(1)}, u32[]{:S(2)}, u32[]{:S(2)}) %collective-permute-start.28) | collective-permute-done | bytes 229408 | tf_op jit(solution)/shard_map/ppermute | solution.py:1546
  491.9 6.1 %collective-permute-start.42 = (bf16[16,224,128]{2,1,0:T(8,128)(2,1)S(1)}, bf16[16,224,128]{2,1,0:T(8,128)(2,1)S(1)}, u32[]{:S(2)}, u32[]{:S(2)}) collective-permute-start(bf16[16,224,128]{2,1,0:T(8,128)(2,1)S(1)} %all-to-all-done.15.refs_8_), channel_id=1, source_target_pairs={{0,4},{4,0},{1,5},{5,1},{2,6},{6,2},{3,7},{7,3},{8,12},{12,8},{9,1... | collective-permute-start | bytes 2752520 | tf_op jit(solution)/shard_map/ppermute | solution.py:1180
  511.5 6.0 %grads_kept.1 = (f32[512,512]{1,0:T(8,128)}, f32[4608,128]{1,0:T(8,128)}, f32[2048,128]{1,0:T(8,128)}, f32[512,512]{1,0:T(8,128)}, f32[1024,512]{1,0:T(8,128)}, ...) custom-call(s32[5]{0:T(128)S(1)} %stack.117.zi, s32[32]{0:T(128)S(1)} %copy-done.49, ...), custom_call_target="tpu_custom_call" | custom-call | bytes 8000000 | tf_op jit(solution)/shard_map/grads_kept/pallas_call | solution.py:1135
  517.7 6.5 %grads_given.1 = (f32[512,512]{1,0:T(8,128)}, f32[4608,128]{1,0:T(8,128)}, f32[2048,128]{1,0:T(8,128)}, f32[512,512]{1,0:T(8,128)}, f32[1024,512]{1,0:T(8,128)},...) custom-call(s32[5]{0:T(128)S(1)} %stack.117.zi, ...), custom_call_target="tpu_custom_call", output_to_operand_aliasing={{0}: (11, {}), {1}: (12, {}), {2}: (13, {}), {3}: (14, {}),... | custom-call | bytes 8000000 | tf_op jit(solution)/shard_map/grads_given/pallas_call | solution.py:1135
  (327 shorter events, 194.5 us)
Async XLA Ops:
  7.2 96.5 %all-gather.5.cloned.1.call-start = ((), (), s32[]{:S(2)}) async-start(), calls=%async_computation.16 | async-start | bytes 13209600 | tf_op jit(solution)/shard_map/all_gather | solution.py:1248
  13.3 168.3 %all-gather.7.cloned.1.call-start = ((), (), s32[]{:S(2)}) async-start(), calls=%async_computation.17 | async-start | bytes 6868992 | tf_op jit(solution)/shard_map/all_gather | solution.py:1249
  14.1 37.3 %collective-permute-start.3 = (bf16[1344,256]{1,0:T(8,128)(2,1)S(1)}, bf16[1344,256]{1,0:T(8,128)(2,1)S(1)}, u32[]{:S(2)}, u32[]{:S(2)}) collective-permute-start(bf16[1344,256]{1,0:T(8,128)(2,1)S(1)} %get-tuple-element.184.refs_1_), channel_id=1, source_target_pairs={{0,3},{1,0},{2,1},{3,2},{4,7},{5,4},{6,5},{7,6},{8,11},{9,8},{10,9... | collective-permute-start | bytes 2064392 | tf_op jit(solution)/shard_map/ppermute | solution.py:1185
  18.8 32.7 %collective-permute-start.1 = (bf16[1344,256]{1,0:T(8,128)(2,1)S(1)}, bf16[1344,256]{1,0:T(8,128)(2,1)}, u32[]{:S(2)}, u32[]{:S(2)}) collective-permute-start(bf16[1344,256]{1,0:T(8,128)(2,1)S(1)} %get-tuple-element.184.refs_1_), channel_id=1, source_target_pairs={{0,1},{1,2},{2,3},{3,0},{4,5},{5,6},{6,7},{7,4},{8,9},{9,10},{10,1... | collective-permute-start | bytes 2064392 | tf_op jit(solution)/shard_map/ppermute | solution.py:1184
  18.8 30.0 %collective-permute-start.2 = (bf16[1312,256]{1,0:T(8,128)(2,1)S(1)}, bf16[1312,256]{1,0:T(8,128)(2,1)S(1)}, u32[]{:S(2)}, u32[]{:S(2)}) collective-permute-start(bf16[1312,256]{1,0:T(8,128)(2,1)S(1)} %get-tuple-element.182.refs_0_.t0), channel_id=1, source_target_pairs={{0,3},{1,0},{2,1},{3,2},{4,7},{5,4},{6,5},{7,6},{8,11},{9,8},{10,9... | collective-permute-start | bytes 2015240 | tf_op jit(solution)/shard_map/ppermute | solution.py:1185
  21.4 30.0 %collective-permute-start = (bf16[1312,256]{1,0:T(8,128)(2,1)S(1)}, bf16[1312,256]{1,0:T(8,128)(2,1)S(1)}, u32[]{:S(2)}, u32[]{:S(2)}) collective-permute-start(bf16[1312,256]{1,0:T(8,128)(2,1)S(1)} %get-tuple-element.182.refs_0_.t0), channel_id=1, source_target_pairs={{0,1},{1,2},{2,3},{3,0},{4,5},{5,6},{6,7},{7,4},{8,9},{9,10},{10,1... | collective-permute-start | bytes 2015240 | tf_op jit(solution)/shard_map/ppermute | solution.py:1184
  51.4 20.6 %collective-permute-start.4 = (bf16[1312,256]{1,0:T(8,128)(2,1)S(1)}, bf16[1312,256]{1,0:T(8,128)(2,1)S(1)}, u32[]{:S(2)}, u32[]{:S(2)}) collective-permute-start(bf16[1312,256]{1,0:T(8,128)(2,1)S(1)} %collective-permute-done.refs_6_.t3), channel_id=1, source_target_pairs={{0,1},{1,2},{2,3},{3,0},{4,5},{5,6},{6,7},{7,4},{8,9},{9,10},{10,1... | collective-permute-start | bytes 2015240 | tf_op jit(solution)/shard_map/ppermute | solution.py:1187
  51.5 20.5 %collective-permute-start.5 = (bf16[1344,256]{1,0:T(8,128)(2,1)S(1)}, bf16[1344,256]{1,0:T(8,128)(2,1)S(1)}, u32[]{:S(2)}, u32[]{:S(2)}) collective-permute-start(bf16[1344,256]{1,0:T(8,128)(2,1)S(1)} %collective-permute-done.3.refs_3_), channel_id=1, source_target_pairs={{0,3},{1,0},{2,1},{3,2},{4,7},{5,4},{6,5},{7,6},{8,11},{9,8},{10,9... | collective-permute-start | bytes 2064392 | tf_op jit(solution)/shard_map/ppermute | solution.py:1187
  54.9 16.3 %all-to-all-start = ((bf16[4,96,128]{2,1,0:T(8,128)(2,1)}), bf16[4,96,128]{2,1,0:T(8,128)(2,1)}, u32[]{:S(2)}, u32[]{:S(2)}) async-start(bf16[4,96,128]{2,1,0:T(8,128)(2,1)} %broadcast_in_dim.14), calls=%async_computation | async-start | bytes 196608 | tf_op jit(solution)/shard_map/all_to_all | solution.py:1154
  165.8 15.8 %all-to-all-start.4 = ((f32[32,4,512]{2,1,0:T(4,128)}), f32[32,4,512]{2,1,0:T(4,128)}, u32[]{:S(2)}, u32[]{:S(2)}) async-start(f32[32,4,512]{2,1,0:T(4,128)} %get-tuple-element.210), calls=%async_computation.4 | async-start | bytes 524288 | tf_op jit(solution)/shard_map/all_to_all | solution.py:1163
  195.5 23.3 %collective-permute-start.10 = (bf16[272,512]{1,0:T(8,128)(2,1)S(1)}, bf16[272,512]{1,0:T(8,128)(2,1)S(1)}, u32[]{:S(2)}, u32[]{:S(2)}) collective-permute-start(bf16[272,512]{1,0:T(8,128)(2,1)S(1)} %get-tuple-element.219.refs_0_), channel_id=1, source_target_pairs={{0,3},{1,0},{2,1},{3,2},{4,7},{5,4},{6,5},{7,6},{8,11},{9,8},{10,9... | collective-permute-start | bytes 835592 | tf_op jit(solution)/shard_map/ppermute | solution.py:1185
  200.5 18.3 %collective-permute-start.8 = (bf16[272,512]{1,0:T(8,128)(2,1)S(1)}, bf16[272,512]{1,0:T(8,128)(2,1)S(1)}, u32[]{:S(2)}, u32[]{:S(2)}) collective-permute-start(bf16[272,512]{1,0:T(8,128)(2,1)S(1)} %get-tuple-element.219.refs_0_), channel_id=1, source_target_pairs={{0,1},{1,2},{2,3},{3,0},{4,5},{5,6},{6,7},{7,4},{8,9},{9,10},{10,1... | collective-permute-start | bytes 835592 | tf_op jit(solution)/shard_map/ppermute | solution.py:1184
  200.5 18.3 %collective-permute-start.11 = (bf16[272,512]{1,0:T(8,128)(2,1)S(1)}, bf16[272,512]{1,0:T(8,128)(2,1)S(1)}, u32[]{:S(2)}, u32[]{:S(2)}) collective-permute-start(bf16[272,512]{1,0:T(8,128)(2,1)S(1)} %get-tuple-element.220.refs_1_), channel_id=1, source_target_pairs={{0,3},{1,0},{2,1},{3,2},{4,7},{5,4},{6,5},{7,6},{8,11},{9,8},{10,9... | collective-permute-start | bytes 835592 | tf_op jit(solution)/shard_map/ppermute | solution.py:1185
  203.6 15.3 %collective-permute-start.9 = (bf16[272,512]{1,0:T(8,128)(2,1)S(1)}, bf16[272,512]{1,0:T(8,128)(2,1)S(1)}, u32[]{:S(2)}, u32[]{:S(2)}) collective-permute-start(bf16[272,512]{1,0:T(8,128)(2,1)S(1)} %get-tuple-element.220.refs_1_), channel_id=1, source_target_pairs={{0,1},{1,2},{2,3},{3,0},{4,5},{5,6},{6,7},{7,4},{8,9},{9,10},{10,1... | collective-permute-start | bytes 835592 | tf_op jit(solution)/shard_map/ppermute | solution.py:1184
  212.0 18.4 %all-to-all-start.6 = ((f32[16,4,2048]{2,1,0:T(4,128)}), f32[16,4,2048]{2,1,0:T(4,128)S(1)}, u32[]{:S(2)}, u32[]{:S(2)}) async-start(f32[16,4,2048]{2,1,0:T(4,128)} %broadcast_in_dim.16), calls=%async_computation.6 | async-start | bytes 1048576 | tf_op jit(solution)/shard_map/all_to_all | solution.py:1154
  242.8 17.4 %all-to-all-start.7 = ((f32[16,4,2048]{2,1,0:T(4,128)}), f32[16,4,2048]{2,1,0:T(4,128)S(1)}, u32[]{:S(2)}, u32[]{:S(2)}) async-start(f32[16,4,2048]{2,1,0:T(4,128)} %broadcast_in_dim.17), calls=%async_computation.7 | async-start | bytes 1048576 | tf_op jit(solution)/shard_map/all_to_all | solution.py:1154
  321.8 21.7 %all-to-all-start.10 = ((f32[16,6,2048]{2,1,0:T(8,128)}), f32[16,6,2048]{2,1,0:T(8,128)S(1)}, u32[]{:S(2)}, u32[]{:S(2)}) async-start(f32[16,6,2048]{2,1,0:T(8,128)} %broadcast_in_dim.18), calls=%async_computation.10 | async-start | bytes 2097152 | tf_op jit(solution)/shard_map/all_to_all | solution.py:1154
  325.5 35.1 %collective-permute-start.16 = (bf16[1024,128]{1,0:T(8,128)(2,1)}, bf16[1024,128]{1,0:T(8,128)(2,1)}, u32[]{:S(2)}, u32[]{:S(2)}) collective-permute-start(bf16[1024,128]{1,0:T(8,128)(2,1)} %copy-done.58), channel_id=1, source_target_pairs={{0,4},{4,0},{1,5},{5,1},{2,6},{6,2},{3,7},{7,3},{8,12},{12,8},{9,1... | collective-permute-start | bytes 786440 | tf_op jit(solution)/shard_map/ppermute | solution.py:1180
  325.8 46.8 %collective-permute-start.17 = (bf16[2304,128]{1,0:T(8,128)(2,1)}, bf16[2304,128]{1,0:T(8,128)(2,1)}, u32[]{:S(2)}, u32[]{:S(2)}) collective-permute-start(bf16[2304,128]{1,0:T(8,128)(2,1)} %copy-done.54), channel_id=1, source_target_pairs={{0,4},{4,0},{1,5},{5,1},{2,6},{6,2},{3,7},{7,3},{8,12},{12,8},{9,1... | collective-permute-start | bytes 1769480 | tf_op jit(solution)/shard_map/ppermute | solution.py:1180
  355.7 16.6 %all-to-all-start.11 = ((f32[32,4,512]{2,1,0:T(4,128)}), f32[32,4,512]{2,1,0:T(4,128)S(1)}, u32[]{:S(2)}, u32[]{:S(2)}) async-start(f32[32,4,512]{2,1,0:T(4,128)} %get-tuple-element.260), calls=%async_computation.11 | async-start | bytes 524288 | tf_op jit(solution)/shard_map/all_to_all | solution.py:1163
  372.3 28.3 %collective-permute-start.19 = (bf16[3072,128]{1,0:T(8,128)(2,1)S(1)}, bf16[3072,128]{1,0:T(8,128)(2,1)}, u32[]{:S(2)}, u32[]{:S(2)}) collective-permute-start(bf16[3072,128]{1,0:T(8,128)(2,1)S(1)} %get-tuple-element.280), channel_id=1, source_target_pairs={{0,4},{4,0},{1,5},{5,1},{2,6},{6,2},{3,7},{7,3},{8,12},{12,8},{9,1... | collective-permute-start | bytes 2359304 | tf_op jit(solution)/shard_map/ppermute | solution.py:1180
  374.7 25.8 %collective-permute-start.18 = (bf16[1024,128]{1,0:T(8,128)(2,1)S(1)}, bf16[1024,128]{1,0:T(8,128)(2,1)S(1)}, u32[]{:S(2)}, u32[]{:S(2)}) collective-permute-start(bf16[1024,128]{1,0:T(8,128)(2,1)S(1)} %copy-done.60), channel_id=1, source_target_pairs={{0,4},{4,0},{1,5},{5,1},{2,6},{6,2},{3,7},{7,3},{8,12},{12,8},{9,1... | collective-permute-start | bytes 786440 | tf_op jit(solution)/shard_map/ppermute | solution.py:1180
  389.3 16.4 %all-to-all-start.12 = ((f32[32,4,512]{2,1,0:T(4,128)}), f32[32,4,512]{2,1,0:T(4,128)S(1)}, u32[]{:S(2)}, u32[]{:S(2)}) async-start(f32[32,4,512]{2,1,0:T(4,128)} %get-tuple-element.272), calls=%async_computation.12 | async-start | bytes 524288 | tf_op jit(solution)/shard_map/all_to_all | solution.py:1163
  406.4 33.7 %all-to-all-start.13 = ((bf16[16,464,128]{2,1,0:T(8,128)(2,1)}), bf16[16,464,128]{2,1,0:T(8,128)(2,1)S(1)}, u32[]{:S(2)}, u32[]{:S(2)}) async-start(bf16[16,464,128]{2,1,0:T(8,128)(2,1)} %bitcast.80), calls=%async_computation.13 | async-start | bytes 3801088 | tf_op jit(solution)/shard_map/all_to_all | solution.py:1485
  440.1 21.4 %all-to-all-start.14 = ((bf16[16,176,128]{2,1,0:T(8,128)(2,1)}), bf16[16,176,128]{2,1,0:T(8,128)(2,1)S(1)}, u32[]{:S(2)}, u32[]{:S(2)}) async-start(bf16[16,176,128]{2,1,0:T(8,128)(2,1)} %bitcast.83), calls=%async_computation.14 | async-start | bytes 1441792 | tf_op jit(solution)/shard_map/all_to_all | solution.py:1511
  462.7 29.2 %all-to-all-start.15 = ((bf16[16,224,128]{2,1,0:T(8,128)(2,1)}), bf16[16,224,128]{2,1,0:T(8,128)(2,1)S(1)}, u32[]{:S(2)}, u32[]{:S(2)}) async-start(bf16[16,224,128]{2,1,0:T(8,128)(2,1)} %broadcast_in_dim.19), calls=%async_computation.15 | async-start | bytes 1835008 | tf_op jit(solution)/shard_map/all_to_all | solution.py:1154
  467.6 16.2 %collective-permute-start.30 = (bf16[896,128]{1,0:T(8,128)(2,1)S(1)}, bf16[896,128]{1,0:T(8,128)(2,1)S(1)}, u32[]{:S(2)}, u32[]{:S(2)}) collective-permute-start(bf16[896,128]{1,0:T(8,128)(2,1)S(1)} %constant_dynamic-update-slice_fusion.refs_0_), channel_id=1, source_target_pairs={{0,96},{32,0},{64,32},{96,64},{1,97},{33,1},{65,33},{97,65},{2,98}... | collective-permute-start | bytes 688136 | tf_op jit(solution)/shard_map/ppermute | solution.py:1546
  470.3 20.9 %collective-permute-start.33 = (bf16[960,128]{1,0:T(8,128)(2,1)S(1)}, bf16[960,128]{1,0:T(8,128)(2,1)S(1)}, u32[]{:S(2)}, u32[]{:S(2)}) collective-permute-start(bf16[960,128]{1,0:T(8,128)(2,1)S(1)} %constant_dynamic-update-slice_fusion.4.refs_4_), channel_id=1, source_target_pairs={{0,24},{8,0},{16,8},{24,16},{1,25},{9,1},{17,9},{25,17},{2,26},{10... | collective-permute-start | bytes 737288 | tf_op jit(solution)/shard_map/ppermute | solution.py:1546
  472.8 18.4 %collective-permute-start.32 = (bf16[960,128]{1,0:T(8,128)(2,1)S(1)}, bf16[960,128]{1,0:T(8,128)(2,1)S(1)}, u32[]{:S(2)}, u32[]{:S(2)}) collective-permute-start(bf16[960,128]{1,0:T(8,128)(2,1)S(1)} %constant_dynamic-update-slice_fusion.4.refs_4_), channel_id=1, source_target_pairs={{0,16},{8,24},{16,0},{24,8},{1,17},{9,25},{17,1},{25,9},{2,18},{10... | collective-permute-start | bytes 737288 | tf_op jit(solution)/shard_map/ppermute | solution.py:1546
  473.3 17.8 %collective-permute-start.31 = (bf16[960,128]{1,0:T(8,128)(2,1)S(1)}, bf16[960,128]{1,0:T(8,128)(2,1)S(1)}, u32[]{:S(2)}, u32[]{:S(2)}) collective-permute-start(bf16[960,128]{1,0:T(8,128)(2,1)S(1)} %constant_dynamic-update-slice_fusion.4.refs_4_), channel_id=1, source_target_pairs={{0,8},{8,16},{16,24},{24,0},{1,9},{9,17},{17,25},{25,1},{2,10},{10... | collective-permute-start | bytes 737288 | tf_op jit(solution)/shard_map/ppermute | solution.py:1546
  502.6 14.9 %collective-permute-start.37 = (bf16[896,128]{1,0:T(8,128)(2,1)S(1)}, bf16[896,128]{1,0:T(8,128)(2,1)S(1)}, u32[]{:S(2)}, u32[]{:S(2)}) collective-permute-start(bf16[896,128]{1,0:T(8,128)(2,1)S(1)} %collective-permute-done.30.refs_3_), channel_id=1, source_target_pairs={{0,4},{4,0},{1,5},{5,1},{2,6},{6,2},{3,7},{7,3},{8,12},{12,8},{9,1... | collective-permute-start | bytes 688136 | tf_op jit(solution)/shard_map/ppermute | solution.py:1180
  503.0 14.6 %collective-permute-start.38 = (bf16[960,128]{1,0:T(8,128)(2,1)S(1)}, bf16[960,128]{1,0:T(8,128)(2,1)S(1)}, u32[]{:S(2)}, u32[]{:S(2)}) collective-permute-start(bf16[960,128]{1,0:T(8,128)(2,1)S(1)} %constant_dynamic-update-slice_fusion.4.refs_4_), channel_id=1, source_target_pairs={{0,4},{4,0},{1,5},{5,1},{2,6},{6,2},{3,7},{7,3},{8,12},{12,8},{9,1... | collective-permute-start | bytes 737288 | tf_op jit(solution)/shard_map/ppermute | solution.py:1180
  (104 other events, 913.0 us)
Sparse Core Ops, SparseCore 0:
  13.5 80.4 all-gather.4
  97.5 72.3 all-gather.6

commit v4 on v2

--- a/solution.py
+++ b/solution.py
@@ -44,7 +44,7 @@
         body,
         name=name,
         out_shape=tuple(pltpu.HBM(o.shape, o.dtype) if s is not VM else o for o, s in outs),
-        in_specs=[VM if s is NEAR else s for _, s in ins],
+        in_specs=[VM if s in (NEAR, FAR) else s for _, s in ins],
         out_specs=tuple(VM if s is FAR else s for _, s in outs),
         scratch_shapes=list(scratch),
         compiler_params=pltpu.CompilerParams(vmem_limit_bytes=50 * 1024 * 1024),
@@ -260,7 +260,7 @@
     return launch(
         name,
         functools.partial(pack_kernel, side, cuts),
-        [(v, VM) for v in (local, glob) + more],
+        [(v, FAR) for v in (local, glob) + more],
         [(shape((n + e, c), BF), VM) for n, e in zip(cuts, extra)],
         [pltpu.VMEM((c // 128, rows, 128), F32)],
         (0, 4 * rows * c),
@@ -1309,6 +1309,8 @@
         "expand_one", 1, 144, st2, norms, z2, near
     )
     st3 = share(jnp.concatenate([s3, ss]))
+    st3, *cots = tie(st3, *cots)
+    cots = tuple(cots)
     mid, h3, z4, s4, sum3, sums = launch(
         "reduce_two",
         middle_kernel,

time: 528 us -> 545 us (1.032)
  waiting for transfers between devices: 151 us -> 162 us
  blocking collectives: 45 us -> 51.9 us
    all_to_all x1 -> x2, blocking collectives: 22.1 us -> 38.1 us  [tell(): return lax.all_to_all(v, BATCH, 0, 0)]
    ppermute x4, waiting for transfers between devices: 27.3 us -> 38.5 us  [around(): right = [lax.ppermute(v, 'z', ring(4, 3)) for v in parts]]
    all_to_all x1, blocking collectives: 23 us -> 13.7 us  [spread(): return lax.all_to_all(jnp.broadcast_to(v[None], (n,) + v.shape), axes, 0, 0)]
    ppermute x4, waiting for transfers between devices: 2.68 us -> 8.44 us  [around(): left = [lax.ppermute(v, 'z', ring(4, 1)) for v in parts]]
    all_to_all x7 -> x6, waiting for transfers between devices: 18 us -> 13.6 us  [tell(): return lax.all_to_all(v, BATCH, 0, 0)]
    all_to_all x7 -> x6, starting transfers between devices: 36.6 us -> 37.7 us  [tell(): return lax.all_to_all(v, BATCH, 0, 0)]
    unnamed x140 -> x130, local copies, waits for them, and re-layouts: 16.9 us -> 15.9 us
  transfers between devices with their start and end apart: 51 -> 50, of which waited for: 24 -> 27; matrix products, arithmetic and copies ran while one was open for 2% -> 2% of each run, Pallas kernels for 24% -> 22%
where the time goes in v4:
time: 545 us; the launch traced here: 536 us
  Pallas kernels  174 us (32%)
  waiting for transfers between devices  162 us (30%)
  starting transfers between devices  102 us (19%)
  blocking collectives  51.9 us (10%)
  local copies, waits for them, and re-layouts  21.6 us (4%)
  between operations  15.7 us (3%)
  other arithmetic  8.93 us (2%)
    pallas_call x29, Pallas kernels, launch(): pl.pallas_call(body, name=name, out_shape=tuple((pltpu.HBM(o.shape, o.dty...  162 us
    ppermute x4, waiting for transfers between devices, around(): right = [lax.ppermute(v, 'z', ring(4, 3)) for v in parts]  38.5 us
    all_to_all x2, blocking collectives, tell(): return lax.all_to_all(v, BATCH, 0, 0)  38.1 us
    all_to_all x6, starting transfers between devices, tell(): return lax.all_to_all(v, BATCH, 0, 0)  37.7 us
    all_to_all x5, waiting for transfers between devices, spread(): return lax.all_to_all(jnp.broadcast_to(v[None], (n,) + v.shape), axes, 0, 0)  37.5 us
    ppermute x3, waiting for transfers between devices, body(): some = [some] + [lax.ppermute(some, 'y', ring(4, k)) for k in (1, 2, 3)]  30.6 us
    all_to_all x5, starting transfers between devices, spread(): return lax.all_to_all(jnp.broadcast_to(v[None], (n,) + v.shape), axes, 0, 0)  21.6 us
    unnamed x130, local copies, waits for them, and re-layouts  15.9 us
  transfers between devices with their start and end apart: 50, of which 27 were waited for; matrix products, arithmetic and copies ran while one was open for 2% of the time, Pallas kernels for 22%

profile of v4, /device:TPU:1, one launch (start us, length us, event | category | flops | bytes accessed | tf_op | source)
XLA Modules:
  0.0 535.7 jit_solution(668302968190698858)
XLA Ops:
  19.7 27.3 %collective-permute-done.2.refs_2_.t1 = bf16[1312,256]{1,0:T(8,128)(2,1)S(1)} collective-permute-done((bf16[1312,256]{1,0:T(8,128)(2,1)S(1)}, bf16[1312,256]{1,0:T(8,128)(2,1)S(1)}, u32[]{:S(2)}, u32[]{:S(2)}) %collective-permute-start.2) | collective-permute-done | bytes 671776 | tf_op jit(solution)/shard_map/ppermute | solution.py:1183
  56.6 12.9 %all-to-all-done = bf16[4,96,128]{2,1,0:T(8,128)(2,1)S(1)} async-done(((bf16[4,96,128]{2,1,0:T(8,128)(2,1)}), bf16[4,96,128]{2,1,0:T(8,128)(2,1)S(1)}, u32[]{:S(2)}, u32[]{:S(2)}) %all-to-all-start) | async-done | bytes 98336 | tf_op jit(solution)/shard_map/all_to_all | solution.py:1152
  71.2 8.0 %reduce_one.1 = (f32[2144,512]{1,0:T(8,128)}, f32[32,4,512]{2,1,0:T(4,128)}) custom-call(s32[5]{0:T(128)S(1)} %stack.101.zi, bf16[1312,256]{1,0:T(8,128)(2,1)} %copy-done, bf16[1344,256]{1,0:T(8,128)(2,1)} %copy-done.10, bf16[1312,256]{1,0:T(8,128)(2,1)} %copy-done.2, bf16[1344,256]{1,0:T(8,128)(2,1)} %collective-permute-done.3.refs_3_, ...), custom_call_target="tpu_custom_call" | custom-call | flops 2248146944 | bytes 10000000 | tf_op jit(solution)/shard_map/reduce_one/pallas_call | solution.py:43
  79.2 22.1 %all_to_all.80.st = f32[32,4,512]{2,1,0:T(4,128)S(1)} all-to-all(f32[32,4,512]{2,1,0:T(4,128)} %get-tuple-element.196), channel_id=1, replica_groups=mesh['y'=4,'x'=4,'c'=2,'z'=4] {'y','x','c'}, dimensions={0} | all-to-all | bytes 524288 | tf_op jit(solution)/shard_map/all_to_all | solution.py:1161
  101.3 8.6 %spatial_one.1 = (bf16[544,4608]{1,0:T(8,128)(2,1)}, f32[544,512]{1,0:T(8,128)}, f32[32,4,512]{2,1,0:T(4,128)}, f32[4,512]{1,0:T(4,128)S(1)}) custom-call(f32[32,4,512]{2,1,0:T(4,128)S(1)} %all_to_all.80.st, f32[4,32,128]{2,1,0:T(8,128)S(1)} %convert_add_fusion.norms, f32[2144,512]{1,0:T(8,128)} %get-tuple-element.197.z1, bf16[32,4,400,128]{3,2,1,0:T(8,128)(2,1)} %bitcast.68), custom_call_target="tpu_custom_call" | custom-call | flops 40000000000 | bytes 20000000 | tf_op jit(solution)/shard_map/spatial_one/pallas_call | solution.py:43
  114.6 9.1 %shortcut.2 = (bf16[544,1024]{1,0:T(8,128)(2,1)}, f32[544,2048]{1,0:T(8,128)}, f32[4,2048]{1,0:T(4,128)S(1)}) custom-call(s32[5]{0:T(128)S(1)} %stack.101.zi, bf16[1312,256]{1,0:T(8,128)(2,1)} %copy-done, bf16[1344,256]{1,0:T(8,128)(2,1)} %copy-done.10, bf16[1312,256]{1,0:T(8,128)(2,1)} %copy-done.2, bf16[1344,256]{1,0:T(8,128)(2,1)} %collective-permute-done.3.refs_3_, ...), custom_call_target="tpu_custom_call" | custom-call | flops 2281701376 | bytes 14000000 | tf_op jit(solution)/shard_map/shortcut/pallas_call | solution.py:43
  131.5 6.8 %all-to-all-start.3 = ((f32[16,8,2048]{2,1,0:T(8,128)}), f32[16,8,2048]{2,1,0:T(8,128)S(1)}, u32[]{:S(2)}, u32[]{:S(2)}) async-start(f32[16,8,2048]{2,1,0:T(8,128)} %broadcast_in_dim.15), calls=%async_computation.3 | async-start | bytes 2097152 | tf_op jit(solution)/shard_map/all_to_all | solution.py:1152
  151.8 8.5 %collective-permute-done.10.refs_3_ = bf16[272,512]{1,0:T(8,128)(2,1)S(1)} collective-permute-done((bf16[272,512]{1,0:T(8,128)(2,1)S(1)}, bf16[272,512]{1,0:T(8,128)(2,1)S(1)}, u32[]{:S(2)}, u32[]{:S(2)}) %collective-permute-start.10) | collective-permute-done | bytes 278560 | tf_op jit(solution)/shard_map/ppermute | solution.py:1183
  172.1 10.1 %reduce_two.2 = (f32[544,2048]{1,0:T(8,128)}, bf16[544,2048]{1,0:T(8,128)(2,1)}, f32[544,512]{1,0:T(8,128)}, f32[32,4,512]{2,1,0:T(4,128)}, f32[4,2048]{1,0:T(4,128)S(1)}, /*index=5*/f32[4,2048]{1,0:T(4,128)S(1)}) custom-call(f32[16,8,2048]{2,1,0:T(8,128)S(1)} %all-to-all-done.3.st3, f32[4,32,128]{2,1,0:T(8,128)S(1)} %convert_add_fusion.norms, ...), custom_call_target="tpu_custom_call" | custom-call | flops 1140850688 | bytes 20000000 | tf_op jit(solution)/shard_map/reduce_two/pallas_call | solution.py:43
  182.2 12.2 %all-to-all-start.4 = ((f32[32,4,512]{2,1,0:T(4,128)}), f32[32,4,512]{2,1,0:T(4,128)}, u32[]{:S(2)}, u32[]{:S(2)}) async-start(f32[32,4,512]{2,1,0:T(4,128)} %get-tuple-element.218), calls=%async_computation.4 | async-start | bytes 524288 | tf_op jit(solution)/shard_map/all_to_all | solution.py:1161
  203.2 8.3 %spatial_two.1 = (bf16[544,4608]{1,0:T(8,128)(2,1)}, f32[544,512]{1,0:T(8,128)}, f32[32,4,512]{2,1,0:T(4,128)}, f32[4,512]{1,0:T(4,128)S(1)}) custom-call(f32[32,4,512]{2,1,0:T(4,128)} %all-to-all-done.4.st, f32[4,32,128]{2,1,0:T(8,128)S(1)} %convert_add_fusion.norms, f32[544,512]{1,0:T(8,128)} %get-tuple-element.220.z4, bf16[32,4,208,128]{3,2,1,0:T(8,128)(2,1)} %bitcast.76), custom_call_target="tpu_custom_call" | custom-call | flops 2566914048 | bytes 20000000 | tf_op jit(solution)/shard_map/spatial_two/pallas_call | solution.py:43
  211.6 16.1 %all_to_all.81.st = f32[32,4,512]{2,1,0:T(4,128)S(1)} all-to-all(f32[32,4,512]{2,1,0:T(4,128)} %get-tuple-element.222), channel_id=1, replica_groups=mesh['y'=4,'x'=4,'c'=2,'z'=4] {'y','x','c'}, dimensions={0} | all-to-all | bytes 524288 | tf_op jit(solution)/shard_map/all_to_all | solution.py:1161
  227.6 5.3 expand_two.2
  234.4 13.7 %all_to_all.82.st = f32[16,4,2048]{2,1,0:T(4,128)S(1)} all-to-all(f32[16,4,2048]{2,1,0:T(4,128)S(1)} %broadcast_in_dim.16), channel_id=1, replica_groups=mesh['y'=4,'x'=4,'c'=2,'z'=4] {'y','x'}, dimensions={0} | all-to-all | bytes 1048576 | tf_op jit(solution)/shard_map/all_to_all | solution.py:1152
  248.1 8.0 %output.1 = (f32[544,512]{1,0:T(8,128)}, f32[544,2048]{1,0:T(8,128)}, f32[4,2048]{1,0:T(4,128)S(1)}, f32[4,2048]{1,0:T(4,128)S(1)}) custom-call(s32[5]{0:T(128)S(1)} %stack.101.zi, f32[16,4,2048]{2,1,0:T(4,128)S(1)} %all_to_all.82.st, f32[4,32,128]{2,1,0:T(8,128)S(1)} %convert_add_fusion.norms, f32[544,2048]{1,0:T(8,128)} %get-tuple-element.225.z6, ...), custom_call_target="tpu_custom_call" | custom-call | bytes 20000000 | tf_op jit(solution)/shard_map/output/pallas_call | solution.py:43
  264.6 9.7 %all-to-all-done.7.stb = f32[16,4,2048]{2,1,0:T(4,128)S(1)} async-done(((f32[16,4,2048]{2,1,0:T(4,128)}), f32[16,4,2048]{2,1,0:T(4,128)S(1)}, u32[]{:S(2)}, u32[]{:S(2)}) %all-to-all-start.7) | async-done | bytes 524320 | tf_op jit(solution)/shard_map/all_to_all | solution.py:1152
  274.3 10.0 %back_expand_two.1 = (bf16[544,512]{1,0:T(8,128)(2,1)S(1)}, f32[544,512]{1,0:T(8,128)}, f32[32,4,512]{2,1,0:T(4,128)}, f32[2,2048]{1,0:T(2,128)S(1)}) custom-call(s32[5]{0:T(128)S(1)} %stack.101.zi, f32[16,4,2048]{2,1,0:T(4,128)S(1)} %all-to-all-done.7.stb, f32[4,32,128]{2,1,0:T(8,128)S(1)} %convert_add_fusion.norms, f32[4,2048]{1,0:T(4,128)S(1)} %get-tuple-element.242.sum6, ...), custom_call_target="tpu_custom_call" | custom-call | flops 1140850688 | bytes 14000000 | tf_op jit(solution)/shard_map/back_expand_two/pallas_call | solution.py:43
  290.9 7.6 %all-to-all-done.8.stb = f32[32,4,512]{2,1,0:T(4,128)S(1)} async-done(((f32[32,4,512]{2,1,0:T(4,128)}), f32[32,4,512]{2,1,0:T(4,128)S(1)}, u32[]{:S(2)}, u32[]{:S(2)}) %all-to-all-start.8) | async-done | bytes 262176 | tf_op jit(solution)/shard_map/all_to_all | solution.py:1161
  298.5 9.0 %back_spatial_two.1 = (bf16[544,128]{1,0:T(8,128)(2,1)S(1)}, f32[544,512]{1,0:T(8,128)}, f32[32,4,512]{2,1,0:T(4,128)}, f32[2,512]{1,0:T(2,128)S(1)}) custom-call(s32[5]{0:T(128)S(1)} %stack.101.zi, f32[32,4,512]{2,1,0:T(4,128)S(1)} %all-to-all-done.8.stb, f32[4,32,128]{2,1,0:T(8,128)S(1)} %convert_add_fusion.norms, f32[4,512]{1,0:T(4,128)S(1)} %get-tuple-element.243.sum5, ...), custom_call_target="tpu_custom_call" | custom-call | flops 2566914048 | bytes 10000000 | tf_op jit(solution)/shard_map/back_spatial_two/pallas_call | solution.py:43
  320.3 11.1 %back_reduce_two.1 = (bf16[544,128]{1,0:T(8,128)(2,1)S(1)}, f32[544,2048]{1,0:T(8,128)}, f32[6,2048]{1,0:T(8,128)S(1)}, f32[2,512]{1,0:T(2,128)S(1)}) custom-call(s32[5]{0:T(128)S(1)} %stack.101.zi, f32[32,4,512]{2,1,0:T(4,128)S(1)} %all-to-all-done.9.stb, f32[4,32,128]{2,1,0:T(8,128)S(1)} %convert_add_fusion.norms, f32[4,512]{1,0:T(4,128)S(1)} %get-tuple-element.251.sum4, ...), custom_call_target="tpu_custom_call" | custom-call | flops 1140850688 | bytes 22000000 | tf_op jit(solution)/shard_map/back_reduce_two/pallas_call | solution.py:43
  340.8 14.8 %all-to-all-done.10.stb = f32[16,6,2048]{2,1,0:T(8,128)S(1)} async-done(((f32[16,6,2048]{2,1,0:T(8,128)}), f32[16,6,2048]{2,1,0:T(8,128)S(1)}, u32[]{:S(2)}, u32[]{:S(2)}) %all-to-all-start.10) | async-done | bytes 786464 | tf_op jit(solution)/shard_map/all_to_all | solution.py:1152
  356.3 10.0 %back_expand_one.1 = (bf16[544,512]{1,0:T(8,128)(2,1)S(1)}, f32[544,512]{1,0:T(8,128)}, f32[32,4,512]{2,1,0:T(4,128)}, f32[2,2048]{1,0:T(2,128)S(1)}, f32[4,2048]{1,0:T(4,128)S(1)}) custom-call(s32[5]{0:T(128)S(1)} %stack.101.zi, f32[16,6,2048]{2,1,0:T(8,128)S(1)} %all-to-all-done.10.stb, f32[4,32,128]{2,1,0:T(8,128)S(1)} %convert_add_fusion.norms, ...), custom_call_target="tpu_custom_call" | custom-call | flops 1140850688 | bytes 16000000 | tf_op jit(solution)/shard_map/back_expand_one/pallas_call | solution.py:43
  372.9 5.4 %back_shortcut.1 = (bf16[544,512]{1,0:T(8,128)(2,1)S(1)}, f32[544,256]{1,0:T(8,128)S(1)}, f32[2,2048]{1,0:T(2,128)S(1)}) custom-call(s32[5]{0:T(128)S(1)} %stack.101.zi, f32[4,32,128]{2,1,0:T(8,128)S(1)} %convert_add_fusion.norms, f32[4,2048]{1,0:T(4,128)S(1)} %get-tuple-element.271.gsum, f32[4,2048]{1,0:T(4,128)S(1)} %get-tuple-element.260.sums, ...), custom_call_target="tpu_custom_call" | custom-call | flops 570425344 | bytes 10000000 | tf_op jit(solution)/shard_map/back_shortcut/pallas_call | solution.py:43
  386.0 13.7 %back_spatial_one.1 = (bf16[544,128]{1,0:T(8,128)(2,1)S(1)}, f32[2144,512]{1,0:T(8,128)}, f32[32,4,512]{2,1,0:T(4,128)}, f32[2,512]{1,0:T(2,128)S(1)}) custom-call(s32[5]{0:T(128)S(1)} %stack.101.zi, f32[32,4,512]{2,1,0:T(4,128)S(1)} %all-to-all-done.11.stb, f32[4,32,128]{2,1,0:T(8,128)S(1)} %convert_add_fusion.norms, f32[4,512]{1,0:T(4,128)S(1)} %copy-done.36, ...), custom_call_target="tpu_custom_call" | custom-call | flops 2566914048 | bytes 20000000 | tf_op jit(solution)/shard_map/back_spatial_one/pallas_call | solution.py:43
  399.7 7.5 %all-to-all-start.12 = ((f32[32,4,512]{2,1,0:T(4,128)}), f32[32,4,512]{2,1,0:T(4,128)S(1)}, u32[]{:S(2)}, u32[]{:S(2)}) async-start(f32[32,4,512]{2,1,0:T(4,128)} %get-tuple-element.282), calls=%async_computation.12 | async-start | bytes 524288 | tf_op jit(solution)/shard_map/all_to_all | solution.py:1161
  416.8 5.4 %all-to-all-start.13 = ((bf16[16,464,128]{2,1,0:T(8,128)(2,1)}), bf16[16,464,128]{2,1,0:T(8,128)(2,1)S(1)}, u32[]{:S(2)}, u32[]{:S(2)}) async-start(bf16[16,464,128]{2,1,0:T(8,128)(2,1)} %bitcast.80), calls=%async_computation.13 | async-start | bytes 3801088 | tf_op jit(solution)/shard_map/all_to_all | solution.py:1485
  423.9 6.1 %back_reduce_one.1 = (bf16[2144,128]{1,0:T(8,128)(2,1)S(1)}, bf16[2144,512]{1,0:T(8,128)(2,1)}, f32[2,512]{1,0:T(2,128)S(1)}) custom-call(s32[5]{0:T(128)S(1)} %stack.101.zi, f32[32,4,512]{2,1,0:T(4,128)S(1)} %copy-done.19, f32[4,32,128]{2,1,0:T(8,128)S(1)} %convert_add_fusion.norms, f32[4,512]{1,0:T(4,128)S(1)} %copy-done.38, ...), custom_call_target="tpu_custom_call" | custom-call | bytes 12000000 | tf_op jit(solution)/shard_map/back_reduce_one/pallas_call | solution.py:43
  436.6 14.6 %all-to-all-done.13.src = bf16[16,464,128]{2,1,0:T(8,128)(2,1)S(1)} async-done(((bf16[16,464,128]{2,1,0:T(8,128)(2,1)}), bf16[16,464,128]{2,1,0:T(8,128)(2,1)S(1)}, u32[]{:S(2)}, u32[]{:S(2)}) %all-to-all-start.13) | async-done | bytes 1900576 | tf_op jit(solution)/shard_map/all_to_all | solution.py:1485
  481.0 17.3 %collective-permute-done.27.a3 = bf16[1856,128]{1,0:T(8,128)(2,1)S(1)} collective-permute-done((bf16[1856,128]{1,0:T(8,128)(2,1)S(1)}, bf16[1856,128]{1,0:T(8,128)(2,1)S(1)}, u32[]{:S(2)}, u32[]{:S(2)}) %collective-permute-start.27) | collective-permute-done | bytes 475168 | tf_op jit(solution)/shard_map/ppermute | solution.py:1541
  500.9 10.8 %collective-permute-done.25.a1 = bf16[1856,128]{1,0:T(8,128)(2,1)S(1)} collective-permute-done((bf16[1856,128]{1,0:T(8,128)(2,1)S(1)}, bf16[1856,128]{1,0:T(8,128)(2,1)S(1)}, u32[]{:S(2)}, u32[]{:S(2)}) %collective-permute-start.25) | collective-permute-done | bytes 475168 | tf_op jit(solution)/shard_map/ppermute | solution.py:1541
  515.8 5.8 %grads_kept.1 = (f32[512,512]{1,0:T(8,128)}, f32[4608,128]{1,0:T(8,128)}, f32[2048,128]{1,0:T(8,128)}, f32[512,512]{1,0:T(8,128)}, f32[1024,512]{1,0:T(8,128)}, ...) custom-call(s32[5]{0:T(128)S(1)} %stack.101.zi, s32[16]{0:T(128)S(1)} %stack.118.places, ...), custom_call_target="tpu_custom_call" | custom-call | bytes 8000000 | tf_op jit(solution)/shard_map/grads_kept/pallas_call | solution.py:1133
  521.7 6.2 %grads_given.1 = (f32[512,512]{1,0:T(8,128)}, f32[4608,128]{1,0:T(8,128)}, f32[2048,128]{1,0:T(8,128)}, f32[512,512]{1,0:T(8,128)}, f32[1024,512]{1,0:T(8,128)},...) custom-call(s32[5]{0:T(128)S(1)} %stack.101.zi, ...), custom_call_target="tpu_custom_call", output_to_operand_aliasing={{0}: (7, {}), {1}: (8, {}), {2}: (9, {}), {3}: (10, {}), {4... | custom-call | bytes 8000000 | tf_op jit(solution)/shard_map/grads_given/pallas_call | solution.py:1133
  (276 shorter events, 178.0 us)
Async XLA Ops:
  7.2 94.1 %all-gather.5.cloned.1.call-start = ((), (), s32[]{:S(2)}) async-start(), calls=%async_computation.16 | async-start | bytes 13209600 | tf_op jit(solution)/shard_map/all_gather | solution.py:1246
  11.6 191.6 %all-gather.7.cloned.1.call-start = ((), (), s32[]{:S(2)}) async-start(), calls=%async_computation.17 | async-start | bytes 6868992 | tf_op jit(solution)/shard_map/all_gather | solution.py:1247
  12.3 37.3 %collective-permute-start.3 = (bf16[1344,256]{1,0:T(8,128)(2,1)S(1)}, bf16[1344,256]{1,0:T(8,128)(2,1)}, u32[]{:S(2)}, u32[]{:S(2)}) collective-permute-start(bf16[1344,256]{1,0:T(8,128)(2,1)S(1)} %get-tuple-element.185.refs_1_), channel_id=1, source_target_pairs={{0,3},{1,0},{2,1},{3,2},{4,7},{5,4},{6,5},{7,6},{8,11},{9,8},{10,9... | collective-permute-start | bytes 2064392 | tf_op jit(solution)/shard_map/ppermute | solution.py:1183
  17.0 32.7 %collective-permute-start.1 = (bf16[1344,256]{1,0:T(8,128)(2,1)S(1)}, bf16[1344,256]{1,0:T(8,128)(2,1)}, u32[]{:S(2)}, u32[]{:S(2)}) collective-permute-start(bf16[1344,256]{1,0:T(8,128)(2,1)S(1)} %get-tuple-element.185.refs_1_), channel_id=1, source_target_pairs={{0,1},{1,2},{2,3},{3,0},{4,5},{5,6},{6,7},{7,4},{8,9},{9,10},{10,1... | collective-permute-start | bytes 2064392 | tf_op jit(solution)/shard_map/ppermute | solution.py:1182
  17.0 30.0 %collective-permute-start.2 = (bf16[1312,256]{1,0:T(8,128)(2,1)S(1)}, bf16[1312,256]{1,0:T(8,128)(2,1)S(1)}, u32[]{:S(2)}, u32[]{:S(2)}) collective-permute-start(bf16[1312,256]{1,0:T(8,128)(2,1)S(1)} %get-tuple-element.183.refs_0_.t0), channel_id=1, source_target_pairs={{0,3},{1,0},{2,1},{3,2},{4,7},{5,4},{6,5},{7,6},{8,11},{9,8},{10,9... | collective-permute-start | bytes 2015240 | tf_op jit(solution)/shard_map/ppermute | solution.py:1183
  19.7 30.0 %collective-permute-start = (bf16[1312,256]{1,0:T(8,128)(2,1)S(1)}, bf16[1312,256]{1,0:T(8,128)(2,1)S(1)}, u32[]{:S(2)}, u32[]{:S(2)}) collective-permute-start(bf16[1312,256]{1,0:T(8,128)(2,1)S(1)} %get-tuple-element.183.refs_0_.t0), channel_id=1, source_target_pairs={{0,1},{1,2},{2,3},{3,0},{4,5},{5,6},{6,7},{7,4},{8,9},{9,10},{10,1... | collective-permute-start | bytes 2015240 | tf_op jit(solution)/shard_map/ppermute | solution.py:1182
  49.7 19.8 %collective-permute-start.4 = (bf16[1312,256]{1,0:T(8,128)(2,1)S(1)}, bf16[1312,256]{1,0:T(8,128)(2,1)S(1)}, u32[]{:S(2)}, u32[]{:S(2)}) collective-permute-start(bf16[1312,256]{1,0:T(8,128)(2,1)S(1)} %collective-permute-done.refs_6_.t3), channel_id=1, source_target_pairs={{0,1},{1,2},{2,3},{3,0},{4,5},{5,6},{6,7},{7,4},{8,9},{9,10},{10,1... | collective-permute-start | bytes 2015240 | tf_op jit(solution)/shard_map/ppermute | solution.py:1185
  49.8 19.8 %collective-permute-start.5 = (bf16[1344,256]{1,0:T(8,128)(2,1)}, bf16[1344,256]{1,0:T(8,128)(2,1)S(1)}, u32[]{:S(2)}, u32[]{:S(2)}) collective-permute-start(bf16[1344,256]{1,0:T(8,128)(2,1)} %collective-permute-done.3.refs_3_), channel_id=1, source_target_pairs={{0,3},{1,0},{2,1},{3,2},{4,7},{5,4},{6,5},{7,6},{8,11},{9,8},{10,9... | collective-permute-start | bytes 2064392 | tf_op jit(solution)/shard_map/ppermute | solution.py:1185
  53.1 16.4 %all-to-all-start = ((bf16[4,96,128]{2,1,0:T(8,128)(2,1)}), bf16[4,96,128]{2,1,0:T(8,128)(2,1)S(1)}, u32[]{:S(2)}, u32[]{:S(2)}) async-start(bf16[4,96,128]{2,1,0:T(8,128)(2,1)} %broadcast_in_dim.14), calls=%async_computation | async-start | bytes 196608 | tf_op jit(solution)/shard_map/all_to_all | solution.py:1152
  110.5 13.2 %all-to-all-start.2 = ((f32[32,4,512]{2,1,0:T(4,128)}), f32[32,4,512]{2,1,0:T(4,128)S(1)}, u32[]{:S(2)}, u32[]{:S(2)}) async-start(f32[32,4,512]{2,1,0:T(4,128)} %get-tuple-element.205), calls=%async_computation.2 | async-start | bytes 524288 | tf_op jit(solution)/shard_map/all_to_all | solution.py:1161
  131.5 39.9 %all-to-all-start.3 = ((f32[16,8,2048]{2,1,0:T(8,128)}), f32[16,8,2048]{2,1,0:T(8,128)S(1)}, u32[]{:S(2)}, u32[]{:S(2)}) async-start(f32[16,8,2048]{2,1,0:T(8,128)} %broadcast_in_dim.15), calls=%async_computation.3 | async-start | bytes 2097152 | tf_op jit(solution)/shard_map/all_to_all | solution.py:1152
  143.4 17.0 %collective-permute-start.10 = (bf16[272,512]{1,0:T(8,128)(2,1)S(1)}, bf16[272,512]{1,0:T(8,128)(2,1)S(1)}, u32[]{:S(2)}, u32[]{:S(2)}) collective-permute-start(bf16[272,512]{1,0:T(8,128)(2,1)S(1)} %get-tuple-element.228.refs_1_), channel_id=1, source_target_pairs={{0,3},{1,0},{2,1},{3,2},{4,7},{5,4},{6,5},{7,6},{8,11},{9,8},{10,9... | collective-permute-start | bytes 835592 | tf_op jit(solution)/shard_map/ppermute | solution.py:1183
  146.1 17.0 %collective-permute-start.8 = (bf16[272,512]{1,0:T(8,128)(2,1)S(1)}, bf16[272,512]{1,0:T(8,128)(2,1)S(1)}, u32[]{:S(2)}, u32[]{:S(2)}) collective-permute-start(bf16[272,512]{1,0:T(8,128)(2,1)S(1)} %get-tuple-element.228.refs_1_), channel_id=1, source_target_pairs={{0,1},{1,2},{2,3},{3,0},{4,5},{5,6},{6,7},{7,4},{8,9},{9,10},{10,1... | collective-permute-start | bytes 835592 | tf_op jit(solution)/shard_map/ppermute | solution.py:1182
  182.2 21.0 %all-to-all-start.4 = ((f32[32,4,512]{2,1,0:T(4,128)}), f32[32,4,512]{2,1,0:T(4,128)}, u32[]{:S(2)}, u32[]{:S(2)}) async-start(f32[32,4,512]{2,1,0:T(4,128)} %get-tuple-element.218), calls=%async_computation.4 | async-start | bytes 524288 | tf_op jit(solution)/shard_map/all_to_all | solution.py:1161
  259.7 14.6 %all-to-all-start.7 = ((f32[16,4,2048]{2,1,0:T(4,128)}), f32[16,4,2048]{2,1,0:T(4,128)S(1)}, u32[]{:S(2)}, u32[]{:S(2)}) async-start(f32[16,4,2048]{2,1,0:T(4,128)} %broadcast_in_dim.17), calls=%async_computation.7 | async-start | bytes 1048576 | tf_op jit(solution)/shard_map/all_to_all | solution.py:1152
  284.3 14.2 %all-to-all-start.8 = ((f32[32,4,512]{2,1,0:T(4,128)}), f32[32,4,512]{2,1,0:T(4,128)S(1)}, u32[]{:S(2)}, u32[]{:S(2)}) async-start(f32[32,4,512]{2,1,0:T(4,128)} %get-tuple-element.245), calls=%async_computation.8 | async-start | bytes 524288 | tf_op jit(solution)/shard_map/all_to_all | solution.py:1161
  307.5 12.8 %all-to-all-start.9 = ((f32[32,4,512]{2,1,0:T(4,128)}), f32[32,4,512]{2,1,0:T(4,128)S(1)}, u32[]{:S(2)}, u32[]{:S(2)}) async-start(f32[32,4,512]{2,1,0:T(4,128)} %get-tuple-element.253), calls=%async_computation.9 | async-start | bytes 524288 | tf_op jit(solution)/shard_map/all_to_all | solution.py:1161
  333.9 21.7 %all-to-all-start.10 = ((f32[16,6,2048]{2,1,0:T(8,128)}), f32[16,6,2048]{2,1,0:T(8,128)S(1)}, u32[]{:S(2)}, u32[]{:S(2)}) async-start(f32[16,6,2048]{2,1,0:T(8,128)} %broadcast_in_dim.18), calls=%async_computation.10 | async-start | bytes 2097152 | tf_op jit(solution)/shard_map/all_to_all | solution.py:1152
  337.6 33.6 %collective-permute-start.16 = (bf16[1024,128]{1,0:T(8,128)(2,1)}, bf16[1024,128]{1,0:T(8,128)(2,1)}, u32[]{:S(2)}, u32[]{:S(2)}) collective-permute-start(bf16[1024,128]{1,0:T(8,128)(2,1)} %copy-done.47), channel_id=1, source_target_pairs={{0,4},{4,0},{1,5},{5,1},{2,6},{6,2},{3,7},{7,3},{8,12},{12,8},{9,1... | collective-permute-start | bytes 786440 | tf_op jit(solution)/shard_map/ppermute | solution.py:1178
  337.9 45.9 %collective-permute-start.17 = (bf16[2304,128]{1,0:T(8,128)(2,1)}, bf16[2304,128]{1,0:T(8,128)(2,1)}, u32[]{:S(2)}, u32[]{:S(2)}) collective-permute-start(bf16[2304,128]{1,0:T(8,128)(2,1)} %copy-done.43), channel_id=1, source_target_pairs={{0,4},{4,0},{1,5},{5,1},{2,6},{6,2},{3,7},{7,3},{8,12},{12,8},{9,1... | collective-permute-start | bytes 1769480 | tf_op jit(solution)/shard_map/ppermute | solution.py:1178
  366.3 17.0 %all-to-all-start.11 = ((f32[32,4,512]{2,1,0:T(4,128)}), f32[32,4,512]{2,1,0:T(4,128)S(1)}, u32[]{:S(2)}, u32[]{:S(2)}) async-start(f32[32,4,512]{2,1,0:T(4,128)} %get-tuple-element.270), calls=%async_computation.11 | async-start | bytes 524288 | tf_op jit(solution)/shard_map/all_to_all | solution.py:1161
  383.3 28.5 %collective-permute-start.19 = (bf16[3072,128]{1,0:T(8,128)(2,1)S(1)}, bf16[3072,128]{1,0:T(8,128)(2,1)}, u32[]{:S(2)}, u32[]{:S(2)}) collective-permute-start(bf16[3072,128]{1,0:T(8,128)(2,1)S(1)} %get-tuple-element.290), channel_id=1, source_target_pairs={{0,4},{4,0},{1,5},{5,1},{2,6},{6,2},{3,7},{7,3},{8,12},{12,8},{9,1... | collective-permute-start | bytes 2359304 | tf_op jit(solution)/shard_map/ppermute | solution.py:1178
  385.8 25.9 %collective-permute-start.18 = (bf16[1024,128]{1,0:T(8,128)(2,1)S(1)}, bf16[1024,128]{1,0:T(8,128)(2,1)S(1)}, u32[]{:S(2)}, u32[]{:S(2)}) collective-permute-start(bf16[1024,128]{1,0:T(8,128)(2,1)S(1)} %copy-done.49), channel_id=1, source_target_pairs={{0,4},{4,0},{1,5},{5,1},{2,6},{6,2},{3,7},{7,3},{8,12},{12,8},{9,1... | collective-permute-start | bytes 786440 | tf_op jit(solution)/shard_map/ppermute | solution.py:1178
  399.7 16.4 %all-to-all-start.12 = ((f32[32,4,512]{2,1,0:T(4,128)}), f32[32,4,512]{2,1,0:T(4,128)S(1)}, u32[]{:S(2)}, u32[]{:S(2)}) async-start(f32[32,4,512]{2,1,0:T(4,128)} %get-tuple-element.282), calls=%async_computation.12 | async-start | bytes 524288 | tf_op jit(solution)/shard_map/all_to_all | solution.py:1161
  416.8 34.4 %all-to-all-start.13 = ((bf16[16,464,128]{2,1,0:T(8,128)(2,1)}), bf16[16,464,128]{2,1,0:T(8,128)(2,1)S(1)}, u32[]{:S(2)}, u32[]{:S(2)}) async-start(bf16[16,464,128]{2,1,0:T(8,128)(2,1)} %bitcast.80), calls=%async_computation.13 | async-start | bytes 3801088 | tf_op jit(solution)/shard_map/all_to_all | solution.py:1485
  422.2 13.3 %collective-permute-start.20 = (bf16[2304,128]{1,0:T(8,128)(2,1)}, bf16[2304,128]{1,0:T(8,128)(2,1)S(1)}, u32[]{:S(2)}, u32[]{:S(2)}) collective-permute-start(bf16[2304,128]{1,0:T(8,128)(2,1)} %get-tuple-element.297), channel_id=1, source_target_pairs={{0,4},{4,0},{1,5},{5,1},{2,6},{6,2},{3,7},{7,3},{8,12},{12,8},{9,1... | collective-permute-start | bytes 1769480 | tf_op jit(solution)/shard_map/ppermute | solution.py:1178
  451.2 20.2 %all-to-all-start.14 = ((bf16[16,176,128]{2,1,0:T(8,128)(2,1)}), bf16[16,176,128]{2,1,0:T(8,128)(2,1)S(1)}, u32[]{:S(2)}, u32[]{:S(2)}) async-start(bf16[16,176,128]{2,1,0:T(8,128)(2,1)} %bitcast.83), calls=%async_computation.14 | async-start | bytes 1441792 | tf_op jit(solution)/shard_map/all_to_all | solution.py:1511
  458.8 12.6 %collective-permute-start.22 = (bf16[464,128]{1,0:T(8,128)(2,1)S(1)}, bf16[464,128]{1,0:T(8,128)(2,1)S(1)}, u32[]{:S(2)}, u32[]{:S(2)}) collective-permute-start(bf16[464,128]{1,0:T(8,128)(2,1)S(1)} %get-tuple-element.315), channel_id=1, source_target_pairs={{0,8},{8,16},{16,24},{24,0},{1,9},{9,17},{17,25},{25,1},{2,10},{10... | collective-permute-start | bytes 356360 | tf_op jit(solution)/shard_map/ppermute | solution.py:1521
  472.6 39.0 %all-to-all-start.15 = ((bf16[16,224,128]{2,1,0:T(8,128)(2,1)}), bf16[16,224,128]{2,1,0:T(8,128)(2,1)S(1)}, u32[]{:S(2)}, u32[]{:S(2)}) async-start(bf16[16,224,128]{2,1,0:T(8,128)(2,1)} %broadcast_in_dim.19), calls=%async_computation.15 | async-start | bytes 1835008 | tf_op jit(solution)/shard_map/all_to_all | solution.py:1152
  477.0 21.3 %collective-permute-start.27 = (bf16[1856,128]{1,0:T(8,128)(2,1)S(1)}, bf16[1856,128]{1,0:T(8,128)(2,1)S(1)}, u32[]{:S(2)}, u32[]{:S(2)}) collective-permute-start(bf16[1856,128]{1,0:T(8,128)(2,1)S(1)} %constant_dynamic-update-slice_fusion.a0), channel_id=1, source_target_pairs={{0,96},{32,0},{64,32},{96,64},{1,97},{33,1},{65,33},{97,65},{2,98}... | collective-permute-start | bytes 1425416 | tf_op jit(solution)/shard_map/ppermute | solution.py:1541
  479.6 21.3 %collective-permute-start.26 = (bf16[1856,128]{1,0:T(8,128)(2,1)S(1)}, bf16[1856,128]{1,0:T(8,128)(2,1)S(1)}, u32[]{:S(2)}, u32[]{:S(2)}) collective-permute-start(bf16[1856,128]{1,0:T(8,128)(2,1)S(1)} %constant_dynamic-update-slice_fusion.a0), channel_id=1, source_target_pairs={{0,64},{32,96},{64,0},{96,32},{1,65},{33,97},{65,1},{97,33},{2,66}... | collective-permute-start | bytes 1425416 | tf_op jit(solution)/shard_map/ppermute | solution.py:1541
  480.2 31.5 %collective-permute-start.25 = (bf16[1856,128]{1,0:T(8,128)(2,1)S(1)}, bf16[1856,128]{1,0:T(8,128)(2,1)S(1)}, u32[]{:S(2)}, u32[]{:S(2)}) collective-permute-start(bf16[1856,128]{1,0:T(8,128)(2,1)S(1)} %constant_dynamic-update-slice_fusion.a0), channel_id=1, source_target_pairs={{0,32},{32,64},{64,96},{96,0},{1,33},{33,65},{65,97},{97,1},{2,34}... | collective-permute-start | bytes 1425416 | tf_op jit(solution)/shard_map/ppermute | solution.py:1541
  (81 other events, 774.8 us)
Sparse Core Ops, SparseCore 0:
  11.7 80.4 all-gather.4
  95.1 76.3 all-gather.6
